TPU v7x, 128 devices: a whole 4x4x4 slice. The times are simulated.
128 devices in a mesh: dp: 32 (over z_lo, x, y), tensor: 4 (over z_hi, core).
Axes of the slice: x: 4, y: 4, z: 4 (z_hi: 2, z_lo: 2; z = z_hi * 2 + z_lo), core: 2. Of those that a mesh axis runs over, the one named last changes fastest.
Arguments:
- hidden_in: bfloat16 [16384, 2048], P('dp'), may hold values from -6 to 6
- segment_ids: int32 [16384], P('dp'), may hold values from 0 to 3, as said below
- positions: int32 [16384], P('dp'), may hold values from 0 to 508, as said below
- ln1_gain: float32 [2048], replicated, may hold values from 0.1 to 1.9
- ln1_bias: float32 [2048], replicated, may hold values from -3 to 3
- qkv_weight: bfloat16 [2048, 6144], P(None, 'tensor'), may hold values from -0.125 to 0.125
- qkv_bias: float32 [8, 768], P('tensor'), may hold values from -3 to 3
- dense_weight: bfloat16 [2048, 2048], P('tensor'), may hold values from -0.5 to 0.5
- dense_bias: float32 [2048], replicated, may hold values from -3 to 3
- ln2_gain: float32 [2048], replicated, may hold values from 0.1 to 1.9
- ln2_bias: float32 [2048], replicated, may hold values from -3 to 3
- fc1_weight: bfloat16 [2048, 8192], P(None, 'tensor'), may hold values from -0.125 to 0.125
- fc1_bias: float32 [64, 128], P('tensor'), may hold values from -3 to 3
- fc2_weight: bfloat16 [8192, 2048], P('tensor'), may hold values from -0.0625 to 0.0625
- fc2_bias: float32 [2048], replicated, may hold values from -3 to 3
- cotangent: bfloat16 [16384, 2048], P('dp'), may hold values from -6 to 6
Outputs:
- output: float32 [16384, 2048], P('dp')
- input_grad: float32 [16384, 2048], P('dp')
- ln1_gain_grad: float32 [2048], P('dp')
- ln1_bias_grad: float32 [2048], P('dp')
- qkv_weight_grad: float32 [2048, 6144], P('dp', 'tensor')
- qkv_bias_grad: float32 [8, 768], P('tensor', 'dp')
- dense_weight_grad: float32 [2048, 2048], P('tensor', 'dp')
- dense_bias_grad: float32 [2048], P('dp')
- ln2_gain_grad: float32 [2048], P('dp')
- ln2_bias_grad: float32 [2048], P('dp')
- fc1_weight_grad: float32 [2048, 8192], P('dp', 'tensor')
- fc1_bias_grad: float32 [64, 128], P('tensor', 'dp')
- fc2_weight_grad: float32 [8192, 2048], P('tensor', 'dp')
- fc2_bias_grad: float32 [2048], P('dp')
Inputs may be any that keep to these rules, and one draw needn't show every extreme that they name: `segment_ids`: within each sequence of 512 tokens the segment numbers start at 0, never fall, and take each of the 4 values. `positions`: A token's index in its sequence minus the index of its document's first token.
All inputs are finite; a program needn't handle non-finite values.
Results may differ from a plain program's by a relative error of at most 0.011.
Values sent between devices are 32-bit elements; how exact they have to be, the bound alone decides.
No kernel may reach another device: no remote copies, remote signals or barrier semaphores. Data moves between devices by JAX's collectives and lax.ppermute only.
A program may use at most 256 MiB of HBM per device.

v0:
```python
from functools import partial
import math

import jax
import jax.numpy as jnp
import numpy as np
from jax import lax
from jax.experimental import pallas as pl
from jax.experimental.pallas import tpu as pltpu
from jax.sharding import Mesh, PartitionSpec as P

HD = 256
ROT = 64
TOK = 512
D = 2048
EPSILON = 1e-05
NEGATIVE = -1000000000.0
SIZES = {"zl": 2, "x": 4, "y": 4, "zh": 2, "c": 2}
DP = ("zl", "x", "y")
TENSOR = ("zh", "c")
F32 = jnp.float32
BF16 = jnp.bfloat16


def send(value, axis, step=1):
    n = SIZES[axis]
    return lax.ppermute(value, axis, [(i, (i + step) % n) for i in range(n)])


def swap(value, axis, bit):
    return lax.ppermute(value, axis, [(i, i ^ bit) for i in range(SIZES[axis])])


def plain_dot(left, right):
    return jnp.dot(left, right, preferred_element_type=F32)


def contract_cols(left, right):
    return lax.dot_general(left, right, (((1,), (1,)), ((), ())), preferred_element_type=F32)


VMEM = 56 * 1024 * 1024
COST = pl.CostEstimate(flops=1000000, bytes_accessed=1000000, transcendentals=0)


def whole(shape):
    return pl.BlockSpec(shape, lambda *_: (0,) * len(shape), pipeline_mode=pl.Buffered(1))


def put_turned(target, rows):
    for z in range(2):
        for pair in range(8):
            start = z * 1024 + pair * 128
            block = rows[:, start : start + 128].T.astype(BF16)
            target[2 * pair, z] = block[:64]
            target[2 * pair + 1, z] = block[64:]


def normalise(hidden):
    average = jnp.mean(hidden, axis=-1, keepdims=True)
    centred = hidden - average
    inv_std = lax.rsqrt(jnp.mean(centred * centred, axis=-1, keepdims=True) + EPSILON)
    return centred * inv_std, inv_std


def second_kernel(hidden, cot, gain, shift, second_out, cot_turned, stats):
    rows = hidden[...].astype(F32)
    average = jnp.mean(rows, axis=-1, keepdims=True)
    centred = rows - average
    inv_std = lax.rsqrt(jnp.mean(centred * centred, axis=-1, keepdims=True) + EPSILON)
    second_out[...] = (centred * inv_std * gain[...] + shift[...]).astype(BF16)
    put_turned(cot_turned, cot[...].astype(F32))
    lane = lax.broadcasted_iota(jnp.int32, (rows.shape[0], 128), 1)
    stats[...] = jnp.where(lane < 64, average, inv_std)


def first_kernel(hidden, gain, shift, gain_two, shift_two, first_out, first_turned, second_turned):
    normed, _ = normalise(hidden[...].astype(F32))
    first = normed * gain[...] + shift[...]
    first_out[...] = first.astype(BF16)
    put_turned(first_turned, first)
    put_turned(second_turned, normed * gain_two[...] + shift_two[...])


def first_far_kernel(near, other, gain, shift, gain_two, shift_two, *refs):
    first_out, second_out, first_turned, second_turned = refs[2:]

    def step(rows):
        normed, _ = normalise(rows)
        first = normed * gain[...] + shift[...]
        second = normed * gain_two[...] + shift_two[...]
        first_out[...] = first.astype(BF16)
        second_out[...] = second.astype(BF16)
        put_turned(first_turned, first)
        put_turned(second_turned, second)

    @pl.when(pl.program_id(0) < 2)
    def _():
        step(near[0])

    @pl.when(pl.program_id(0) >= 2)
    def _():
        step(other[0])


TURNED = (16, 2, 64, 2 * TOK)


def norm_call(kernel, rows, n_rows, n_plain, n_turned, params, stats=False):
    plain = pl.BlockSpec((rows, D), lambda i: (i, 0))
    return pl.pallas_call(
        kernel,
        grid=(TOK // rows,),
        in_specs=[plain] * len(n_rows) + [whole((1, D))] * len(params),
        out_specs=[plain] * n_plain
        + [pl.BlockSpec((16, 2, 64, rows), lambda i: (0, 0, 0, i))] * n_turned
        + [pl.BlockSpec((rows, 128), lambda i: (i, 0))] * stats,
        out_shape=[jax.ShapeDtypeStruct((TOK, D), BF16)] * n_plain
        + [jax.ShapeDtypeStruct(TURNED, BF16)] * n_turned
        + [jax.ShapeDtypeStruct((TOK, 128), F32)] * stats,
        compiler_params=pltpu.CompilerParams(vmem_limit_bytes=VMEM),
        cost_estimate=COST,
    )(*n_rows, *(p.reshape(1, D) for p in params))


def first_far(near, other, params, held):
    rows = 128
    plain = pl.BlockSpec((rows, D), lambda i: (i, 0))
    return pl.pallas_call(
        first_far_kernel,
        grid=(TOK // rows,),
        in_specs=[
            pl.BlockSpec((1, rows, D), lambda i: (0, lax.min(i, 1), 0)),
            pl.BlockSpec((1, rows, D), lambda i: (0, lax.max(i - 2, 0), 0)),
        ]
        + [whole((1, D))] * 4
        + [pl.BlockSpec(memory_space=pl.ANY)] * 2,
        out_specs=[plain] * 2
        + [pl.BlockSpec((16, 2, 64, rows), lambda i: (0, 0, 0, i + TOK // rows))] * 2,
        out_shape=[jax.ShapeDtypeStruct((TOK, D), BF16)] * 2
        + [jax.ShapeDtypeStruct(TURNED, BF16)] * 2,
        input_output_aliases={6: 2, 7: 3},
        compiler_params=pltpu.CompilerParams(vmem_limit_bytes=VMEM),
        cost_estimate=COST,
    )(near, other, *(p.reshape(1, D) for p in params), *held)


def phi(upward):
    return 0.5 * (1.0 + lax.erf(upward * math.sqrt(0.5)))


def gelu_slope(upward, below):
    return below + upward * (jnp.exp(-0.5 * upward * upward) * (1.0 / math.sqrt(2.0 * math.pi)))


def as_row(block):
    return jnp.concatenate([block[i : i + 1, :] for i in range(block.shape[0])], axis=1)


def feed_kernel(second, cot_turned, weight, bias, act_out, slope_out, down_grad):
    upward = plain_dot(second[...], weight[...]) + as_row(bias[0])
    below = phi(upward)
    act = (upward * below).astype(BF16)
    act_out[...] = act
    slope_out[...] = gelu_slope(upward, below)
    down_grad[...] = plain_dot(cot_turned[...].reshape(D, TOK), act).reshape(16, 128, -1)


def feed(second, cot_turned, weight, bias):
    units, width = weight.shape[1], 512
    column = pl.BlockSpec((TOK, width), lambda j: (0, j))
    return pl.pallas_call(
        feed_kernel,
        grid=(units // width,),
        in_specs=[
            whole((TOK, D)),
            whole((16, 2, 64, TOK)),
            pl.BlockSpec((D, width), lambda j: (0, j)),
            pl.BlockSpec((1, width // 128, 128), lambda j: (j, 0, 0)),
        ],
        out_specs=[column, column, pl.BlockSpec((16, 128, width), lambda j: (0, 0, j))],
        out_shape=[
            jax.ShapeDtypeStruct((TOK, units), BF16),
            jax.ShapeDtypeStruct((TOK, units), F32),
            jax.ShapeDtypeStruct((16, 128, units), F32),
        ],
        compiler_params=pltpu.CompilerParams(vmem_limit_bytes=VMEM),
        cost_estimate=COST,
    )(second, cot_turned, weight, bias.reshape(-1, width // 128, 128))


def feed_back_kernel(cot, weight, slope, dense, up_grad, grad_mixed):
    up_grad[...] = (contract_cols(cot[...], weight[...]) * slope[...]).astype(BF16)

    @pl.when(pl.program_id(0) == 0)
    def _():
        grad_mixed[...] = contract_cols(cot[...], dense[...]).astype(BF16)


def feed_back(cot, weight, slope, dense):
    units, width = slope.shape[1], 512
    column = pl.BlockSpec((TOK, width), lambda j: (0, j))
    mixed = dense.shape[0]
    return pl.pallas_call(
        feed_back_kernel,
        grid=(units // width,),
        in_specs=[
            whole((TOK, D)),
            pl.BlockSpec((width, D), lambda j: (j, 0)),
            column,
            whole(dense.shape),
        ],
        out_specs=[column, pl.BlockSpec((TOK, mixed), lambda j: (0, 0))],
        out_shape=[
            jax.ShapeDtypeStruct((TOK, units), BF16),
            jax.ShapeDtypeStruct((TOK, mixed), BF16),
        ],
        compiler_params=pltpu.CompilerParams(vmem_limit_bytes=VMEM),
        cost_estimate=COST,
    )(cot, weight, slope, dense)


def cot_far_kernel(n, m, side, rows, weight, slope, dense, *refs):
    sums, (up_grad, grad_mixed, cot_turned), totals, low = (
        refs[:m],
        refs[m + n : m + n + 3],
        refs[m + n + 3 : -1],
        refs[-1],
    )

    @pl.when(pl.program_id(0) == 0)
    def _():
        low[...] = rows[...].astype(BF16)
        put_turned(cot_turned, rows[...])
        grad_mixed[...] = contract_cols(low[...], dense[...]).astype(BF16)

    up_grad[...] = (contract_cols(low[...], weight[...]) * slope[...]).astype(BF16)
    for k, total in enumerate(totals):
        total[...] = sums[2 * k][...] + sums[2 * k + 1][...]


def cot_far_half(k, side, rows, weight, slope, dense, held, sums=()):
    half, width = TOK // 2, 256
    steps = slope.shape[1] // width
    shapes = [
        jax.ShapeDtypeStruct((TOK, slope.shape[1]), BF16),
        jax.ShapeDtypeStruct((TOK, HD), BF16),
        jax.ShapeDtypeStruct(TURNED, BF16),
    ]
    piece = pl.BlockSpec((half, D // steps), lambda j, s: (0, j))
    first = 5 + len(sums)
    return pl.pallas_call(
        partial(cot_far_kernel, len(held), len(sums)),
        grid_spec=pltpu.PrefetchScalarGridSpec(
            num_scalar_prefetch=1,
            grid=(steps,),
            in_specs=[
                whole((half, D)),
                pl.BlockSpec((width, D), lambda j, s: (s[0] * steps + j, 0)),
                pl.BlockSpec((half, width), lambda j, s: (k, j)),
                pl.BlockSpec((HD, D), lambda j, s: (s[0], 0)),
            ]
            + [piece] * len(sums)
            + [pl.BlockSpec(memory_space=pl.ANY)] * len(held),
            out_specs=[
                pl.BlockSpec((half, width), lambda j, s: (k, j)),
                pl.BlockSpec((half, HD), lambda j, s: (k, 0)),
                pl.BlockSpec((16, 2, 64, half), lambda j, s: (0, 0, 0, 2 + k)),
            ]
            + [piece] * (len(sums) // 2),
            scratch_shapes=[pltpu.VMEM((half, D), BF16)],
        ),
        out_shape=shapes + [jax.ShapeDtypeStruct((half, D), F32)] * (len(sums) // 2),
        input_output_aliases={first: 2} if len(held) == 1 else {first + i: i for i in range(3)},
        compiler_params=pltpu.CompilerParams(vmem_limit_bytes=VMEM),
        cost_estimate=COST,
    )(side, rows, weight, slope, dense, *sums, *held)


def slope_far_kernel(side, second, weight, bias, slope):
    upward = plain_dot(second[...], weight[...]) + as_row(bias[0])
    slope[...] = gelu_slope(upward, phi(upward))


def slope_far(side, second, weight, bias):
    units, width = weight.shape[1] // 2, 512
    steps = units // width
    return pl.pallas_call(
        slope_far_kernel,
        grid_spec=pltpu.PrefetchScalarGridSpec(
            num_scalar_prefetch=1,
            grid=(steps,),
            in_specs=[
                whole((TOK, D)),
                pl.BlockSpec((D, width), lambda j, s: (0, s[0] * steps + j)),
                pl.BlockSpec((1, width // 128, 128), lambda j, s: (s[0] * steps + j, 0, 0)),
            ],
            out_specs=pl.BlockSpec((TOK, width), lambda j, s: (0, j)),
        ),
        out_shape=jax.ShapeDtypeStruct((TOK, units), F32),
        compiler_params=pltpu.CompilerParams(vmem_limit_bytes=VMEM),
        cost_estimate=COST,
    )(side, second, weight, bias.reshape(-1, width // 128, 128))


def turn(values, tables, sign):
    first = values[:, :128]
    cosine, rising, falling = tables
    first = (
        first * cosine[...]
        + (pltpu.roll(first, 32, 1) * rising[...] + pltpu.roll(first, 96, 1) * falling[...]) * sign
    )
    return jnp.concatenate([first, values[:, 128:]], axis=1)


def as_column(row):
    return jnp.broadcast_to(row, (8, row.shape[1])).T[:, 0:1]


def cosine_and_sine(angles):
    turns = jnp.floor(angles * (2.0 / math.pi) + 0.5)
    rest = ((angles - turns * 1.5703125) - turns * 4.837512969970703e-4) - turns * 7.549789954891882e-8
    square = rest * rest
    sine = ((-1.9515295891e-4 * square + 8.3321608736e-3) * square - 1.6666654611e-1) * square
    sine = sine * rest + rest
    cosine = (2.443315711809948e-5 * square - 1.388731625493765e-3) * square + 4.166664568298827e-2
    cosine = cosine * (square * square) - 0.5 * square + 1.0
    quarter = turns.astype(jnp.int32) & 3
    odd = (quarter & 1) == 1
    flipped = jnp.where(odd, sine, cosine), jnp.where(odd, cosine, sine)
    return (
        jnp.where((quarter == 1) | (quarter == 2), -flipped[0], flipped[0]),
        jnp.where(quarter >= 2, -flipped[1], flipped[1]),
    )


def project_kernel(place, first, weight, bias, marks, inverse, queries, keys, values, *tables):
    @pl.when(pl.program_id(0) == 0)
    def _():
        angles = inverse[...] * marks[1:2, :]
        cosine, sine = cosine_and_sine(angles)
        none, rest = jnp.zeros_like(sine), jnp.zeros((64, TOK), F32)
        tables[0][...] = jnp.concatenate([cosine, cosine, rest + 1.0], axis=0).T
        tables[1][...] = jnp.concatenate([none, sine, rest], axis=0).T
        tables[2][...] = jnp.concatenate([-sine, none, rest], axis=0).T

    head = pl.program_id(0) + place[0] * (2 - pl.num_programs(0))
    packed = plain_dot(first[...], weight[...]) + bias[pl.ds(head, 1), :]
    queries[...] = turn(packed[:, :HD], tables, 1.0).astype(BF16)
    keys[...] = turn(packed[:, HD : 2 * HD], tables, 1.0).astype(BF16)
    values[...] = packed[:, 2 * HD :].astype(BF16)


def project(place, heads, first, weight, bias, marks):
    inverse = jnp.asarray((10000.0 ** (-2.0 * np.arange(32) / ROT)).astype(np.float32).reshape(32, 1))
    at = (lambda h, s: h) if heads == 2 else (lambda h, s: s[0])
    column = pl.BlockSpec((TOK, HD), lambda h, s: (0, h))
    return pl.pallas_call(
        project_kernel,
        grid_spec=pltpu.PrefetchScalarGridSpec(
            num_scalar_prefetch=1,
            grid=(heads,),
            in_specs=[
                whole((TOK, D)),
                pl.BlockSpec((D, 3 * HD), lambda h, s: (0, at(h, s))),
                whole((2, 3 * HD)),
                whole((2, TOK)),
                whole((32, 1)),
            ],
            out_specs=[column] * 3 + [pl.BlockSpec((TOK, 128), lambda h, s: (0, 0))] * 3,
        ),
        out_shape=[jax.ShapeDtypeStruct((TOK, heads * HD), BF16)] * 3
        + [jax.ShapeDtypeStruct((TOK, 128), F32)] * 3,
        compiler_params=pltpu.CompilerParams(vmem_limit_bytes=VMEM),
        cost_estimate=COST,
    )(place, first, weight, bias, marks, inverse)


def attend_kernel(
    place, queries, keys, values, cosine, rising, falling, grad_mixed, marks, mixed_out, grad_out
):
    tables = (cosine, rising, falling)
    scale = 1.0 / math.sqrt(HD)
    queries, keys, values = queries[...], keys[...], values[...]
    segments = marks[0:1, :]

    def order(axis):
        return lax.rem(lax.broadcasted_iota(jnp.int32, (TOK, TOK), axis) + place[1], TOK)

    allowed = (as_column(segments) == segments) & (order(0) >= order(1))
    scores = jnp.where(allowed, contract_cols(queries, keys) * scale, NEGATIVE)
    top = jnp.max(scores, axis=-1, keepdims=True)
    weights = jnp.exp(scores - top)
    probs = weights / jnp.sum(weights, axis=-1, keepdims=True)
    probs_low = probs.astype(BF16)
    mixed_out[...] = plain_dot(probs_low, values).astype(BF16)
    grad_probs = contract_cols(grad_mixed[...], values)
    along = jnp.sum(probs * grad_probs, axis=-1, keepdims=True)
    grad_scores = (probs * (grad_probs - along)).astype(BF16)
    grad_query = plain_dot(grad_scores, keys) * scale
    grad_key = plain_dot(grad_scores.T, queries) * scale
    grad_value = plain_dot(probs_low.T, grad_mixed[...])
    grad_out[:, :HD] = turn(grad_query, tables, -1.0).astype(BF16)
    grad_out[:, HD : 2 * HD] = turn(grad_key, tables, -1.0).astype(BF16)
    grad_out[:, 2 * HD :] = grad_value.astype(BF16)


def attend(place, heads, projected, grad_mixed, marks):
    column = pl.BlockSpec((TOK, HD), lambda h, s: (0, h))
    return pl.pallas_call(
        attend_kernel,
        grid_spec=pltpu.PrefetchScalarGridSpec(
            num_scalar_prefetch=1,
            grid=(heads,),
            in_specs=[column] * 3
            + [whole((TOK, 128))] * 3
            + [column, whole((2, TOK))],
            out_specs=[column, pl.BlockSpec((TOK, 3 * HD), lambda h, s: (0, h))],
        ),
        out_shape=[
            jax.ShapeDtypeStruct((TOK, heads * HD), BF16),
            jax.ShapeDtypeStruct((TOK, heads * 3 * HD), BF16),
        ],
        compiler_params=pltpu.CompilerParams(vmem_limit_bytes=VMEM),
        cost_estimate=COST,
    )(place, *projected, grad_mixed, marks)


def put_halves(core, values, scratch, mine, other):
    scratch[...] = values
    half = TOK // 2
    mine[...] = scratch[pl.ds(pl.multiple_of(core[0] * half, half), half), :]
    other[...] = scratch[pl.ds(pl.multiple_of((1 - core[0]) * half, half), half), :]


def branch_kernel(core, mixed, act, dense, down, mine, other, scratch):
    total = plain_dot(act[...], down[...]) + plain_dot(mixed[...], dense[...])
    put_halves(core, total, scratch, mine, other)


def back_kernel(
    core, packed, up_grad, qkv, up, hidden, stats, gain, gain_two, mine, other, sums, scratch
):
    first = contract_cols(packed[...], qkv[...])
    second = contract_cols(up_grad[...], up[...])
    put_halves(core, first * gain[...] + second * gain_two[...], scratch, mine, other)
    normed = (hidden[...].astype(F32) - stats[:, 0:1]) * stats[:, 64:65]
    rows = [
        jnp.sum(v, axis=0, keepdims=True) for v in (first * normed, first, second * normed, second)
    ]
    sums[...] = jnp.concatenate(rows + [jnp.zeros((4, first.shape[1]), F32)], axis=0)


def halves_call(kernel, core, operands, specs, with_sums):
    width = 512
    half = pl.BlockSpec((TOK // 2, width), lambda j, s: (0, j))
    return pl.pallas_call(
        kernel,
        grid_spec=pltpu.PrefetchScalarGridSpec(
            num_scalar_prefetch=1,
            grid=(D // width,),
            in_specs=specs,
            out_specs=[half, half] + [pl.BlockSpec((8, width), lambda j, s: (0, j))] * with_sums,
            scratch_shapes=[pltpu.VMEM((TOK, width), F32)],
        ),
        out_shape=[jax.ShapeDtypeStruct((TOK // 2, D), F32)] * 2
        + [jax.ShapeDtypeStruct((8, D), F32)] * with_sums,
        compiler_params=pltpu.CompilerParams(vmem_limit_bytes=VMEM),
        cost_estimate=COST,
    )(core, *operands)


def branch_halves(core, mixed, act, dense, down):
    specs = [whole(mixed.shape), whole(act.shape)]
    specs += [pl.BlockSpec((w.shape[0], 512), lambda j, s: (0, j)) for w in (dense, down)]
    return halves_call(branch_kernel, core, (mixed, act, dense, down), specs, False)


def back_halves(core, packed, up_grad, qkv, up, hidden, stats, gain, gain_two):
    specs = [whole(packed.shape), whole(up_grad.shape)]
    specs += [pl.BlockSpec((512, w.shape[1]), lambda j, s: (j, 0)) for w in (qkv, up)]
    specs += [pl.BlockSpec((TOK, 512), lambda j, s: (0, j)), whole((TOK, 128))]
    specs += [pl.BlockSpec((1, 512), lambda j, s: (0, j))] * 2
    operands = (packed, up_grad, qkv, up, hidden, stats, gain.reshape(1, D), gain_two.reshape(1, D))
    return halves_call(back_kernel, core, operands, specs, True)


def final_kernel(n, half, branch, combined, hidden, cot, stats, bias, bias_too, *refs):
    output, input_grad = refs[n:]
    rows = hidden[...].astype(F32)
    output[...] = rows + branch[...] + bias[...] + bias_too[...]
    e = combined[...]
    inv_std = stats[:, 64:65]
    normed = (rows - stats[:, 0:1]) * inv_std
    input_grad[...] = cot[...].astype(F32) + inv_std * (
        e
        - jnp.mean(e, axis=-1, keepdims=True)
        - normed * jnp.mean(e * normed, axis=-1, keepdims=True)
    )


def final_half(half, branch, combined, hidden, cot, stats, biases, held):
    rows = 128
    steps = TOK // 2 // rows
    given = pl.BlockSpec((rows, D), lambda i, s: (i, 0))
    placed = pl.BlockSpec((rows, D), lambda i, s: (s[0] * steps + i, 0))
    return pl.pallas_call(
        partial(final_kernel, len(held)),
        grid_spec=pltpu.PrefetchScalarGridSpec(
            num_scalar_prefetch=1,
            grid=(steps,),
            in_specs=[given, given, placed, placed]
            + [pl.BlockSpec((rows, 128), lambda i, s: (s[0] * steps + i, 0))]
            + [whole((1, D))] * 2
            + [pl.BlockSpec(memory_space=pl.ANY)] * len(held),
            out_specs=[placed, placed],
        ),
        out_shape=[jax.ShapeDtypeStruct((TOK, D), F32)] * 2,
        input_output_aliases={8: 0, 9: 1} if held else {},
        compiler_params=pltpu.CompilerParams(vmem_limit_bytes=VMEM),
        cost_estimate=COST,
    )(half, branch, combined, hidden, cot, stats, *(b.reshape(1, D) for b in biases), *held)


def joint_kernel(side, *refs):
    lefts, rights, target, held, arrived = refs[:3], refs[3:9], refs[9], refs[10:13], refs[13]
    step = pl.program_id(0)
    copies = [pltpu.make_async_copy(lefts[k], held[k], arrived.at[k]) for k in range(3)]

    @pl.when(step == 0)
    def _():
        for copy in copies:
            copy.start()

    for k, (start, stop) in enumerate(((0, 4), (4, 5), (5, 8))):

        @pl.when(step == start)
        def _(k=k):
            copies[k].wait()

        @pl.when((step >= start) & (step < stop))
        def _(k=k):
            right = jnp.concatenate([rights[2 * k][...], rights[2 * k + 1][...]], axis=0)
            total = plain_dot(held[k][...].reshape(D, 2 * TOK), right)
            target[...] = total.reshape(16, 128, -1)


def joint(side, lefts, rights):
    width = 256
    specs = [pl.BlockSpec(memory_space=pl.ANY)] * 3
    for start, n in ((0, 4), (4, 1), (5, 3)):

        def near(j, s, start=start, n=n):
            return (0, s[0] * n + jnp.clip(j - start, 0, n - 1))

        def far(j, s, start=start, n=n):
            return (0, jnp.clip(j - start, 0, n - 1))

        specs += [pl.BlockSpec((TOK, width), near), pl.BlockSpec((TOK, width), far)]
    return pl.pallas_call(
        joint_kernel,
        grid_spec=pltpu.PrefetchScalarGridSpec(
            num_scalar_prefetch=1,
            grid=(8,),
            in_specs=specs,
            out_specs=pl.BlockSpec((16, 128, width), lambda j, s: (0, 0, j)),
            scratch_shapes=[pltpu.VMEM(TURNED, BF16)] * 3 + [pltpu.SemaphoreType.DMA((3,))],
        ),
        out_shape=jax.ShapeDtypeStruct((16, 128, 8 * width), F32),
        compiler_params=pltpu.CompilerParams(vmem_limit_bytes=VMEM),
        cost_estimate=COST,
    )(side, *lefts, *rights)


def assemble_kernel(side, near, far, up, dense, qkv):
    def put(low, high):
        up[...] = jnp.concatenate([low[:, :1024], high[:, :1024]], axis=1)
        dense[...] = jnp.concatenate([low[:, 1024:1280], high[:, 1024:1280]], axis=1).T
        qkv[...] = jnp.concatenate([low[:, 1280:], high[:, 1280:]], axis=1)

    @pl.when(side[0] == 0)
    def _():
        put(near[0], far[...])

    @pl.when(side[0] != 0)
    def _():
        put(far[...], near[0])


def assemble(side, near, far):
    shapes = ((64, 2048), (512, 64), (64, 1536))
    return pl.pallas_call(
        assemble_kernel,
        grid_spec=pltpu.PrefetchScalarGridSpec(
            num_scalar_prefetch=1,
            grid=(1,),
            in_specs=[
                pl.BlockSpec((1, 64, 2048), lambda i, s: (0, s[0], 0)),
                pl.BlockSpec((64, 2048), lambda i, s: (0, 0)),
            ],
            out_specs=[pl.BlockSpec(shape, lambda i, s: (0, 0)) for shape in shapes],
        ),
        out_shape=[jax.ShapeDtypeStruct(shape, F32) for shape in shapes],
        compiler_params=pltpu.CompilerParams(vmem_limit_bytes=VMEM),
        cost_estimate=COST,
    )(side, near, far)


def body(
    hidden_in,
    segment_ids,
    positions,
    ln1_gain,
    ln1_bias,
    qkv_weight,
    qkv_bias,
    dense_weight,
    dense_bias,
    ln2_gain,
    ln2_bias,
    fc1_weight,
    fc1_bias,
    fc2_weight,
    fc2_bias,
    cotangent,
):
    core = lax.axis_index("c")
    side = lax.axis_index("zl")
    half_rows = TOK // 2
    at_side = side.astype(jnp.int32).reshape(1)
    at_core = core.astype(jnp.int32).reshape(1)
    own_place = jnp.zeros((2,), jnp.int32)
    far_place = jnp.stack([side, core * half_rows]).astype(jnp.int32)
    after = lax.optimization_barrier
    params = (ln1_gain, ln1_bias, ln2_gain, ln2_bias)

    def of_core(values, which):
        return lax.dynamic_slice_in_dim(values, which * half_rows, half_rows, 0)

    marks = jnp.concatenate([segment_ids, positions]).astype(F32).reshape(1, 2 * TOK)
    hidden_sent = jnp.concatenate(
        [of_core(hidden_in, core).astype(F32), jnp.pad(marks, ((0, 7), (0, D - 2 * TOK)))], axis=0
    )
    hidden_pair = lax.all_gather(hidden_sent, "zl")

    second_in, cot_turned, stats = norm_call(
        second_kernel, 256, (hidden_in, cotangent), 1, 1, (ln2_gain, ln2_bias), stats=True
    )
    act_low, slope, down_grad = feed(second_in, cot_turned, fc1_weight, fc1_bias)
    down_sum = after(lax.psum_scatter(down_grad, ("x", "y"), scatter_dimension=0, tiled=True))
    _, cotangent, hidden_in = after((down_grad, cotangent, hidden_in))

    own_marks = marks.reshape(2, TOK)
    first_in, first_turned, second_turned = norm_call(first_kernel, 256, (hidden_in,), 1, 2, params)
    projected = project(own_place, 2, first_in, qkv_weight, qkv_bias, own_marks)
    grad_up, grad_mixed = feed_back(cotangent, fc2_weight, slope, dense_weight)
    mixed_low, grad_packed = attend(own_place, 2, projected, grad_mixed, own_marks)
    mixed_low, cot_sent = after((mixed_low, of_core(cotangent, core).astype(F32)))

    hidden_pair, mixed_low, cot_sent, grad_up = after((hidden_pair, mixed_low, cot_sent, grad_up))
    cot_got = send(cot_sent, "zl")
    hidden_got = lax.dynamic_slice_in_dim(hidden_pair, 1 - side, 1, 0)
    hidden_too = send(hidden_got, "c")

    def beside(hidden_got, hidden_too, first_turned, second_turned, mixed_low, grad_packed, grad_up):
        first_in, second_in, first_turned, second_turned = first_far(
            hidden_got, hidden_too, params, (first_turned, second_turned)
        )
        slope_side = slope_far(at_side, second_in, fc1_weight, fc1_bias)
        marks_got = hidden_got[0, half_rows, : 2 * TOK].reshape(2, 2, half_rows)
        marks_far = jnp.where(core == 0, marks_got, marks_got[:, ::-1]).reshape(2, TOK)
        projected_far = project(far_place, 1, first_in, qkv_weight, qkv_bias, marks_far)
        branches = branch_halves(at_core, mixed_low, act_low, dense_weight, fc2_weight)
        backs = back_halves(
            at_core,
            grad_packed,
            grad_up,
            qkv_weight,
            fc1_weight,
            hidden_in,
            stats,
            ln1_gain,
            ln2_gain,
        )
        return first_turned, second_turned, slope_side, marks_far, *branches, *backs, *projected_far

    (
        first_turned,
        second_turned,
        slope_side,
        marks_far,
        branch,
        branch_other,
        combined,
        combined_other,
        norms,
        *projected_far,
    ) = lax.cond(
        core > 1,
        beside,
        beside,
        hidden_got,
        hidden_too,
        first_turned,
        second_turned,
        mixed_low,
        grad_packed,
        grad_up,
    )

    slope_side, cot_got, branch_other, combined_other = after(
        (slope_side, cot_got, branch_other, combined_other)
    )
    cot_too = send(cot_got, "c")
    branch_too, combined_too = send(branch_other, "c"), send(combined_other, "c")
    held = cot_far_half(0, at_side, cot_got, fc2_weight, slope_side, dense_weight, (cot_turned,))
    *held, cot_too, branch_too, combined_too = after((*held, cot_too, branch_too, combined_too))
    grad_up_far, grad_mixed_far, cot_turned, branch, combined = cot_far_half(
        1,
        at_side,
        cot_too,
        fc2_weight,
        slope_side,
        dense_weight,
        held,
        (branch, branch_too, combined, combined_too),
    )
    branch = lax.psum(branch, "zh")
    combined = lax.psum(combined, "zh")
    mixed_far, grad_packed_far = attend(far_place, 1, projected_far, grad_mixed_far, marks_far)
    joint_grad = joint(
        at_side,
        (second_turned, cot_turned, first_turned),
        (grad_up, grad_up_far, mixed_low, mixed_far, grad_packed, grad_packed_far),
    )
    joint_grad, down_sum = after((joint_grad, down_sum))
    joint_sum = after(lax.psum_scatter(joint_grad, ("x", "y"), scatter_dimension=0, tiled=True))
    _, norms, grad_packed, grad_up, cotangent, down_sum = after(
        (joint_grad, norms, grad_packed, grad_up, cotangent, down_sum)
    )

    norms = norms[:4].reshape(4, 32, 64).transpose(1, 0, 2).reshape(32, 256)
    grad_out = cotangent.astype(F32)
    bias_sum = jnp.sum(grad_out, axis=0)
    qkv_bias_sum = jnp.sum(grad_packed.astype(F32), axis=0)
    up_bias_grad = jnp.sum(grad_up.astype(F32), axis=0)
    small = jnp.concatenate(
        [
            norms,
            bias_sum.reshape(32, 64),
            qkv_bias_sum.reshape(2, 32, 24).transpose(1, 0, 2).reshape(32, 48),
            up_bias_grad.reshape(16, 32, 4).transpose(1, 0, 2).reshape(32, 64),
            jnp.zeros((32, 80), F32),
        ],
        axis=1,
    )
    def of_side(values, which):
        return lax.dynamic_slice_in_dim(values[0], which * 64, 64, 0)

    down_far = send(of_side(down_sum, 1 - side), "zl")
    for axis in ("x", "y"):
        small = small + swap(small, axis, 1)
        small = small + swap(small, axis, 2)
        small, down_far = after((small, down_far))
    block = lax.axis_index("x") * 4 + lax.axis_index("y")
    own_small = lax.dynamic_slice_in_dim(small, side * 16 + block, 1, 0)
    far_small = lax.dynamic_slice_in_dim(small, (1 - side) * 16 + block, 1, 0)
    small = (own_small + send(far_small, "zl")).reshape(-1)

    norms = small[:256]
    norms = norms + send(norms, "c")
    norms = norms + send(norms, "zh")
    norms, branch, combined = after((norms, branch, combined))
    norms = norms.reshape(4, 64)
    bias_total = small[256:320]
    biases = (dense_bias, fc2_bias)
    own = (hidden_in, cotangent, stats, biases)
    branch_too, combined_too = send(branch, "c"), send(combined, "c")
    *finals, joint_sum = after((*final_half(at_core, branch, combined, *own, ()), joint_sum))
    output, input_grad = final_half(1 - at_core, branch_too, combined_too, *own, finals)

    down_sum = of_side(down_sum, side) + down_far
    joint_far = send(of_side(joint_sum, 1 - side), "zl")
    up_sum, dense_sum, qkv_sum = assemble(at_side, joint_sum, joint_far)
    return (
        output,
        input_grad,
        norms[0],
        norms[1],
        qkv_sum,
        small[320:368].reshape(2, 24),
        dense_sum,
        bias_total,
        norms[2],
        norms[3],
        up_sum,
        small[368:432].reshape(16, 4),
        down_sum.T,
        bias_total,
    )


def solution(mesh):
    fine = Mesh(mesh.devices.reshape(tuple(SIZES.values())), tuple(SIZES))
    return jax.shard_map(
        body,
        mesh=fine,
        in_specs=(
            P(DP, None),
            P(DP),
            P(DP),
            P(),
            P(),
            P(None, TENSOR),
            P(TENSOR, None),
            P(TENSOR, None),
            P(),
            P(),
            P(),
            P(None, TENSOR),
            P(TENSOR, None),
            P(TENSOR, None),
            P(),
            P(DP, None),
        ),
        out_specs=(
            P(DP, None),
            P(DP, None),
            P(DP),
            P(DP),
            P(DP, TENSOR),
            P(TENSOR, DP),
            P(TENSOR, DP),
            P(DP),
            P(DP),
            P(DP),
            P(DP, TENSOR),
            P(TENSOR, DP),
            P(TENSOR, DP),
            P(DP),
        ),
        check_vma=False,
    )
```

profile of v0, /device:TPU:0, one launch (start us, length us, event | category | flops | bytes accessed | tf_op | source)
XLA Modules:
  0.0 310.8 jit_solution(14431349783959815475)
XLA Ops:
  13.3 4.7 %shard_map.281 = (bf16[512,2048]{1,0:T(8,128)(2,1)}, bf16[16,2,64,1024]{3,2,1,0:T(8,128)(2,1)}, f32[512,128]{1,0:T(8,128)S(1)}) custom-call(bf16[512,2048]{1,0:T(8,128)(2,1)S(1)} %copy-done.2, bf16[512,2048]{1,0:T(8,128)(2,1)} %cot.4, f32[1,2048]{1,0:T(1,128)S(1)} %bitcast.52, f32[1,2048]{1,0:T(1,128)S(1)} %bitcast.64), custom_call_target="tpu_custom_call" | custom-call | flops 1000000 | bytes 1000000 | tf_op jit(solution)/shard_map/pallas_call | solution.py:111
  18.0 16.6 %shard_map.282 = (bf16[512,2048]{1,0:T(8,128)(2,1)}, f32[512,2048]{1,0:T(8,128)}, f32[16,128,2048]{2,1,0:T(8,128)}) custom-call(bf16[512,2048]{1,0:T(8,128)(2,1)} %get-tuple-element.280.second, bf16[16,2,64,1024]{3,2,1,0:T(8,128)(2,1)} %get-tuple-element.281.cot_turned.refs_0_, bf16[2048,2048]{1,0:T(8,128)(2,1)} %weight.5, f32[4,4,128]{2,1,0:T(4,128)S(1)} %bitcast.74), custom_call_target="tpu_custom_call" | custom-call | flops 1000000 | bytes 1000000 | tf_op jit(solution)/shard_map/pallas_call | solution.py:172
  36.0 3.9 %shard_map.283 = (bf16[512,2048]{1,0:T(8,128)(2,1)}, bf16[16,2,64,1024]{3,2,1,0:T(8,128)(2,1)}, bf16[16,2,64,1024]{3,2,1,0:T(8,128)(2,1)}) custom-call(bf16[512,2048]{1,0:T(8,128)(2,1)S(1)} %copy-done.2, f32[1,2048]{1,0:T(1,128)S(1)} %bitcast.59, f32[1,2048]{1,0:T(1,128)S(1)} %bitcast.71, f32[1,2048]{1,0:T(1,128)S(1)} %bitcast.53, f32[1,2048]{1,0:T(1,128)S(1)} %bitcast.65), custom_call_target="tpu_custom_call" | custom-call | flops 1000000 | bytes 1000000 | tf_op jit(solution)/shard_map/pallas_call | solution.py:111
  39.9 12.3 %shard_map.285 = (bf16[512,2048]{1,0:T(8,128)(2,1)}, bf16[512,512]{1,0:T(8,128)(2,1)}) custom-call(bf16[512,2048]{1,0:T(8,128)(2,1)} %cot.4, bf16[2048,2048]{1,0:T(8,128)(2,1)} %weight.9, f32[512,2048]{1,0:T(8,128)} %get-tuple-element.292.slope, bf16[512,2048]{1,0:T(8,128)(2,1)} %dense.5), custom_call_target="tpu_custom_call" | custom-call | flops 1000000 | bytes 1000000 | tf_op jit(solution)/shard_map/pallas_call | solution.py:204
  52.7 7.5 %shard_map.284 = (bf16[512,512]{1,0:T(8,128)(2,1)}, bf16[512,512]{1,0:T(8,128)(2,1)}, bf16[512,512]{1,0:T(8,128)(2,1)}, f32[512,128]{1,0:T(8,128)}, f32[512,128]{1,0:T(8,128)}, /*index=5*/f32[512,128]{1,0:T(8,128)}) custom-call(s32[2]{0:T(128)} %broadcast_1_place.2.place, bf16[512,2048]{1,0:T(8,128)(2,1)} %get-tuple-element.284.first, ...), custom_call_target="tpu_custom_call" | custom-call | flops 1000000 | bytes 1000000 | tf_op jit(solution)/shard_map/pallas_call | solution.py:358
  60.2 6.4 %shard_map.286 = (bf16[512,512]{1,0:T(8,128)(2,1)}, bf16[512,1536]{1,0:T(8,128)(2,1)S(1)}) custom-call(s32[2]{0:T(128)} %broadcast_1_place.2.place, bf16[512,512]{1,0:T(8,128)(2,1)} %get-tuple-element.285.queries, bf16[512,512]{1,0:T(8,128)(2,1)} %get-tuple-element.286.keys, bf16[512,512]{1,0:T(8,128)(2,1)} %get-tuple-element.287.values, ...), custom_call_target="tpu_custom_call" | custom-call | flops 1000000 | bytes 1000000 | tf_op jit(solution)/shard_map/pallas_call | solution.py:410
  68.4 6.8 %all-gather.3.cloned.1.call-done = f32[528,2048]{1,0:T(8,128)} async-done(((f32[264,2048]{1,0:T(8,128)}), f32[528,2048]{1,0:T(8,128)}) %all-gather.3.cloned.1.call-update) | async-done | bytes 4325392 | tf_op jit(solution)/shard_map/all_gather | solution.py:644
  75.2 3.3 %constant_dynamic-slice_fusion.1 = f32[1,264,2048]{2,1,0:T(8,128)} fusion(f32[2,264,2048]{2,1,0:T(8,128)} %bitcast.50, s32[]{:T(128)S(6)} %select_n.35), kind=kLoop, calls=%fused_computation.19 | loop fusion | bytes 4325380 | tf_op jit(solution)/shard_map/dynamic_slice | solution.py:662
  78.8 4.3 %collective-permute-done = f32[1,264,2048]{2,1,0:T(8,128)} collective-permute-done((f32[1,264,2048]{2,1,0:T(8,128)}, f32[1,264,2048]{2,1,0:T(8,128)}, u32[]{:S(2)}, u32[]{:S(2)}) %collective-permute-start) | collective-permute-done | bytes 2162720 | tf_op jit(solution)/shard_map/ppermute | solution.py:27
  83.1 43.5 %conditional.1 = (bf16[16,2,64,1024]{3,2,1,0:T(8,128)(2,1)}, bf16[16,2,64,1024]{3,2,1,0:T(8,128)(2,1)}, f32[512,1024]{1,0:T(8,128)S(1)}, f32[2,512]{1,0:T(2,128)...) conditional(s32[]{:T(128)} %convert_element_type.36, ...), branch_computations={%region_0.1_spmd, %region_1.2_spmd} | conditional | flops 5001025 | bytes 51276904 | solution.py:698
  83.9 7.2 %branch_0_fun.5 = (bf16[512,2048]{1,0:T(8,128)(2,1)}, bf16[512,2048]{1,0:T(8,128)(2,1)}, bf16[16,2,64,1024]{3,2,1,0:T(8,128)(2,1)}, bf16[16,2,64,1024]{3,2,1,0:T(8,128)(2,1)}) custom-call(f32[1,264,2048]{2,1,0:T(8,128)} %get-tuple-element.100.near, f32[1,264,2048]{2,1,0:T(8,128)} %get-tuple-element.101.other, ...), custom_call_target="tpu_custom_call", output_to_operand_aliasing={{2}: (6, {}), {3}: (7, {})} | custom-call | flops 1000000 | bytes 1000000 | tf_op jit(solution)/shard_map/cond/branch_0_fun/pallas_call | solution.py:129
  91.2 6.1 %branch_0_fun.9 = (bf16[512,256]{1,0:T(8,128)(2,1)}, bf16[512,256]{1,0:T(8,128)(2,1)}, bf16[512,256]{1,0:T(8,128)(2,1)}, f32[512,128]{1,0:T(8,128)}, f32[512,128]{1,0:T(8,128)}, /*index=5*/f32[512,128]{1,0:T(8,128)}) custom-call(s32[2]{0:T(128)S(1)} %get-tuple-element.130.place, bf16[512,2048]{1,0:T(8,128)(2,1)} %get-tuple-element.131.first, ...), custom_call_target="tpu_custom_call" | custom-call | flops 1000000 | bytes 1000000 | tf_op jit(solution)/shard_map/cond/branch_0_fun/pallas_call | solution.py:358
  97.3 13.9 %branch_0_fun.8 = (f32[256,2048]{1,0:T(8,128)}, f32[256,2048]{1,0:T(8,128)}, f32[8,2048]{1,0:T(8,128)S(1)}) custom-call(s32[1]{0:T(128)} %get-tuple-element.115.core, bf16[512,1536]{1,0:T(8,128)(2,1)S(1)} %get-tuple-element.122.packed, bf16[512,2048]{1,0:T(8,128)(2,1)} %get-tuple-element.123.up_grad, bf16[2048,1536]{1,0:T(8,128)(2,1)S(1)} %copy-done, ...), custom_call_target="tpu_custom_call" | custom-call | flops 1000000 | bytes 1000000 | tf_op jit(solution)/shard_map/cond/branch_0_fun/pallas_call | solution.py:457
  111.2 5.7 %branch_0_fun.6 = f32[512,1024]{1,0:T(8,128)S(1)} custom-call(s32[1]{0:T(128)} %get-tuple-element.110.side, bf16[512,2048]{1,0:T(8,128)(2,1)} %get-tuple-element.111.second, bf16[2048,2048]{1,0:T(8,128)(2,1)} %get-tuple-element.112.weight.up, f32[4,4,128]{2,1,0:T(4,128)S(1)} %bitcast.75), custom_call_target="tpu_custom_call" | custom-call | flops 1000000 | bytes 1000000 | tf_op jit(solution)/shard_map/cond/branch_0_fun/pallas_call | solution.py:288
  117.0 9.5 %branch_0_fun.7 = (f32[256,2048]{1,0:T(8,128)}, f32[256,2048]{1,0:T(8,128)}) custom-call(s32[1]{0:T(128)} %get-tuple-element.115.core, bf16[512,512]{1,0:T(8,128)(2,1)S(1)} %copy-done.15, bf16[512,2048]{1,0:T(8,128)(2,1)S(1)} %copy-done.12, bf16[512,2048]{1,0:T(8,128)(2,1)S(1)} %copy-done.7, bf16[2048,2048]{1,0:T(8,128)(2,1)} %get-tuple-element.119.down), custom_call_target="tpu_custom_call" | custom-call | flops 1000000 | bytes 1000000 | tf_op jit(solution)/shard_map/cond/branch_0_fun/pallas_call | solution.py:457
  127.4 6.5 %shard_map.287 = (bf16[512,1024]{1,0:T(8,128)(2,1)}, bf16[512,256]{1,0:T(8,128)(2,1)}, bf16[16,2,64,1024]{3,2,1,0:T(8,128)(2,1)}) custom-call(s32[1]{0:T(128)} %bitcast.11.side, f32[256,2048]{1,0:T(8,128)} %collective-permute-done.1.rows, bf16[2048,2048]{1,0:T(8,128)(2,1)} %weight.9, ...), custom_call_target="tpu_custom_call", output_to_operand_aliasing={{2}: (5, {})} | custom-call | flops 1000000 | bytes 1000000 | tf_op jit(solution)/shard_map/pallas_call | solution.py:252
  134.3 3.0 collective-permute-done.2.rows
  137.4 9.5 %shard_map.288 = (bf16[512,1024]{1,0:T(8,128)(2,1)}, bf16[512,256]{1,0:T(8,128)(2,1)}, bf16[16,2,64,1024]{3,2,1,0:T(8,128)(2,1)}, f32[256,2048]{1,0:T(8,128)}, f32[256,2048]{1,0:T(8,128)}) custom-call(s32[1]{0:T(128)} %bitcast.11.side, f32[256,2048]{1,0:T(8,128)} %collective-permute-done.2.rows, ...), custom_call_target="tpu_custom_call", output_to_operand_aliasing={{0}: (9, {}), {1}: (10, {}), {2}: (11, {})} | custom-call | flops 1000000 | bytes 1000000 | tf_op jit(solution)/shard_map/pallas_call | solution.py:252
  147.2 5.2 %shard_map.289 = (bf16[512,256]{1,0:T(8,128)(2,1)}, bf16[512,768]{1,0:T(8,128)(2,1)}) custom-call(s32[2]{0:T(128)S(1)} %pad_add_fusion.place, bf16[512,256]{1,0:T(8,128)(2,1)} %get-tuple-element.329.queries, bf16[512,256]{1,0:T(8,128)(2,1)} %get-tuple-element.330.keys, bf16[512,256]{1,0:T(8,128)(2,1)} %get-tuple-element.331.values, ...), custom_call_target="tpu_custom_call" | custom-call | flops 1000000 | bytes 1000000 | tf_op jit(solution)/shard_map/pallas_call | solution.py:410
  152.4 17.3 %shard_map.290 = f32[16,128,2048]{2,1,0:T(8,128)} custom-call(s32[1]{0:T(128)} %bitcast.11.side, bf16[16,2,64,1024]{3,2,1,0:T(8,128)(2,1)} %get-tuple-element.306.refs_0_, bf16[16,2,64,1024]{3,2,1,0:T(8,128)(2,1)} %get-tuple-element.326.refs_1_, bf16[16,2,64,1024]{3,2,1,0:T(8,128)(2,1)} %get-tuple-element.327.refs_2_, bf16[512,2048]{1,0:T(8,128)(2,1)S(1)} %copy-done.9, ...), custom_call_target="tpu_custom_call" | custom-call | flops 1000000 | bytes 1000000 | tf_op jit(solution)/shard_map/pallas_call | solution.py:560
  178.5 4.0 %collective-permute-done.5 = f32[32,512]{1,0:T(8,128)S(1)} collective-permute-done((f32[32,512]{1,0:T(8,128)S(1)}, f32[32,512]{1,0:T(8,128)S(1)}, u32[]{:S(2)}, u32[]{:S(2)}) %collective-permute-start.5) | collective-permute-done | bytes 65568 | tf_op jit(solution)/shard_map/ppermute | solution.py:31
  185.0 4.6 %collective-permute-done.6 = f32[32,512]{1,0:T(8,128)S(1)} collective-permute-done((f32[32,512]{1,0:T(8,128)S(1)}, f32[32,512]{1,0:T(8,128)S(1)}, u32[]{:S(2)}, u32[]{:S(2)}) %collective-permute-start.6) | collective-permute-done | bytes 65568 | tf_op jit(solution)/shard_map/ppermute | solution.py:31
  189.7 8.1 %collective-permute-done.7 = f32[64,2048]{1,0:T(8,128)S(1)} collective-permute-done((f32[64,2048]{1,0:T(8,128)}, f32[64,2048]{1,0:T(8,128)S(1)}, u32[]{:S(2)}, u32[]{:S(2)}) %collective-permute-start.7) | collective-permute-done | bytes 524320 | tf_op jit(solution)/shard_map/ppermute | solution.py:27
  198.9 4.3 %collective-permute-done.8 = f32[32,512]{1,0:T(8,128)S(1)} collective-permute-done((f32[32,512]{1,0:T(8,128)S(1)}, f32[32,512]{1,0:T(8,128)S(1)}, u32[]{:S(2)}, u32[]{:S(2)}) %collective-permute-start.8) | collective-permute-done | bytes 65568 | tf_op jit(solution)/shard_map/ppermute | solution.py:31
  203.3 2.7 collective-permute-start.9
  206.0 4.5 %collective-permute-done.9 = f32[32,512]{1,0:T(8,128)S(1)} collective-permute-done((f32[32,512]{1,0:T(8,128)S(1)}, f32[32,512]{1,0:T(8,128)S(1)}, u32[]{:S(2)}, u32[]{:S(2)}) %collective-permute-start.9) | collective-permute-done | bytes 65568 | tf_op jit(solution)/shard_map/ppermute | solution.py:31
  210.9 3.3 %collective-permute-done.10 = f32[1,512]{1,0:T(1,128)S(1)} collective-permute-done((f32[1,512]{1,0:T(1,128)S(1)}, f32[1,512]{1,0:T(1,128)S(1)}, u32[]{:S(2)}, u32[]{:S(2)}) %collective-permute-start.10) | collective-permute-done | bytes 2080 | tf_op jit(solution)/shard_map/ppermute | solution.py:27
  220.5 55.2 %all-reduce.6.cloned.1.call-done = (f32[256,2048]{1,0:T(8,128)}, f32[256,2048]{1,0:T(8,128)}) async-done(((f32[256,2048]{1,0:T(8,128)}, f32[256,2048]{1,0:T(8,128)}), (f32[256,2048]{1,0:T(8,128)}, f32[256,2048]{1,0:T(8,128)})) %all-reduce.6.cloned.1.call-update) | async-done | bytes 4194320 | tf_op jit(solution)/shard_map/psum | solution.py:728
  276.3 4.4 %shard_map.291 = (f32[512,2048]{1,0:T(8,128)}, f32[512,2048]{1,0:T(8,128)}) custom-call(s32[1]{0:T(128)} %bitcast.10.half, f32[256,2048]{1,0:T(8,128)} %get-tuple-element.352.branch, f32[256,2048]{1,0:T(8,128)} %get-tuple-element.353.combined, bf16[512,2048]{1,0:T(8,128)(2,1)S(1)} %copy-done.3, bf16[512,2048]{1,0:T(8,128)(2,1)} %cot.4, ...), custom_call_target="tpu_custom_call" | custom-call | flops 1000000 | bytes 1000000 | tf_op jit(solution)/shard_map/pallas_call | solution.py:507
  280.7 2.7 reduce-scatter.9.cloned.1.call-done.near
  290.9 4.3 %shard_map.292 = (f32[512,2048]{1,0:T(8,128)}, f32[512,2048]{1,0:T(8,128)}) custom-call(s32[1]{0:T(128)S(6)} %sub.4.half, f32[256,2048]{1,0:T(8,128)} %collective-permute-done.13.branch, f32[256,2048]{1,0:T(8,128)} %collective-permute-done.14.combined, bf16[512,2048]{1,0:T(8,128)(2,1)S(1)} %copy-done.3, ...), custom_call_target="tpu_custom_call", output_to_operand_aliasing={{0}: (8, {}), {1}: (9, {})} | custom-call | flops 1000000 | bytes 1000000 | tf_op jit(solution)/shard_map/pallas_call | solution.py:507
  295.2 3.6 %collective-permute-done.15.far = f32[64,2048]{1,0:T(8,128)} collective-permute-done((f32[64,2048]{1,0:T(8,128)}, f32[64,2048]{1,0:T(8,128)}, u32[]{:S(2)}, u32[]{:S(2)}) %collective-permute-start.15) | collective-permute-done | bytes 524320 | tf_op jit(solution)/shard_map/ppermute | solution.py:27
  (139 shorter events, 43.3 us)
Async XLA Ops:
  8.0 67.2 %all-gather.3.cloned.1.call-start = ((), (), s32[]{:S(2)}) async-start(), calls=%async_computation.2 | async-start | bytes 6488064 | tf_op jit(solution)/shard_map/all_gather | solution.py:644
  11.7 158.0 %reduce-scatter.7.cloned.1.call-start = ((), (), s32[]{:S(2)}) async-start(), calls=%async_computation.3 | async-start | bytes 17825792
  34.7 241.1 %all-reduce.6.cloned.1.call-start = ((), (), s32[]{:S(2)}) async-start(), calls=%async_computation.5 | async-start | bytes 8388608 | tf_op jit(solution)/shard_map/psum | solution.py:728
  39.9 12.8 %slice-start = ((s8[6291456]{0:T(1024)(128)(4,1)}), s8[4194304]{0:T(1024)(128)(4,1)S(1)}, s32[]{:S(2)}) async-start(s8[6291456]{0:T(1024)(128)(4,1)} %bitcast.48), calls=%async_computation.6 | async-start | bytes 8388608
  39.9 12.8 %slice-start.1 = ((s8[6291456]{0:T(1024)(128)(4,1)}), s8[2097152]{0:T(1024)(128)(4,1)S(1)}, s32[]{:S(2)}) async-start(s8[6291456]{0:T(1024)(128)(4,1)} %bitcast.48), calls=%async_computation.7 | async-start | bytes 4194304
  39.9 12.8 %copy-start.23 = (f32[32,1]{1,0:T(8,128)S(1)}, f32[32,1]{1,0:T(8,128)}, u32[]{:S(2)}) copy-start(f32[32,1]{1,0:T(8,128)} %constant.54.clone.inverse) | copy-start | bytes 388
  39.9 12.8 %copy-start.29 = (f32[2,768]{1,0:T(2,128)S(1)}, f32[2,768]{1,0:T(2,128)}, u32[]{:S(2)}) copy-start(f32[2,768]{1,0:T(2,128)} %bias.1) | copy-start | bytes 18436
  60.2 6.4 %copy-start.4 = (bf16[512,2048]{1,0:T(8,128)(2,1)S(1)}, bf16[512,2048]{1,0:T(8,128)(2,1)}, u32[]{:S(2)}) copy-start(bf16[512,2048]{1,0:T(8,128)(2,1)} %cot.4) | copy-start | bytes 6291460
  66.6 16.5 %copy-start.10 = (bf16[512,1536]{1,0:T(8,128)(2,1)}, bf16[512,1536]{1,0:T(8,128)(2,1)S(1)}, u32[]{:S(2)}) copy-start(bf16[512,1536]{1,0:T(8,128)(2,1)S(1)} %get-tuple-element.344.refs_7_) | copy-start | bytes 4718596
  78.5 4.6 %collective-permute-start = (f32[1,264,2048]{2,1,0:T(8,128)}, f32[1,264,2048]{2,1,0:T(8,128)}, u32[]{:S(2)}, u32[]{:S(2)}) collective-permute-start(f32[1,264,2048]{2,1,0:T(8,128)} %constant_dynamic-slice_fusion.1), channel_id=1, source_target_pairs={{0,1},{1,0},{2,3},{3,2},{4,5},{5,4},{6,7},{7,6},{8,9},{9,8},{10,11... | collective-permute-start | bytes 6488072 | tf_op jit(solution)/shard_map/ppermute | solution.py:27
  78.5 48.4 %collective-permute-start.1 = (f32[256,2048]{1,0:T(8,128)}, f32[256,2048]{1,0:T(8,128)}, u32[]{:S(2)}, u32[]{:S(2)}) collective-permute-start(f32[256,2048]{1,0:T(8,128)} %dynamic-slice_convert_fusion), channel_id=1, source_target_pairs={{0,64},{64,0},{1,65},{65,1},{2,66},{66,2},{3,67},{67,3},{4,68},{68... | collective-permute-start | bytes 6291464 | tf_op jit(solution)/shard_map/ppermute | solution.py:27
  91.2 6.1 %copy-start = (bf16[2048,1536]{1,0:T(8,128)(2,1)S(1)}, bf16[2048,1536]{1,0:T(8,128)(2,1)}, u32[]{:S(2)}) copy-start(bf16[2048,1536]{1,0:T(8,128)(2,1)} %get-tuple-element.124.qkv.weight) | copy-start | bytes 18874372 | tf_op jit(solution)/shard_map/cond
  126.8 10.5 %copy-start.6 = (bf16[512,2048]{1,0:T(8,128)(2,1)S(1)}, bf16[512,2048]{1,0:T(8,128)(2,1)}, u32[]{:S(2)}) copy-start(bf16[512,2048]{1,0:T(8,128)(2,1)} %dense.5) | copy-start | bytes 6291460
  126.8 7.3 %collective-permute-start.3 = (f32[256,2048]{1,0:T(8,128)}, f32[256,2048]{1,0:T(8,128)S(1)}, u32[]{:S(2)}, u32[]{:S(2)}) collective-permute-start(f32[256,2048]{1,0:T(8,128)} %get-tuple-element.316), channel_id=1, source_target_pairs={{0,1},{1,0},{2,3},{3,2},{4,5},{5,4},{6,7},{7,6},{8,9},{9,8},{10,11... | collective-permute-start | bytes 6291464 | tf_op jit(solution)/shard_map/ppermute | solution.py:27
  126.8 7.5 %collective-permute-start.4 = (f32[256,2048]{1,0:T(8,128)}, f32[256,2048]{1,0:T(8,128)}, u32[]{:S(2)}, u32[]{:S(2)}) collective-permute-start(f32[256,2048]{1,0:T(8,128)} %get-tuple-element.317), channel_id=1, source_target_pairs={{0,1},{1,0},{2,3},{3,2},{4,5},{5,4},{6,7},{7,6},{8,9},{9,8},{10,11... | collective-permute-start | bytes 6291464 | tf_op jit(solution)/shard_map/ppermute | solution.py:27
  127.4 10.0 %collective-permute-start.2 = (f32[256,2048]{1,0:T(8,128)}, f32[256,2048]{1,0:T(8,128)}, u32[]{:S(2)}, u32[]{:S(2)}) collective-permute-start(f32[256,2048]{1,0:T(8,128)} %collective-permute-done.1.rows), channel_id=1, source_target_pairs={{0,1},{1,0},{2,3},{3,2},{4,5},{5,4},{6,7},{7,6},{8,9},{9,8},{10,11... | collective-permute-start | bytes 6291464 | tf_op jit(solution)/shard_map/ppermute | solution.py:27
  146.9 136.5 %reduce-scatter.9.cloned.1.call-start = ((), (), s32[]{:S(2)}) async-start(), calls=%async_computation.4 | async-start | bytes 17825792
  171.8 25.9 %collective-permute-start.7 = (f32[64,2048]{1,0:T(8,128)}, f32[64,2048]{1,0:T(8,128)S(1)}, u32[]{:S(2)}, u32[]{:S(2)}) collective-permute-start(f32[64,2048]{1,0:T(8,128)} %dynamic-slice_bitcast_fusion.1), channel_id=1, source_target_pairs={{0,64},{64,0},{1,65},{65,1},{2,66},{66,2},{3,67},{67,3},{4,68},{68... | collective-permute-start | bytes 1572872 | tf_op jit(solution)/shard_map/ppermute | solution.py:27
  174.3 102.0 %copy-start.3 = (bf16[512,2048]{1,0:T(8,128)(2,1)S(1)}, bf16[512,2048]{1,0:T(8,128)(2,1)}, u32[]{:S(2)}) copy-start(bf16[512,2048]{1,0:T(8,128)(2,1)} %hidden.4) | copy-start | bytes 6291460
  177.3 5.1 %collective-permute-start.5 = (f32[32,512]{1,0:T(8,128)S(1)}, f32[32,512]{1,0:T(8,128)S(1)}, u32[]{:S(2)}, u32[]{:S(2)}) collective-permute-start(f32[32,512]{1,0:T(8,128)S(1)} %concatenate.27), channel_id=1, source_target_pairs={{0,16},{16,0},{32,48},{48,32},{1,17},{17,1},{33,49},{49,33},{2,18}... | collective-permute-start | bytes 196616 | tf_op jit(solution)/shard_map/ppermute | solution.py:31
  182.4 7.2 %collective-permute-start.6 = (f32[32,512]{1,0:T(8,128)S(1)}, f32[32,512]{1,0:T(8,128)S(1)}, u32[]{:S(2)}, u32[]{:S(2)}) collective-permute-start(f32[32,512]{1,0:T(8,128)S(1)} %add.66), channel_id=1, source_target_pairs={{0,32},{16,48},{32,0},{48,16},{1,33},{17,49},{33,1},{49,17},{2,34}... | collective-permute-start | bytes 196616 | tf_op jit(solution)/shard_map/ppermute | solution.py:31
  197.7 78.5 %copy-start.20 = (f32[64,2048]{1,0:T(8,128)}, f32[64,2048]{1,0:T(8,128)S(1)}, u32[]{:S(2)}) copy-start(f32[64,2048]{1,0:T(8,128)S(1)} %collective-permute-done.7) | copy-start | bytes 1572868
  197.7 5.5 %collective-permute-start.8 = (f32[32,512]{1,0:T(8,128)S(1)}, f32[32,512]{1,0:T(8,128)S(1)}, u32[]{:S(2)}, u32[]{:S(2)}) collective-permute-start(f32[32,512]{1,0:T(8,128)S(1)} %add.67), channel_id=1, source_target_pairs={{0,4},{4,0},{8,12},{12,8},{1,5},{5,1},{9,13},{13,9},{2,6},{6,2},{1... | collective-permute-start | bytes 196616 | tf_op jit(solution)/shard_map/ppermute | solution.py:31
  203.3 7.2 %collective-permute-start.9 = (f32[32,512]{1,0:T(8,128)S(1)}, f32[32,512]{1,0:T(8,128)S(1)}, u32[]{:S(2)}, u32[]{:S(2)}) collective-permute-start(f32[32,512]{1,0:T(8,128)S(1)} %add.69), channel_id=1, source_target_pairs={{0,8},{4,12},{8,0},{12,4},{1,9},{5,13},{9,1},{13,5},{2,10},{6,14},... | collective-permute-start | bytes 196616 | tf_op jit(solution)/shard_map/ppermute | solution.py:31
  210.5 3.7 %collective-permute-start.10 = (f32[1,512]{1,0:T(1,128)S(1)}, f32[1,512]{1,0:T(1,128)S(1)}, u32[]{:S(2)}, u32[]{:S(2)}) collective-permute-start(f32[1,512]{1,0:T(1,128)S(1)} %constant_dynamic-slice_fusion), channel_id=1, source_target_pairs={{0,64},{64,0},{1,65},{65,1},{2,66},{66,2},{3,67},{67,3},{4,68},{68... | collective-permute-start | bytes 6152 | tf_op jit(solution)/shard_map/ppermute | solution.py:27
  214.2 1.2 collective-permute-start.11
  215.5 5.1 %collective-permute-start.12 = (f32[256]{0:T(256)S(1)}, f32[256]{0:T(256)S(1)}, u32[]{:S(2)}, u32[]{:S(2)}) collective-permute-start(f32[256]{0:T(256)S(1)} %add.77), channel_id=1, source_target_pairs={{0,2},{2,0},{1,3},{3,1},{4,6},{6,4},{5,7},{7,5},{8,10},{10,8},{9,1... | collective-permute-start | bytes 3080 | tf_op jit(solution)/shard_map/ppermute | solution.py:27
  275.8 15.1 %collective-permute-start.13 = (f32[256,2048]{1,0:T(8,128)}, f32[256,2048]{1,0:T(8,128)}, u32[]{:S(2)}, u32[]{:S(2)}) collective-permute-start(f32[256,2048]{1,0:T(8,128)} %get-tuple-element.352.branch), channel_id=1, source_target_pairs={{0,1},{1,0},{2,3},{3,2},{4,5},{5,4},{6,7},{7,6},{8,9},{9,8},{10,11... | collective-permute-start | bytes 6291464 | tf_op jit(solution)/shard_map/ppermute | solution.py:27
  275.8 15.1 %collective-permute-start.14 = (f32[256,2048]{1,0:T(8,128)}, f32[256,2048]{1,0:T(8,128)}, u32[]{:S(2)}, u32[]{:S(2)}) collective-permute-start(f32[256,2048]{1,0:T(8,128)} %get-tuple-element.353.combined), channel_id=1, source_target_pairs={{0,1},{1,0},{2,3},{3,2},{4,5},{5,4},{6,7},{7,6},{8,9},{9,8},{10,11... | collective-permute-start | bytes 6291464 | tf_op jit(solution)/shard_map/ppermute | solution.py:27
  276.3 10.5 %copy-start.19 = (f32[1,128,2048]{2,1,0:T(8,128)S(1)}, f32[1,128,2048]{2,1,0:T(8,128)}, u32[]{:S(2)}) copy-start(f32[1,128,2048]{2,1,0:T(8,128)} %reduce-scatter.7.cloned.1.call-done) | copy-start | bytes 3145732
  285.3 13.6 %collective-permute-start.15 = (f32[64,2048]{1,0:T(8,128)}, f32[64,2048]{1,0:T(8,128)}, u32[]{:S(2)}, u32[]{:S(2)}) collective-permute-start(f32[64,2048]{1,0:T(8,128)} %dynamic-slice_bitcast_fusion), channel_id=1, source_target_pairs={{0,64},{64,0},{1,65},{65,1},{2,66},{66,2},{3,67},{67,3},{4,68},{68... | collective-permute-start | bytes 1572872 | tf_op jit(solution)/shard_map/ppermute | solution.py:27
  289.5 13.4 %copy-start.32 = (f32[64]{0:T(128)}, f32[64]{0:T(128)S(1)}, u32[]{:S(2)}) copy-start(f32[64]{0:T(128)S(1)} %get-tuple-element.475) | copy-start | bytes 772
  (17 other events, 53.3 us)
Sparse Core Ops, SparseCore 0:
  11.9 63.2 all-gather.2
  147.0 128.6 all-reduce.5
Sparse Core Ops, SparseCore 1:
  34.8 112.7 reduce-scatter.6
  169.9 113.5 reduce-scatter.8
where the time goes:
time: 312 us; the launch traced here: 311 us
  Pallas kernels  143 us (46%)
  waiting for transfers between devices  109 us (35%)
  local copies, waits for them, and re-layouts  16.9 us (5%)
  between operations  15.8 us (5%)
  starting transfers between devices  13.8 us (4%)
  other arithmetic  11.7 us (4%)
    psum x1, waiting for transfers between devices, body(): branch = lax.psum(branch, 'zh')  55.2 us
    ppermute x12, waiting for transfers between devices, send(): return lax.ppermute(value, axis, [(i, (i + step) % n) for i in range(n)])  26.9 us
    pallas_call x2, Pallas kernels, halves_call(): pl.pallas_call(kernel, grid_spec=pltpu.PrefetchScalarGridSpec(num_scalar_...  23.4 us
    ppermute x4, waiting for transfers between devices, swap(): return lax.ppermute(value, axis, [(i, i ^ bit) for i in range(SIZES[axis])])  17.4 us
    pallas_call x1, Pallas kernels, joint(): pl.pallas_call(joint_kernel, grid_spec=pltpu.PrefetchScalarGridSpec(num_s...  17.3 us
    pallas_call x1, Pallas kernels, feed(): pl.pallas_call(feed_kernel, grid=(units // width,), in_specs=[whole((TOK,...  16.6 us
    pallas_call x2, Pallas kernels, cot_far_half(): pl.pallas_call(partial(cot_far_kernel, len(held), len(sums)), grid_spec=p...  16 us
    pallas_call x2, Pallas kernels, project(): pl.pallas_call(project_kernel, grid_spec=pltpu.PrefetchScalarGridSpec(num...  13.6 us
  transfers between devices with their start and end apart: 20, of which 17 were waited for; matrix products, arithmetic and copies ran while one was open for 6% of the time, Pallas kernels for 45%

commit v1 on v0

--- a/solution.py
+++ b/solution.py
@@ -189,35 +189,22 @@
     )(second, cot_turned, weight, bias.reshape(-1, width // 128, 128))
 
 
-def feed_back_kernel(cot, weight, slope, dense, up_grad, grad_mixed):
+def feed_back_kernel(cot, weight, slope, up_grad):
     up_grad[...] = (contract_cols(cot[...], weight[...]) * slope[...]).astype(BF16)
 
-    @pl.when(pl.program_id(0) == 0)
-    def _():
-        grad_mixed[...] = contract_cols(cot[...], dense[...]).astype(BF16)
-
-
-def feed_back(cot, weight, slope, dense):
+
+def feed_back(cot, weight, slope):
     units, width = slope.shape[1], 512
     column = pl.BlockSpec((TOK, width), lambda j: (0, j))
-    mixed = dense.shape[0]
     return pl.pallas_call(
         feed_back_kernel,
         grid=(units // width,),
-        in_specs=[
-            whole((TOK, D)),
-            pl.BlockSpec((width, D), lambda j: (j, 0)),
-            column,
-            whole(dense.shape),
-        ],
-        out_specs=[column, pl.BlockSpec((TOK, mixed), lambda j: (0, 0))],
-        out_shape=[
-            jax.ShapeDtypeStruct((TOK, units), BF16),
-            jax.ShapeDtypeStruct((TOK, mixed), BF16),
-        ],
-        compiler_params=pltpu.CompilerParams(vmem_limit_bytes=VMEM),
-        cost_estimate=COST,
-    )(cot, weight, slope, dense)
+        in_specs=[whole((TOK, D)), pl.BlockSpec((width, D), lambda j: (j, 0)), column],
+        out_specs=column,
+        out_shape=jax.ShapeDtypeStruct((TOK, units), BF16),
+        compiler_params=pltpu.CompilerParams(vmem_limit_bytes=VMEM),
+        cost_estimate=COST,
+    )(cot, weight, slope)
 
 
 def cot_far_kernel(n, m, side, rows, weight, slope, dense, *refs):
@@ -376,9 +363,8 @@
     )(place, first, weight, bias, marks, inverse)
 
 
-def attend_kernel(
-    place, queries, keys, values, cosine, rising, falling, grad_mixed, marks, mixed_out, grad_out
-):
+def attend_kernel(place, queries, keys, values, cosine, rising, falling, marks, *refs):
+    given, (mixed_out, grad_out) = refs[:-2], refs[-2:]
     tables = (cosine, rising, falling)
     scale = 1.0 / math.sqrt(HD)
     queries, keys, values = queries[...], keys[...], values[...]
@@ -394,18 +380,21 @@
     probs = weights / jnp.sum(weights, axis=-1, keepdims=True)
     probs_low = probs.astype(BF16)
     mixed_out[...] = plain_dot(probs_low, values).astype(BF16)
-    grad_probs = contract_cols(grad_mixed[...], values)
+    grad_mixed = given[0][...]
+    if len(given) == 2:
+        grad_mixed = contract_cols(grad_mixed, given[1][...]).astype(BF16)
+    grad_probs = contract_cols(grad_mixed, values)
     along = jnp.sum(probs * grad_probs, axis=-1, keepdims=True)
     grad_scores = (probs * (grad_probs - along)).astype(BF16)
     grad_query = plain_dot(grad_scores, keys) * scale
     grad_key = plain_dot(grad_scores.T, queries) * scale
-    grad_value = plain_dot(probs_low.T, grad_mixed[...])
+    grad_value = plain_dot(probs_low.T, grad_mixed)
     grad_out[:, :HD] = turn(grad_query, tables, -1.0).astype(BF16)
     grad_out[:, HD : 2 * HD] = turn(grad_key, tables, -1.0).astype(BF16)
     grad_out[:, 2 * HD :] = grad_value.astype(BF16)
 
 
-def attend(place, heads, projected, grad_mixed, marks):
+def attend(place, heads, projected, given, marks):
     column = pl.BlockSpec((TOK, HD), lambda h, s: (0, h))
     return pl.pallas_call(
         attend_kernel,
@@ -414,7 +403,8 @@
             grid=(heads,),
             in_specs=[column] * 3
             + [whole((TOK, 128))] * 3
-            + [column, whole((2, TOK))],
+            + [whole((2, TOK))]
+            + ([column] if len(given) == 1 else [whole((TOK, D)), pl.BlockSpec((HD, D), lambda h, s: (h, 0))]),
             out_specs=[column, pl.BlockSpec((TOK, 3 * HD), lambda h, s: (0, h))],
         ),
         out_shape=[
@@ -423,7 +413,7 @@
         ],
         compiler_params=pltpu.CompilerParams(vmem_limit_bytes=VMEM),
         cost_estimate=COST,
-    )(place, *projected, grad_mixed, marks)
+    )(place, *projected, marks, *given)
 
 
 def put_halves(core, values, scratch, mine, other):
@@ -575,7 +565,7 @@
 def assemble_kernel(side, near, far, up, dense, qkv):
     def put(low, high):
         up[...] = jnp.concatenate([low[:, :1024], high[:, :1024]], axis=1)
-        dense[...] = jnp.concatenate([low[:, 1024:1280], high[:, 1024:1280]], axis=1).T
+        dense[...] = jnp.concatenate([low[:, 1024:1280], high[:, 1024:1280]], axis=1)
         qkv[...] = jnp.concatenate([low[:, 1280:], high[:, 1280:]], axis=1)
 
     @pl.when(side[0] == 0)
@@ -588,7 +578,7 @@
 
 
 def assemble(side, near, far):
-    shapes = ((64, 2048), (512, 64), (64, 1536))
+    shapes = ((64, 2048), (64, 512), (64, 1536))
     return pl.pallas_call(
         assemble_kernel,
         grid_spec=pltpu.PrefetchScalarGridSpec(
@@ -653,16 +643,19 @@
     own_marks = marks.reshape(2, TOK)
     first_in, first_turned, second_turned = norm_call(first_kernel, 256, (hidden_in,), 1, 2, params)
     projected = project(own_place, 2, first_in, qkv_weight, qkv_bias, own_marks)
-    grad_up, grad_mixed = feed_back(cotangent, fc2_weight, slope, dense_weight)
-    mixed_low, grad_packed = attend(own_place, 2, projected, grad_mixed, own_marks)
-    mixed_low, cot_sent = after((mixed_low, of_core(cotangent, core).astype(F32)))
-
-    hidden_pair, mixed_low, cot_sent, grad_up = after((hidden_pair, mixed_low, cot_sent, grad_up))
+    mixed_low, grad_packed = attend(
+        own_place, 2, projected, (cotangent, dense_weight), own_marks
+    )
+    branch, branch_other = branch_halves(at_core, mixed_low, act_low, dense_weight, fc2_weight)
+    branch = branch + send(branch_other, "c")
+    branch, cot_sent = after((branch, of_core(cotangent, core).astype(F32)))
+
+    hidden_pair, branch, cot_sent = after((hidden_pair, branch, cot_sent))
     cot_got = send(cot_sent, "zl")
     hidden_got = lax.dynamic_slice_in_dim(hidden_pair, 1 - side, 1, 0)
     hidden_too = send(hidden_got, "c")
 
-    def beside(hidden_got, hidden_too, first_turned, second_turned, mixed_low, grad_packed, grad_up):
+    def beside(hidden_got, hidden_too, first_turned, second_turned, slope, grad_packed):
         first_in, second_in, first_turned, second_turned = first_far(
             hidden_got, hidden_too, params, (first_turned, second_turned)
         )
@@ -670,7 +663,7 @@
         marks_got = hidden_got[0, half_rows, : 2 * TOK].reshape(2, 2, half_rows)
         marks_far = jnp.where(core == 0, marks_got, marks_got[:, ::-1]).reshape(2, TOK)
         projected_far = project(far_place, 1, first_in, qkv_weight, qkv_bias, marks_far)
-        branches = branch_halves(at_core, mixed_low, act_low, dense_weight, fc2_weight)
+        grad_up = feed_back(cotangent, fc2_weight, slope)
         backs = back_halves(
             at_core,
             grad_packed,
@@ -682,15 +675,14 @@
             ln1_gain,
             ln2_gain,
         )
-        return first_turned, second_turned, slope_side, marks_far, *branches, *backs, *projected_far
+        return first_turned, second_turned, slope_side, marks_far, grad_up, *backs, *projected_far
 
     (
         first_turned,
         second_turned,
         slope_side,
         marks_far,
-        branch,
-        branch_other,
+        grad_up,
         combined,
         combined_other,
         norms,
@@ -703,19 +695,16 @@
         hidden_too,
         first_turned,
         second_turned,
-        mixed_low,
+        slope,
         grad_packed,
-        grad_up,
-    )
-
-    slope_side, cot_got, branch_other, combined_other = after(
-        (slope_side, cot_got, branch_other, combined_other)
-    )
+    )
+
+    slope_side, cot_got, combined_other = after((slope_side, cot_got, combined_other))
     cot_too = send(cot_got, "c")
-    branch_too, combined_too = send(branch_other, "c"), send(combined_other, "c")
+    combined_too = send(combined_other, "c")
     held = cot_far_half(0, at_side, cot_got, fc2_weight, slope_side, dense_weight, (cot_turned,))
-    *held, cot_too, branch_too, combined_too = after((*held, cot_too, branch_too, combined_too))
-    grad_up_far, grad_mixed_far, cot_turned, branch, combined = cot_far_half(
+    *held, cot_too, combined_too = after((*held, cot_too, combined_too))
+    grad_up_far, grad_mixed_far, cot_turned, combined = cot_far_half(
         1,
         at_side,
         cot_too,
@@ -723,11 +712,12 @@
         slope_side,
         dense_weight,
         held,
-        (branch, branch_too, combined, combined_too),
-    )
+        (combined, combined_too),
+    )
+    branch, combined = after((branch, combined))
     branch = lax.psum(branch, "zh")
     combined = lax.psum(combined, "zh")
-    mixed_far, grad_packed_far = attend(far_place, 1, projected_far, grad_mixed_far, marks_far)
+    mixed_far, grad_packed_far = attend(far_place, 1, projected_far, (grad_mixed_far,), marks_far)
     joint_grad = joint(
         at_side,
         (second_turned, cot_turned, first_turned),
@@ -789,7 +779,7 @@
         norms[1],
         qkv_sum,
         small[320:368].reshape(2, 24),
-        dense_sum,
+        dense_sum.T,
         bias_total,
         norms[2],
         norms[3],

time: 312 us -> 313 us (level)
  waiting for transfers between devices: 109 us -> 94.9 us
  starting transfers between devices: 13.8 us -> 24.5 us
    ppermute x12, starting transfers between devices: 5.71 us -> 13.3 us  [send(): return lax.ppermute(value, axis, [(i, (i + step) % n) for i in range(n)])]
    all_gather x1, waiting for transfers between devices: 6.83 us -> 0.01 us  [body(): hidden_pair = lax.all_gather(hidden_sent, 'zl')]
    ppermute x12, waiting for transfers between devices: 26.9 us -> 20.3 us  [send(): return lax.ppermute(value, axis, [(i, (i + step) % n) for i in range(n)])]
    add x0 -> x1, other arithmetic: none -> 3.24 us  [body(): branch = branch + send(branch_other, 'c')]
    ppermute x4, waiting for transfers between devices: 17.4 us -> 14.3 us  [swap(): return lax.ppermute(value, axis, [(i, i ^ bit) for i in range(SIZES[axis])])]
  transfers between devices with their start and end apart: 20 -> 20, of which waited for: 17 -> 14; matrix products, arithmetic and copies ran while one was open for 6% -> 8% of each run, Pallas kernels for 45% -> 46%
where the time goes in v1:
time: 313 us; the launch traced here: 312 us
  Pallas kernels  145 us (46%)
  waiting for transfers between devices  94.9 us (30%)
  starting transfers between devices  24.5 us (8%)
  local copies, waits for them, and re-layouts  17.8 us (6%)
  between operations  15.8 us (5%)
  other arithmetic  14.7 us (5%)
    psum x1, waiting for transfers between devices, body(): branch = lax.psum(branch, 'zh')  56.3 us
    pallas_call x2, Pallas kernels, halves_call(): pl.pallas_call(kernel, grid_spec=pltpu.PrefetchScalarGridSpec(num_scalar_...  24.4 us
    ppermute x12, waiting for transfers between devices, send(): return lax.ppermute(value, axis, [(i, (i + step) % n) for i in range(n)])  20.3 us
    pallas_call x1, Pallas kernels, feed(): pl.pallas_call(feed_kernel, grid=(units // width,), in_specs=[whole((TOK,...  16.6 us
    pallas_call x1, Pallas kernels, joint(): pl.pallas_call(joint_kernel, grid_spec=pltpu.PrefetchScalarGridSpec(num_s...  16.3 us
    pallas_call x2, Pallas kernels, cot_far_half(): pl.pallas_call(partial(cot_far_kernel, len(held), len(sums)), grid_spec=p...  14.8 us
    ppermute x4, waiting for transfers between devices, swap(): return lax.ppermute(value, axis, [(i, i ^ bit) for i in range(SIZES[axis])])  14.3 us
    pallas_call x2, Pallas kernels, project(): pl.pallas_call(project_kernel, grid_spec=pltpu.PrefetchScalarGridSpec(num...  14.3 us
  transfers between devices with their start and end apart: 20, of which 14 were waited for; matrix products, arithmetic and copies ran while one was open for 8% of the time, Pallas kernels for 46%

profile of v1, /device:TPU:0, one launch (start us, length us, event | category | flops | bytes accessed | tf_op | source)
XLA Modules:
  0.0 312.3 jit_solution(14132055221176328127)
XLA Ops:
  13.3 4.7 %shard_map.281 = (bf16[512,2048]{1,0:T(8,128)(2,1)}, bf16[16,2,64,1024]{3,2,1,0:T(8,128)(2,1)}, f32[512,128]{1,0:T(8,128)S(1)}) custom-call(bf16[512,2048]{1,0:T(8,128)(2,1)} %hidden.4, bf16[512,2048]{1,0:T(8,128)(2,1)S(1)} %copy-done, f32[1,2048]{1,0:T(1,128)S(1)} %bitcast.55, f32[1,2048]{1,0:T(1,128)S(1)} %bitcast.67), custom_call_target="tpu_custom_call" | custom-call | flops 1000000 | bytes 1000000 | tf_op jit(solution)/shard_map/pallas_call | solution.py:111
  18.0 16.6 %shard_map.282 = (bf16[512,2048]{1,0:T(8,128)(2,1)}, f32[512,2048]{1,0:T(8,128)}, f32[16,128,2048]{2,1,0:T(8,128)}) custom-call(bf16[512,2048]{1,0:T(8,128)(2,1)} %get-tuple-element.261.second, bf16[16,2,64,1024]{3,2,1,0:T(8,128)(2,1)} %get-tuple-element.262.cot_turned.refs_0_, bf16[2048,2048]{1,0:T(8,128)(2,1)} %weight.4, f32[4,4,128]{2,1,0:T(4,128)S(1)} %bitcast.77), custom_call_target="tpu_custom_call" | custom-call | flops 1000000 | bytes 1000000 | tf_op jit(solution)/shard_map/pallas_call | solution.py:172
  35.9 5.1 %shard_map.283 = (bf16[512,2048]{1,0:T(8,128)(2,1)}, bf16[16,2,64,1024]{3,2,1,0:T(8,128)(2,1)}, bf16[16,2,64,1024]{3,2,1,0:T(8,128)(2,1)}) custom-call(bf16[512,2048]{1,0:T(8,128)(2,1)} %hidden.4, f32[1,2048]{1,0:T(1,128)S(1)} %bitcast.62, f32[1,2048]{1,0:T(1,128)S(1)} %bitcast.74, f32[1,2048]{1,0:T(1,128)S(1)} %bitcast.56, f32[1,2048]{1,0:T(1,128)S(1)} %bitcast.68), custom_call_target="tpu_custom_call" | custom-call | flops 1000000 | bytes 1000000 | tf_op jit(solution)/shard_map/pallas_call | solution.py:111
  41.6 8.4 %shard_map.284 = (bf16[512,512]{1,0:T(8,128)(2,1)}, bf16[512,512]{1,0:T(8,128)(2,1)}, bf16[512,512]{1,0:T(8,128)(2,1)}, f32[512,128]{1,0:T(8,128)}, f32[512,128]{1,0:T(8,128)}, /*index=5*/f32[512,128]{1,0:T(8,128)}) custom-call(s32[2]{0:T(128)} %broadcast_1_place.2.place, bf16[512,2048]{1,0:T(8,128)(2,1)} %get-tuple-element.265.first, ...), custom_call_target="tpu_custom_call" | custom-call | flops 1000000 | bytes 1000000 | tf_op jit(solution)/shard_map/pallas_call | solution.py:345
  50.0 9.0 %shard_map.285 = (bf16[512,512]{1,0:T(8,128)(2,1)}, bf16[512,1536]{1,0:T(8,128)(2,1)}) custom-call(s32[2]{0:T(128)} %broadcast_1_place.2.place, bf16[512,512]{1,0:T(8,128)(2,1)} %get-tuple-element.266.queries, bf16[512,512]{1,0:T(8,128)(2,1)} %get-tuple-element.267.keys, bf16[512,512]{1,0:T(8,128)(2,1)} %get-tuple-element.268.values, ...), custom_call_target="tpu_custom_call" | custom-call | flops 1000000 | bytes 1000000 | tf_op jit(solution)/shard_map/pallas_call | solution.py:399
  59.0 10.9 %shard_map.286 = (f32[256,2048]{1,0:T(8,128)}, f32[256,2048]{1,0:T(8,128)}) custom-call(s32[1]{0:T(128)} %bitcast.10.core.half, bf16[512,512]{1,0:T(8,128)(2,1)} %get-tuple-element.273.mixed.refs_5_, bf16[512,2048]{1,0:T(8,128)(2,1)} %get-tuple-element.274.act, bf16[512,2048]{1,0:T(8,128)(2,1)} %dense.5, bf16[2048,2048]{1,0:T(8,128)(2,1)} %weight.7), custom_call_target="tpu_custom_call" | custom-call | flops 1000000 | bytes 1000000 | tf_op jit(solution)/shard_map/pallas_call | solution.py:447
  71.5 2.8 collective-permute-done
  74.3 3.2 %add.68 = f32[256,2048]{1,0:T(8,128)} add(f32[256,2048]{1,0:T(8,128)S(1)} %copy-done.9, f32[256,2048]{1,0:T(8,128)} %collective-permute-done) | non-fusion elementwise | flops 524288 | bytes 6291456 | tf_op jit(solution)/shard_map/add | solution.py:650
  77.6 3.2 %constant_dynamic-slice_fusion.1 = f32[1,264,2048]{2,1,0:T(8,128)} fusion(f32[2,264,2048]{2,1,0:T(8,128)} %bitcast.53, s32[]{:T(128)S(6)} %select_n.35), kind=kLoop, calls=%fused_computation.19 | loop fusion | bytes 4325380 | tf_op jit(solution)/shard_map/dynamic_slice | solution.py:655
  85.4 44.7 %conditional.1 = (bf16[16,2,64,1024]{3,2,1,0:T(8,128)(2,1)}, bf16[16,2,64,1024]{3,2,1,0:T(8,128)(2,1)}, f32[512,1024]{1,0:T(8,128)}, f32[2,512]{1,0:T(2,128)S(1)...) conditional(s32[]{:T(128)} %convert_element_type.36, ...), branch_computations={%region_0.1_spmd, %region_1.2_spmd} | conditional | flops 5001025 | bytes 40791128 | solution.py:690
  86.2 7.0 %branch_0_fun.5 = (bf16[512,2048]{1,0:T(8,128)(2,1)}, bf16[512,2048]{1,0:T(8,128)(2,1)}, bf16[16,2,64,1024]{3,2,1,0:T(8,128)(2,1)}, bf16[16,2,64,1024]{3,2,1,0:T(8,128)(2,1)}) custom-call(f32[1,264,2048]{2,1,0:T(8,128)} %get-tuple-element.92.near, f32[1,264,2048]{2,1,0:T(8,128)} %get-tuple-element.93.other, ...), custom_call_target="tpu_custom_call", output_to_operand_aliasing={{2}: (6, {}), {3}: (7, {})} | custom-call | flops 1000000 | bytes 1000000 | tf_op jit(solution)/shard_map/cond/branch_0_fun/pallas_call | solution.py:129
  93.3 5.8 %branch_0_fun.9 = (bf16[512,256]{1,0:T(8,128)(2,1)}, bf16[512,256]{1,0:T(8,128)(2,1)}, bf16[512,256]{1,0:T(8,128)(2,1)}, f32[512,128]{1,0:T(8,128)}, f32[512,128]{1,0:T(8,128)}, /*index=5*/f32[512,128]{1,0:T(8,128)}) custom-call(s32[2]{0:T(128)S(1)} %get-tuple-element.118.place, bf16[512,2048]{1,0:T(8,128)(2,1)} %get-tuple-element.119.first, ...), custom_call_target="tpu_custom_call" | custom-call | flops 1000000 | bytes 1000000 | tf_op jit(solution)/shard_map/cond/branch_0_fun/pallas_call | solution.py:345
  99.2 6.8 %branch_0_fun.6 = f32[512,1024]{1,0:T(8,128)} custom-call(s32[1]{0:T(128)} %get-tuple-element.102.side, bf16[512,2048]{1,0:T(8,128)(2,1)} %get-tuple-element.103.second, bf16[2048,2048]{1,0:T(8,128)(2,1)} %get-tuple-element.104.weight.up, f32[4,4,128]{2,1,0:T(4,128)S(1)} %bitcast.78), custom_call_target="tpu_custom_call" | custom-call | flops 1000000 | bytes 1000000 | tf_op jit(solution)/shard_map/cond/branch_0_fun/pallas_call | solution.py:275
  106.0 10.5 %branch_0_fun.7.up_grad = bf16[512,2048]{1,0:T(8,128)(2,1)} custom-call(bf16[512,2048]{1,0:T(8,128)(2,1)} %copy-done.2, bf16[2048,2048]{1,0:T(8,128)(2,1)} %get-tuple-element.108.weight, f32[512,2048]{1,0:T(8,128)} %get-tuple-element.109.slope), custom_call_target="tpu_custom_call" | custom-call | flops 1000000 | bytes 1000000 | tf_op jit(solution)/shard_map/cond/branch_0_fun/pallas_call | solution.py:199
  116.5 13.6 %branch_0_fun.8 = (f32[256,2048]{1,0:T(8,128)}, f32[256,2048]{1,0:T(8,128)}, f32[8,2048]{1,0:T(8,128)S(1)}) custom-call(s32[1]{0:T(128)} %get-tuple-element.110.core, bf16[512,1536]{1,0:T(8,128)(2,1)S(1)} %copy-done.6, bf16[512,2048]{1,0:T(8,128)(2,1)} %branch_0_fun.7.up_grad, bf16[2048,1536]{1,0:T(8,128)(2,1)S(1)} %bitcast.50, ...), custom_call_target="tpu_custom_call" | custom-call | flops 1000000 | bytes 1000000 | tf_op jit(solution)/shard_map/cond/branch_0_fun/pallas_call | solution.py:447
  130.7 6.6 %shard_map.287 = (bf16[512,1024]{1,0:T(8,128)(2,1)}, bf16[512,256]{1,0:T(8,128)(2,1)}, bf16[16,2,64,1024]{3,2,1,0:T(8,128)(2,1)}) custom-call(s32[1]{0:T(128)} %bitcast.11.side, f32[256,2048]{1,0:T(8,128)} %collective-permute-done.2.rows, bf16[2048,2048]{1,0:T(8,128)(2,1)} %weight.7, ...), custom_call_target="tpu_custom_call", output_to_operand_aliasing={{2}: (5, {})} | custom-call | flops 1000000 | bytes 1000000 | tf_op jit(solution)/shard_map/pallas_call | solution.py:239
  139.4 8.2 %shard_map.288 = (bf16[512,1024]{1,0:T(8,128)(2,1)}, bf16[512,256]{1,0:T(8,128)(2,1)}, bf16[16,2,64,1024]{3,2,1,0:T(8,128)(2,1)}, f32[256,2048]{1,0:T(8,128)}) custom-call(s32[1]{0:T(128)} %bitcast.11.side, f32[256,2048]{1,0:T(8,128)} %copy-done.11, bf16[2048,2048]{1,0:T(8,128)(2,1)} %weight.7, ...), custom_call_target="tpu_custom_call", output_to_operand_aliasing={{0}: (7, {}), {1}: (8, {}), {2}: (9, {})} | custom-call | flops 1000000 | bytes 1000000 | tf_op jit(solution)/shard_map/pallas_call | solution.py:239
  148.7 4.5 %shard_map.289 = (bf16[512,256]{1,0:T(8,128)(2,1)}, bf16[512,768]{1,0:T(8,128)(2,1)}) custom-call(s32[2]{0:T(128)S(1)} %pad_add_fusion.place, bf16[512,256]{1,0:T(8,128)(2,1)S(1)} %copy-done.13, bf16[512,256]{1,0:T(8,128)(2,1)S(1)} %copy-done.14, bf16[512,256]{1,0:T(8,128)(2,1)S(1)} %copy-done.15, f32[512,128]{1,0:T(8,128)} %get-tuple-element.308.cosine, ...), custom_call_target="tpu_custom_call" | custom-call | flops 1000000 | bytes 1000000 | tf_op jit(solution)/shard_map/pallas_call | solution.py:399
  153.2 16.3 %shard_map.290 = f32[16,128,2048]{2,1,0:T(8,128)} custom-call(s32[1]{0:T(128)} %bitcast.11.side, bf16[16,2,64,1024]{3,2,1,0:T(8,128)(2,1)} %get-tuple-element.285.refs_0_, bf16[16,2,64,1024]{3,2,1,0:T(8,128)(2,1)} %get-tuple-element.301.refs_1_, bf16[16,2,64,1024]{3,2,1,0:T(8,128)(2,1)} %get-tuple-element.302.refs_2_, bf16[512,2048]{1,0:T(8,128)(2,1)S(1)} %copy-done.4, ...), custom_call_target="tpu_custom_call" | custom-call | flops 1000000 | bytes 1000000 | tf_op jit(solution)/shard_map/pallas_call | solution.py:550
  180.9 2.9 collective-permute-done.5
  183.8 3.6 %collective-permute-start.6 = (f32[32,512]{1,0:T(8,128)S(1)}, f32[32,512]{1,0:T(8,128)S(1)}, u32[]{:S(2)}, u32[]{:S(2)}) collective-permute-start(f32[32,512]{1,0:T(8,128)S(1)} %add.70), channel_id=1, source_target_pairs={{0,32},{16,48},{32,0},{48,16},{1,33},{17,49},{33,1},{49,17},{2,34}... | collective-permute-start | bytes 196616 | tf_op jit(solution)/shard_map/ppermute | solution.py:31
  187.3 3.7 %collective-permute-done.6 = f32[32,512]{1,0:T(8,128)S(1)} collective-permute-done((f32[32,512]{1,0:T(8,128)S(1)}, f32[32,512]{1,0:T(8,128)S(1)}, u32[]{:S(2)}, u32[]{:S(2)}) %collective-permute-start.6) | collective-permute-done | bytes 65568 | tf_op jit(solution)/shard_map/ppermute | solution.py:31
  191.0 6.8 %collective-permute-done.7 = f32[64,2048]{1,0:T(8,128)S(1)} collective-permute-done((f32[64,2048]{1,0:T(8,128)}, f32[64,2048]{1,0:T(8,128)S(1)}, u32[]{:S(2)}, u32[]{:S(2)}) %collective-permute-start.7) | collective-permute-done | bytes 524320 | tf_op jit(solution)/shard_map/ppermute | solution.py:27
  199.6 4.1 %collective-permute-done.8 = f32[32,512]{1,0:T(8,128)S(1)} collective-permute-done((f32[32,512]{1,0:T(8,128)S(1)}, f32[32,512]{1,0:T(8,128)S(1)}, u32[]{:S(2)}, u32[]{:S(2)}) %collective-permute-start.8) | collective-permute-done | bytes 65568 | tf_op jit(solution)/shard_map/ppermute | solution.py:31
  203.7 3.6 %collective-permute-start.9 = (f32[32,512]{1,0:T(8,128)S(1)}, f32[32,512]{1,0:T(8,128)S(1)}, u32[]{:S(2)}, u32[]{:S(2)}) collective-permute-start(f32[32,512]{1,0:T(8,128)S(1)} %add.73), channel_id=1, source_target_pairs={{0,8},{4,12},{8,0},{12,4},{1,9},{5,13},{9,1},{13,5},{2,10},{6,14},... | collective-permute-start | bytes 196616 | tf_op jit(solution)/shard_map/ppermute | solution.py:31
  207.4 3.6 %collective-permute-done.9 = f32[32,512]{1,0:T(8,128)S(1)} collective-permute-done((f32[32,512]{1,0:T(8,128)S(1)}, f32[32,512]{1,0:T(8,128)S(1)}, u32[]{:S(2)}, u32[]{:S(2)}) %collective-permute-start.9) | collective-permute-done | bytes 65568 | tf_op jit(solution)/shard_map/ppermute | solution.py:31
  216.0 4.1 %collective-permute-start.12 = (f32[256]{0:T(256)S(1)}, f32[256]{0:T(256)S(1)}, u32[]{:S(2)}, u32[]{:S(2)}) collective-permute-start(f32[256]{0:T(256)S(1)} %add.81), channel_id=1, source_target_pairs={{0,2},{2,0},{1,3},{3,1},{4,6},{6,4},{5,7},{7,5},{8,10},{10,8},{9,1... | collective-permute-start | bytes 3080 | tf_op jit(solution)/shard_map/ppermute | solution.py:27
  221.7 56.3 %all-reduce.6.cloned.1.call-done = (f32[256,2048]{1,0:T(8,128)}, f32[256,2048]{1,0:T(8,128)}) async-done(((f32[256,2048]{1,0:T(8,128)}, f32[256,2048]{1,0:T(8,128)}), (f32[256,2048]{1,0:T(8,128)}, f32[256,2048]{1,0:T(8,128)})) %all-reduce.6.cloned.1.call-update) | async-done | bytes 4194320 | tf_op jit(solution)/shard_map/psum | solution.py:718
  278.5 4.3 %shard_map.291 = (f32[512,2048]{1,0:T(8,128)}, f32[512,2048]{1,0:T(8,128)}) custom-call(s32[1]{0:T(128)} %bitcast.10.core.half, f32[256,2048]{1,0:T(8,128)} %get-tuple-element.330.branch, f32[256,2048]{1,0:T(8,128)} %get-tuple-element.331.combined, bf16[512,2048]{1,0:T(8,128)(2,1)} %hidden.4, bf16[512,2048]{1,0:T(8,128)(2,1)S(1)} %copy-done.1, ...), custom_call_target="tpu_custom_call" | custom-call | flops 1000000 | bytes 1000000 | tf_op jit(solution)/shard_map/pallas_call | solution.py:497
  282.8 3.9 %reduce-scatter.9.cloned.1.call-done.near = f32[1,128,2048]{2,1,0:T(8,128)} async-done(((f32[16,128,2048]{2,1,0:T(8,128)}), f32[1,128,2048]{2,1,0:T(8,128)}) %reduce-scatter.9.cloned.1.call-update) | async-done | bytes 1048592 | tf_op jit(solution)/shard_map/optimization_barrier | solution.py:769
  294.2 4.3 %shard_map.292 = (f32[512,2048]{1,0:T(8,128)}, f32[512,2048]{1,0:T(8,128)}) custom-call(s32[1]{0:T(128)S(6)} %sub.4.half, f32[256,2048]{1,0:T(8,128)} %collective-permute-done.13.branch, f32[256,2048]{1,0:T(8,128)} %collective-permute-done.14.combined, bf16[512,2048]{1,0:T(8,128)(2,1)} %hidden.4, ...), custom_call_target="tpu_custom_call", output_to_operand_aliasing={{0}: (8, {}), {1}: (9, {})} | custom-call | flops 1000000 | bytes 1000000 | tf_op jit(solution)/shard_map/pallas_call | solution.py:497
  298.5 3.7 %collective-permute-done.15.far = f32[64,2048]{1,0:T(8,128)} collective-permute-done((f32[64,2048]{1,0:T(8,128)}, f32[64,2048]{1,0:T(8,128)}, u32[]{:S(2)}, u32[]{:S(2)}) %collective-permute-start.15) | collective-permute-done | bytes 524320 | tf_op jit(solution)/shard_map/ppermute | solution.py:27
  (131 shorter events, 48.3 us)
Async XLA Ops:
  8.0 69.6 %all-gather.3.cloned.1.call-start = ((), (), s32[]{:S(2)}) async-start(), calls=%async_computation.2 | async-start | bytes 6488064 | tf_op jit(solution)/shard_map/all_gather | solution.py:634
  11.8 157.7 %reduce-scatter.7.cloned.1.call-start = ((), (), s32[]{:S(2)}) async-start(), calls=%async_computation.3 | async-start | bytes 17825792
  13.3 4.7 %copy-start.20 = (f32[16,128]{1,0:T(8,128)S(1)}, f32[16,128]{1,0:T(8,128)}, u32[]{:S(2)}) copy-start(f32[16,128]{1,0:T(8,128)} %param.32) | copy-start | bytes 24580
  34.7 6.9 %copy-start.17 = (f32[32,1]{1,0:T(8,128)S(1)}, f32[32,1]{1,0:T(8,128)}, u32[]{:S(2)}) copy-start(f32[32,1]{1,0:T(8,128)} %constant.54.clone.inverse) | copy-start | bytes 388
  34.7 6.9 %copy-start.23 = (f32[2,768]{1,0:T(2,128)S(1)}, f32[2,768]{1,0:T(2,128)}, u32[]{:S(2)}) copy-start(f32[2,768]{1,0:T(2,128)} %bias.1) | copy-start | bytes 18436
  34.7 243.3 %all-reduce.6.cloned.1.call-start = ((), (), s32[]{:S(2)}) async-start(), calls=%async_computation.5 | async-start | bytes 8388608 | tf_op jit(solution)/shard_map/psum | solution.py:718
  69.8 4.5 %collective-permute-start = (f32[256,2048]{1,0:T(8,128)}, f32[256,2048]{1,0:T(8,128)}, u32[]{:S(2)}, u32[]{:S(2)}) collective-permute-start(f32[256,2048]{1,0:T(8,128)} %get-tuple-element.276), channel_id=1, source_target_pairs={{0,1},{1,0},{2,3},{3,2},{4,5},{5,4},{6,7},{7,6},{8,9},{9,8},{10,11... | collective-permute-start | bytes 6291464 | tf_op jit(solution)/shard_map/ppermute | solution.py:27
  69.8 4.5 %copy-start.9 = (f32[256,2048]{1,0:T(8,128)S(1)}, f32[256,2048]{1,0:T(8,128)}, u32[]{:S(2)}) copy-start(f32[256,2048]{1,0:T(8,128)} %get-tuple-element.275) | copy-start | bytes 6291460
  80.8 4.6 %collective-permute-start.1 = (f32[1,264,2048]{2,1,0:T(8,128)}, f32[1,264,2048]{2,1,0:T(8,128)}, u32[]{:S(2)}, u32[]{:S(2)}) collective-permute-start(f32[1,264,2048]{2,1,0:T(8,128)} %constant_dynamic-slice_fusion.1), channel_id=1, source_target_pairs={{0,1},{1,0},{2,3},{3,2},{4,5},{5,4},{6,7},{7,6},{8,9},{9,8},{10,11... | collective-permute-start | bytes 6488072 | tf_op jit(solution)/shard_map/ppermute | solution.py:27
  80.9 49.2 %collective-permute-start.2 = (f32[256,2048]{1,0:T(8,128)}, f32[256,2048]{1,0:T(8,128)}, u32[]{:S(2)}, u32[]{:S(2)}) collective-permute-start(f32[256,2048]{1,0:T(8,128)} %dynamic-slice_convert_fusion), channel_id=1, source_target_pairs={{0,64},{64,0},{1,65},{65,1},{2,66},{66,2},{3,67},{67,3},{4,68},{68... | collective-permute-start | bytes 6291464 | tf_op jit(solution)/shard_map/ppermute | solution.py:27
  85.4 7.8 %copy-start.2 = (bf16[512,2048]{1,0:T(8,128)(2,1)}, bf16[512,2048]{1,0:T(8,128)(2,1)S(1)}, u32[]{:S(2)}) copy-start(bf16[512,2048]{1,0:T(8,128)(2,1)S(1)} %get-tuple-element.107.cot) | copy-start | bytes 6291460 | tf_op jit(solution)/shard_map/cond
  99.2 17.3 %slice-start = ((s8[6291456]{0:T(1024)(128)(4,1)}), s8[4194304]{0:T(1024)(128)(4,1)S(1)}, s32[]{:S(2)}) async-start(s8[6291456]{0:T(1024)(128)(4,1)} %bitcast.49), calls=%async_computation.6 | async-start | bytes 8388608 | tf_op jit(solution)/shard_map/cond
  106.0 10.5 %slice-start.1 = ((s8[6291456]{0:T(1024)(128)(4,1)}), s8[2097152]{0:T(1024)(128)(4,1)S(1)}, s32[]{:S(2)}) async-start(s8[6291456]{0:T(1024)(128)(4,1)} %bitcast.49), calls=%async_computation.7 | async-start | bytes 4194304 | tf_op jit(solution)/shard_map/cond
  106.0 10.5 %copy-start.6 = (bf16[512,1536]{1,0:T(8,128)(2,1)S(1)}, bf16[512,1536]{1,0:T(8,128)(2,1)}, u32[]{:S(2)}) copy-start(bf16[512,1536]{1,0:T(8,128)(2,1)} %get-tuple-element.111.packed) | copy-start | bytes 4718596 | tf_op jit(solution)/shard_map/cond
  130.1 9.3 %copy-start.8 = (f32[512,1024]{1,0:T(8,128)S(1)}, f32[512,1024]{1,0:T(8,128)}, u32[]{:S(2)}) copy-start(f32[512,1024]{1,0:T(8,128)} %get-tuple-element.290.slope) | copy-start | bytes 6291460
  130.1 7.2 %collective-permute-start.4 = (f32[256,2048]{1,0:T(8,128)}, f32[256,2048]{1,0:T(8,128)S(1)}, u32[]{:S(2)}, u32[]{:S(2)}) collective-permute-start(f32[256,2048]{1,0:T(8,128)} %get-tuple-element.294), channel_id=1, source_target_pairs={{0,1},{1,0},{2,3},{3,2},{4,5},{5,4},{6,7},{7,6},{8,9},{9,8},{10,11... | collective-permute-start | bytes 6291464 | tf_op jit(solution)/shard_map/ppermute | solution.py:27
  130.4 7.2 %collective-permute-start.3 = (f32[256,2048]{1,0:T(8,128)}, f32[256,2048]{1,0:T(8,128)S(1)}, u32[]{:S(2)}, u32[]{:S(2)}) collective-permute-start(f32[256,2048]{1,0:T(8,128)} %collective-permute-done.2.rows), channel_id=1, source_target_pairs={{0,1},{1,0},{2,3},{3,2},{4,5},{5,4},{6,7},{7,6},{8,9},{9,8},{10,11... | collective-permute-start | bytes 6291464 | tf_op jit(solution)/shard_map/ppermute | solution.py:27
  147.6 5.5 %copy-start.4 = (bf16[512,2048]{1,0:T(8,128)(2,1)S(1)}, bf16[512,2048]{1,0:T(8,128)(2,1)}, u32[]{:S(2)}) copy-start(bf16[512,2048]{1,0:T(8,128)(2,1)} %get-tuple-element.321.refs_3_) | copy-start | bytes 6291460
  147.6 139.0 %reduce-scatter.9.cloned.1.call-start = ((), (), s32[]{:S(2)}) async-start(), calls=%async_computation.4 | async-start | bytes 17825792
  147.9 5.2 %copy-start.5 = (bf16[512,1536]{1,0:T(8,128)(2,1)S(1)}, bf16[512,1536]{1,0:T(8,128)(2,1)}, u32[]{:S(2)}) copy-start(bf16[512,1536]{1,0:T(8,128)(2,1)} %get-tuple-element.320.refs_7_) | copy-start | bytes 4718596
  171.6 26.3 %collective-permute-start.7 = (f32[64,2048]{1,0:T(8,128)}, f32[64,2048]{1,0:T(8,128)S(1)}, u32[]{:S(2)}, u32[]{:S(2)}) collective-permute-start(f32[64,2048]{1,0:T(8,128)} %dynamic-slice_bitcast_fusion.1), channel_id=1, source_target_pairs={{0,64},{64,0},{1,65},{65,1},{2,66},{66,2},{3,67},{67,3},{4,68},{68... | collective-permute-start | bytes 1572872 | tf_op jit(solution)/shard_map/ppermute | solution.py:27
  179.1 4.6 %collective-permute-start.5 = (f32[32,512]{1,0:T(8,128)S(1)}, f32[32,512]{1,0:T(8,128)S(1)}, u32[]{:S(2)}, u32[]{:S(2)}) collective-permute-start(f32[32,512]{1,0:T(8,128)S(1)} %concatenate.27), channel_id=1, source_target_pairs={{0,16},{16,0},{32,48},{48,32},{1,17},{17,1},{33,49},{49,33},{2,18}... | collective-permute-start | bytes 196616 | tf_op jit(solution)/shard_map/ppermute | solution.py:31
  183.8 7.2 %collective-permute-start.6 = (f32[32,512]{1,0:T(8,128)S(1)}, f32[32,512]{1,0:T(8,128)S(1)}, u32[]{:S(2)}, u32[]{:S(2)}) collective-permute-start(f32[32,512]{1,0:T(8,128)S(1)} %add.70), channel_id=1, source_target_pairs={{0,32},{16,48},{32,0},{48,16},{1,33},{17,49},{33,1},{49,17},{2,34}... | collective-permute-start | bytes 196616 | tf_op jit(solution)/shard_map/ppermute | solution.py:31
  197.8 5.9 %collective-permute-start.8 = (f32[32,512]{1,0:T(8,128)S(1)}, f32[32,512]{1,0:T(8,128)S(1)}, u32[]{:S(2)}, u32[]{:S(2)}) collective-permute-start(f32[32,512]{1,0:T(8,128)S(1)} %add.71), channel_id=1, source_target_pairs={{0,4},{4,0},{8,12},{12,8},{1,5},{5,1},{9,13},{13,9},{2,6},{6,2},{1... | collective-permute-start | bytes 196616 | tf_op jit(solution)/shard_map/ppermute | solution.py:31
  203.7 7.3 %collective-permute-start.9 = (f32[32,512]{1,0:T(8,128)S(1)}, f32[32,512]{1,0:T(8,128)S(1)}, u32[]{:S(2)}, u32[]{:S(2)}) collective-permute-start(f32[32,512]{1,0:T(8,128)S(1)} %add.73), channel_id=1, source_target_pairs={{0,8},{4,12},{8,0},{12,4},{1,9},{5,13},{9,1},{13,5},{2,10},{6,14},... | collective-permute-start | bytes 196616 | tf_op jit(solution)/shard_map/ppermute | solution.py:31
  211.1 3.7 %collective-permute-start.10 = (f32[1,512]{1,0:T(1,128)S(1)}, f32[1,512]{1,0:T(1,128)S(1)}, u32[]{:S(2)}, u32[]{:S(2)}) collective-permute-start(f32[1,512]{1,0:T(1,128)S(1)} %constant_dynamic-slice_fusion), channel_id=1, source_target_pairs={{0,64},{64,0},{1,65},{65,1},{2,66},{66,2},{3,67},{67,3},{4,68},{68... | collective-permute-start | bytes 6152 | tf_op jit(solution)/shard_map/ppermute | solution.py:27
  214.8 1.2 collective-permute-start.11
  216.0 5.7 %collective-permute-start.12 = (f32[256]{0:T(256)S(1)}, f32[256]{0:T(256)S(1)}, u32[]{:S(2)}, u32[]{:S(2)}) collective-permute-start(f32[256]{0:T(256)S(1)} %add.81), channel_id=1, source_target_pairs={{0,2},{2,0},{1,3},{3,1},{4,6},{6,4},{5,7},{7,5},{8,10},{10,8},{9,1... | collective-permute-start | bytes 3080 | tf_op jit(solution)/shard_map/ppermute | solution.py:27
  278.0 16.2 %collective-permute-start.13 = (f32[256,2048]{1,0:T(8,128)}, f32[256,2048]{1,0:T(8,128)}, u32[]{:S(2)}, u32[]{:S(2)}) collective-permute-start(f32[256,2048]{1,0:T(8,128)} %get-tuple-element.330.branch), channel_id=1, source_target_pairs={{0,1},{1,0},{2,3},{3,2},{4,5},{5,4},{6,7},{7,6},{8,9},{9,8},{10,11... | collective-permute-start | bytes 6291464 | tf_op jit(solution)/shard_map/ppermute | solution.py:27
  278.0 16.2 %collective-permute-start.14 = (f32[256,2048]{1,0:T(8,128)}, f32[256,2048]{1,0:T(8,128)}, u32[]{:S(2)}, u32[]{:S(2)}) collective-permute-start(f32[256,2048]{1,0:T(8,128)} %get-tuple-element.331.combined), channel_id=1, source_target_pairs={{0,1},{1,0},{2,3},{3,2},{4,5},{5,4},{6,7},{7,6},{8,9},{9,8},{10,11... | collective-permute-start | bytes 6291464 | tf_op jit(solution)/shard_map/ppermute | solution.py:27
  288.6 13.5 %collective-permute-start.15 = (f32[64,2048]{1,0:T(8,128)}, f32[64,2048]{1,0:T(8,128)}, u32[]{:S(2)}, u32[]{:S(2)}) collective-permute-start(f32[64,2048]{1,0:T(8,128)} %dynamic-slice_bitcast_fusion), channel_id=1, source_target_pairs={{0,64},{64,0},{1,65},{65,1},{2,66},{66,2},{3,67},{67,3},{4,68},{68... | collective-permute-start | bytes 1572872 | tf_op jit(solution)/shard_map/ppermute | solution.py:27
  292.8 11.5 %copy-start.26 = (f32[64]{0:T(128)}, f32[64]{0:T(128)S(1)}, u32[]{:S(2)}) copy-start(f32[64]{0:T(128)S(1)} %get-tuple-element.451) | copy-start | bytes 772
  (13 other events, 19.4 us)
Sparse Core Ops, SparseCore 0:
  11.9 63.2 all-gather.2
  147.8 130.1 all-reduce.5
Sparse Core Ops, SparseCore 1:
  34.8 112.8 reduce-scatter.6
  169.6 117.0 reduce-scatter.8

commit v2 on v1

--- a/solution.py
+++ b/solution.py
@@ -207,61 +207,52 @@
     )(cot, weight, slope)
 
 
-def cot_far_kernel(n, m, side, rows, weight, slope, dense, *refs):
-    sums, (up_grad, grad_mixed, cot_turned), totals, low = (
-        refs[:m],
-        refs[m + n : m + n + 3],
-        refs[m + n + 3 : -1],
-        refs[-1],
-    )
+def cot_far_kernel(side, near, other, weight, slope, dense, held, up_grad, grad_mixed, cot_turned, low):
+    half = TOK // 2
 
     @pl.when(pl.program_id(0) == 0)
     def _():
-        low[...] = rows[...].astype(BF16)
-        put_turned(cot_turned, rows[...])
+        for k, rows in enumerate((near, other)):
+            low[k * half : k * half + half] = rows[...].astype(BF16)
+            put_turned(cot_turned.at[:, :, :, k * half : k * half + half], rows[...])
         grad_mixed[...] = contract_cols(low[...], dense[...]).astype(BF16)
 
     up_grad[...] = (contract_cols(low[...], weight[...]) * slope[...]).astype(BF16)
-    for k, total in enumerate(totals):
-        total[...] = sums[2 * k][...] + sums[2 * k + 1][...]
-
-
-def cot_far_half(k, side, rows, weight, slope, dense, held, sums=()):
-    half, width = TOK // 2, 256
+
+
+def cot_far(side, near, other, weight, slope, dense, held):
+    width = 256
     steps = slope.shape[1] // width
-    shapes = [
-        jax.ShapeDtypeStruct((TOK, slope.shape[1]), BF16),
-        jax.ShapeDtypeStruct((TOK, HD), BF16),
-        jax.ShapeDtypeStruct(TURNED, BF16),
-    ]
-    piece = pl.BlockSpec((half, D // steps), lambda j, s: (0, j))
-    first = 5 + len(sums)
-    return pl.pallas_call(
-        partial(cot_far_kernel, len(held), len(sums)),
+    column = pl.BlockSpec((TOK, width), lambda j, s: (0, j))
+    return pl.pallas_call(
+        cot_far_kernel,
         grid_spec=pltpu.PrefetchScalarGridSpec(
             num_scalar_prefetch=1,
             grid=(steps,),
             in_specs=[
-                whole((half, D)),
+                whole((TOK // 2, D)),
+                whole((TOK // 2, D)),
                 pl.BlockSpec((width, D), lambda j, s: (s[0] * steps + j, 0)),
-                pl.BlockSpec((half, width), lambda j, s: (k, j)),
+                column,
                 pl.BlockSpec((HD, D), lambda j, s: (s[0], 0)),
-            ]
-            + [piece] * len(sums)
-            + [pl.BlockSpec(memory_space=pl.ANY)] * len(held),
+                pl.BlockSpec(memory_space=pl.ANY),
+            ],
             out_specs=[
-                pl.BlockSpec((half, width), lambda j, s: (k, j)),
-                pl.BlockSpec((half, HD), lambda j, s: (k, 0)),
-                pl.BlockSpec((16, 2, 64, half), lambda j, s: (0, 0, 0, 2 + k)),
-            ]
-            + [piece] * (len(sums) // 2),
-            scratch_shapes=[pltpu.VMEM((half, D), BF16)],
-        ),
-        out_shape=shapes + [jax.ShapeDtypeStruct((half, D), F32)] * (len(sums) // 2),
-        input_output_aliases={first: 2} if len(held) == 1 else {first + i: i for i in range(3)},
-        compiler_params=pltpu.CompilerParams(vmem_limit_bytes=VMEM),
-        cost_estimate=COST,
-    )(side, rows, weight, slope, dense, *sums, *held)
+                column,
+                pl.BlockSpec((TOK, HD), lambda j, s: (0, 0)),
+                pl.BlockSpec((16, 2, 64, TOK), lambda j, s: (0, 0, 0, 1)),
+            ],
+            scratch_shapes=[pltpu.VMEM((TOK, D), BF16)],
+        ),
+        out_shape=[
+            jax.ShapeDtypeStruct((TOK, slope.shape[1]), BF16),
+            jax.ShapeDtypeStruct((TOK, HD), BF16),
+            jax.ShapeDtypeStruct(TURNED, BF16),
+        ],
+        input_output_aliases={6: 2},
+        compiler_params=pltpu.CompilerParams(vmem_limit_bytes=VMEM),
+        cost_estimate=COST,
+    )(side, near, other, weight, slope, dense, held)
 
 
 def slope_far_kernel(side, second, weight, bias, slope):
@@ -640,84 +631,48 @@
     down_sum = after(lax.psum_scatter(down_grad, ("x", "y"), scatter_dimension=0, tiled=True))
     _, cotangent, hidden_in = after((down_grad, cotangent, hidden_in))
 
+    cot_got = lax.ppermute(
+        of_core(cotangent, core).astype(F32), ("zl", "zh"), [(i, 3 - i) for i in range(4)]
+    )
+
     own_marks = marks.reshape(2, TOK)
-    first_in, first_turned, second_turned = norm_call(first_kernel, 256, (hidden_in,), 1, 2, params)
-    projected = project(own_place, 2, first_in, qkv_weight, qkv_bias, own_marks)
-    mixed_low, grad_packed = attend(
-        own_place, 2, projected, (cotangent, dense_weight), own_marks
-    )
+
+    def own_step(hidden_in, cotangent, slope):
+        first_in, first_turned, second_turned = norm_call(
+            first_kernel, 256, (hidden_in,), 1, 2, params
+        )
+        projected = project(own_place, 2, first_in, qkv_weight, qkv_bias, own_marks)
+        mixed_low, grad_packed = attend(
+            own_place, 2, projected, (cotangent, dense_weight), own_marks
+        )
+        grad_up = feed_back(cotangent, fc2_weight, slope)
+        return first_turned, second_turned, mixed_low, grad_packed, grad_up
+
+    first_turned, second_turned, mixed_low, grad_packed, grad_up = lax.cond(
+        core > 1, own_step, own_step, hidden_in, cotangent, slope
+    )
+    hidden_pair, cot_got, mixed_low = after((hidden_pair, cot_got, mixed_low))
+    hidden_got = lax.dynamic_slice_in_dim(hidden_pair, 1 - side, 1, 0)
+    hidden_too, cot_too = send(hidden_got, "c"), send(cot_got, "c")
     branch, branch_other = branch_halves(at_core, mixed_low, act_low, dense_weight, fc2_weight)
-    branch = branch + send(branch_other, "c")
-    branch, cot_sent = after((branch, of_core(cotangent, core).astype(F32)))
-
-    hidden_pair, branch, cot_sent = after((hidden_pair, branch, cot_sent))
-    cot_got = send(cot_sent, "zl")
-    hidden_got = lax.dynamic_slice_in_dim(hidden_pair, 1 - side, 1, 0)
-    hidden_too = send(hidden_got, "c")
-
-    def beside(hidden_got, hidden_too, first_turned, second_turned, slope, grad_packed):
-        first_in, second_in, first_turned, second_turned = first_far(
-            hidden_got, hidden_too, params, (first_turned, second_turned)
-        )
-        slope_side = slope_far(at_side, second_in, fc1_weight, fc1_bias)
-        marks_got = hidden_got[0, half_rows, : 2 * TOK].reshape(2, 2, half_rows)
-        marks_far = jnp.where(core == 0, marks_got, marks_got[:, ::-1]).reshape(2, TOK)
-        projected_far = project(far_place, 1, first_in, qkv_weight, qkv_bias, marks_far)
-        grad_up = feed_back(cotangent, fc2_weight, slope)
-        backs = back_halves(
-            at_core,
-            grad_packed,
-            grad_up,
-            qkv_weight,
-            fc1_weight,
-            hidden_in,
-            stats,
-            ln1_gain,
-            ln2_gain,
-        )
-        return first_turned, second_turned, slope_side, marks_far, grad_up, *backs, *projected_far
-
-    (
-        first_turned,
-        second_turned,
-        slope_side,
-        marks_far,
-        grad_up,
-        combined,
-        combined_other,
-        norms,
-        *projected_far,
-    ) = lax.cond(
-        core > 1,
-        beside,
-        beside,
-        hidden_got,
-        hidden_too,
-        first_turned,
-        second_turned,
-        slope,
-        grad_packed,
-    )
-
-    slope_side, cot_got, combined_other = after((slope_side, cot_got, combined_other))
-    cot_too = send(cot_got, "c")
-    combined_too = send(combined_other, "c")
-    held = cot_far_half(0, at_side, cot_got, fc2_weight, slope_side, dense_weight, (cot_turned,))
-    *held, cot_too, combined_too = after((*held, cot_too, combined_too))
-    grad_up_far, grad_mixed_far, cot_turned, combined = cot_far_half(
-        1,
-        at_side,
-        cot_too,
-        fc2_weight,
-        slope_side,
-        dense_weight,
-        held,
-        (combined, combined_too),
-    )
-    branch, combined = after((branch, combined))
-    branch = lax.psum(branch, "zh")
-    combined = lax.psum(combined, "zh")
-    mixed_far, grad_packed_far = attend(far_place, 1, projected_far, (grad_mixed_far,), marks_far)
+    hidden_too, branch_other = after((hidden_too, branch_other))
+    branch_too = send(branch_other, "c")
+
+    first_far_in, second_far_in, first_turned, second_turned = first_far(
+        hidden_got, hidden_too, params, (first_turned, second_turned)
+    )
+    second_far_in, branch_too = after((second_far_in, branch_too))
+    branch = lax.psum(branch + branch_too, "zh")
+    slope_side = slope_far(at_side, second_far_in, fc1_weight, fc1_bias)
+    marks_got = hidden_got[0, half_rows, : 2 * TOK].reshape(2, 2, half_rows)
+    marks_far = jnp.where(core == 0, marks_got, marks_got[:, ::-1]).reshape(2, TOK)
+    projected_far = project(far_place, 1, first_far_in, qkv_weight, qkv_bias, marks_far)
+    grad_up_far, grad_mixed_far, cot_turned = cot_far(
+        at_side, cot_got, cot_too, fc2_weight, slope_side, dense_weight, cot_turned
+    )
+    mixed_far, grad_packed_far = attend(
+        far_place, 1, projected_far, (grad_mixed_far,), marks_far
+    )
     joint_grad = joint(
         at_side,
         (second_turned, cot_turned, first_turned),
@@ -725,9 +680,15 @@
     )
     joint_grad, down_sum = after((joint_grad, down_sum))
     joint_sum = after(lax.psum_scatter(joint_grad, ("x", "y"), scatter_dimension=0, tiled=True))
-    _, norms, grad_packed, grad_up, cotangent, down_sum = after(
-        (joint_grad, norms, grad_packed, grad_up, cotangent, down_sum)
-    )
+    _, grad_packed, grad_up, cotangent, down_sum = after(
+        (joint_grad, grad_packed, grad_up, cotangent, down_sum)
+    )
+
+    combined, combined_other, norms = back_halves(
+        at_core, grad_packed, grad_up, qkv_weight, fc1_weight, hidden_in, stats, ln1_gain, ln2_gain
+    )
+    combined = combined + send(combined_other, "c")
+    combined_too = send(combined, "zh")
 
     norms = norms[:4].reshape(4, 32, 64).transpose(1, 0, 2).reshape(32, 256)
     grad_out = cotangent.astype(F32)
@@ -760,14 +721,16 @@
     norms = small[:256]
     norms = norms + send(norms, "c")
     norms = norms + send(norms, "zh")
-    norms, branch, combined = after((norms, branch, combined))
+    norms, branch, combined_too = after((norms, branch, combined_too))
+    combined = combined + combined_too
     norms = norms.reshape(4, 64)
     bias_total = small[256:320]
     biases = (dense_bias, fc2_bias)
     own = (hidden_in, cotangent, stats, biases)
     branch_too, combined_too = send(branch, "c"), send(combined, "c")
-    *finals, joint_sum = after((*final_half(at_core, branch, combined, *own, ()), joint_sum))
-    output, input_grad = final_half(1 - at_core, branch_too, combined_too, *own, finals)
+    finals = final_half(at_core, branch, combined, *own, ())
+    finals = final_half(1 - at_core, branch_too, combined_too, *own, finals)
+    output, input_grad, joint_sum = after((*finals, joint_sum))
 
     down_sum = of_side(down_sum, side) + down_far
     joint_far = send(of_side(joint_sum, 1 - side), "zl")

time: 313 us -> 303 us (0.968)
  other arithmetic: 14.7 us -> 21.4 us
  local copies, waits for them, and re-layouts: 17.8 us -> 12.2 us
  starting transfers between devices: 24.5 us -> 19 us
  Pallas kernels: 145 us -> 141 us
    psum x1, waiting for transfers between devices: 56.3 us -> 0.01 us  [body(): branch = lax.psum(branch + branch_too, 'zh')]
    ppermute x12, waiting for transfers between devices: 20.3 us -> 62.8 us  [send(): return lax.ppermute(value, axis, [(i, (i + step) % n) for i in range(n)])]
    ppermute x0 -> x1, waiting for transfers between devices: none -> 14.4 us  [body(): lax.ppermute(of_core(cotangent, core).astype(F32), ('zl', 'zh'), [(i, 3 -...]
    ppermute x12, starting transfers between devices: 13.3 us -> 6.06 us  [send(): return lax.ppermute(value, axis, [(i, (i + step) % n) for i in range(n)])]
    add x1 -> x3, other arithmetic: 3.24 us -> 8.99 us  [the longest x1 3.99 us: body(): combined = combined + combined_too]
    pallas_call x2 -> x1, Pallas kernels: 14.8 us -> 9.13 us  [cot_far(): pl.pallas_call(cot_far_kernel, grid_spec=pltpu.PrefetchScalarGridSpec(num...]
    ppermute x0 -> x1, starting transfers between devices: none -> 4.09 us  [body(): lax.ppermute(of_core(cotangent, core).astype(F32), ('zl', 'zh'), [(i, 3 -...]
    optimization_barrier x1, waiting for transfers between devices: 3.87 us -> 0.01 us  [body(): output, input_grad, joint_sum = after((*finals, joint_sum))]
  transfers between devices with their start and end apart: 20 -> 21, of which waited for: 14 -> 12; matrix products, arithmetic and copies ran while one was open for 8% -> 9% of each run, Pallas kernels for 46% -> 46%
where the time goes in v2:
time: 303 us; the launch traced here: 302 us
  Pallas kernels  141 us (47%)
  waiting for transfers between devices  92.5 us (31%)
  other arithmetic  21.4 us (7%)
  starting transfers between devices  19 us (6%)
  between operations  15.8 us (5%)
  local copies, waits for them, and re-layouts  12.2 us (4%)
    ppermute x12, waiting for transfers between devices, send(): return lax.ppermute(value, axis, [(i, (i + step) % n) for i in range(n)])  62.8 us
    pallas_call x2, Pallas kernels, halves_call(): pl.pallas_call(kernel, grid_spec=pltpu.PrefetchScalarGridSpec(num_scalar_...  26.5 us
    pallas_call x1, Pallas kernels, joint(): pl.pallas_call(joint_kernel, grid_spec=pltpu.PrefetchScalarGridSpec(num_s...  16.7 us
    pallas_call x1, Pallas kernels, feed(): pl.pallas_call(feed_kernel, grid=(units // width,), in_specs=[whole((TOK,...  16.6 us
    ppermute x4, waiting for transfers between devices, swap(): return lax.ppermute(value, axis, [(i, i ^ bit) for i in range(SIZES[axis])])  15.2 us
    pallas_call x2, Pallas kernels, project(): pl.pallas_call(project_kernel, grid_spec=pltpu.PrefetchScalarGridSpec(num...  14.4 us
    ppermute x1, waiting for transfers between devices, body(): lax.ppermute(of_core(cotangent, core).astype(F32), ('zl', 'zh'), [(i, 3 -...  14.4 us
    pallas_call x2, Pallas kernels, attend(): pl.pallas_call(attend_kernel, grid_spec=pltpu.PrefetchScalarGridSpec(num_...  13.6 us
  transfers between devices with their start and end apart: 21, of which 12 were waited for; matrix products, arithmetic and copies ran while one was open for 9% of the time, Pallas kernels for 46%

profile of v2, /device:TPU:0, one launch (start us, length us, event | category | flops | bytes accessed | tf_op | source)
XLA Modules:
  0.0 301.8 jit_solution(2376656304617942590)
XLA Ops:
  13.4 4.4 %shard_map.281 = (bf16[512,2048]{1,0:T(8,128)(2,1)}, bf16[16,2,64,1024]{3,2,1,0:T(8,128)(2,1)}, f32[512,128]{1,0:T(8,128)}) custom-call(bf16[512,2048]{1,0:T(8,128)(2,1)} %hidden.4, bf16[512,2048]{1,0:T(8,128)(2,1)S(1)} %copy-done, f32[1,2048]{1,0:T(1,128)S(1)} %bitcast.48, f32[1,2048]{1,0:T(1,128)S(1)} %bitcast.57), custom_call_target="tpu_custom_call" | custom-call | flops 1000000 | bytes 1000000 | tf_op jit(solution)/shard_map/pallas_call | solution.py:111
  17.9 16.6 %shard_map.282 = (bf16[512,2048]{1,0:T(8,128)(2,1)}, f32[512,2048]{1,0:T(8,128)}, f32[16,128,2048]{2,1,0:T(8,128)}) custom-call(bf16[512,2048]{1,0:T(8,128)(2,1)} %get-tuple-element.177.second, bf16[16,2,64,1024]{3,2,1,0:T(8,128)(2,1)} %get-tuple-element.178.cot_turned.held, bf16[2048,2048]{1,0:T(8,128)(2,1)} %up.1, f32[4,4,128]{2,1,0:T(4,128)} %bitcast.69), custom_call_target="tpu_custom_call" | custom-call | flops 1000000 | bytes 1000000 | tf_op jit(solution)/shard_map/pallas_call | solution.py:172
  36.3 4.1 %collective-permute-start = (f32[256,2048]{1,0:T(8,128)}, f32[256,2048]{1,0:T(8,128)}, u32[]{:S(2)}, u32[]{:S(2)}) collective-permute-start(f32[256,2048]{1,0:T(8,128)} %dynamic-slice_convert_fusion), channel_id=1, source_target_pairs={{0,66},{2,64},{64,2},{66,0},{1,67},{3,65},{65,3},{67,1},{4,70},{6,... | collective-permute-start | bytes 6291464 | tf_op jit(solution)/shard_map/ppermute | solution.py:634
  40.5 31.5 %conditional.1 = (bf16[16,2,64,1024]{3,2,1,0:T(8,128)(2,1)}, bf16[16,2,64,1024]{3,2,1,0:T(8,128)(2,1)}, bf16[512,512]{1,0:T(8,128)(2,1)S(1)}, bf16[512,1536]{1,0:T(8,128)(2,1)}, bf16[512,2048]{1,0:T(8,128)(2,1)}) conditional(s32[]{:T(128)} %convert_element_type.39, (f32[2048]{0:T(1024)S(1)}, f32[2048]{0:T(1024)S(1)}, f32[2048]{0:T(1024)S(1)}, ...), branch_computations={%region_0.1_spmd, %region_1.2_spmd} | conditional | flops 4000000 | bytes 20777324 | solution.py:651
  40.5 9.7 %branch_0_fun.7 = bf16[512,2048]{1,0:T(8,128)(2,1)} custom-call(bf16[512,2048]{1,0:T(8,128)(2,1)S(1)} %get-tuple-element.70.refs_0_.cot, bf16[2048,2048]{1,0:T(8,128)(2,1)} %get-tuple-element.74.weight, f32[512,2048]{1,0:T(8,128)} %get-tuple-element.75.slope), custom_call_target="tpu_custom_call" | custom-call | flops 1000000 | bytes 1000000 | tf_op jit(solution)/shard_map/cond/branch_0_fun/pallas_call | solution.py:199
  50.2 4.0 %branch_0_fun.4 = (bf16[512,2048]{1,0:T(8,128)(2,1)}, bf16[16,2,64,1024]{3,2,1,0:T(8,128)(2,1)}, bf16[16,2,64,1024]{3,2,1,0:T(8,128)(2,1)}) custom-call(bf16[512,2048]{1,0:T(8,128)(2,1)S(1)} %copy-done.2, f32[1,2048]{1,0:T(1,128)S(1)} %bitcast.55, f32[1,2048]{1,0:T(1,128)S(1)} %bitcast.65, f32[1,2048]{1,0:T(1,128)S(1)} %bitcast.51, f32[1,2048]{1,0:T(1,128)S(1)} %bitcast.59), custom_call_target="tpu_custom_call" | custom-call | flops 1000000 | bytes 1000000 | tf_op jit(solution)/shard_map/cond/branch_0_fun/pallas_call | solution.py:111
  54.8 8.5 %branch_0_fun.5 = (bf16[512,512]{1,0:T(8,128)(2,1)}, bf16[512,512]{1,0:T(8,128)(2,1)}, bf16[512,512]{1,0:T(8,128)(2,1)}, f32[512,128]{1,0:T(8,128)}, f32[512,128]{1,0:T(8,128)}, /*index=5*/f32[512,128]{1,0:T(8,128)}) custom-call(s32[2]{0:T(128)} %broadcast_1_place.0.place, bf16[512,2048]{1,0:T(8,128)(2,1)} %get-tuple-element.59.first, ...), custom_call_target="tpu_custom_call" | custom-call | flops 1000000 | bytes 1000000 | tf_op jit(solution)/shard_map/cond/branch_0_fun/pallas_call | solution.py:336
  63.3 8.7 %branch_0_fun.6 = (bf16[512,512]{1,0:T(8,128)(2,1)S(1)}, bf16[512,1536]{1,0:T(8,128)(2,1)}) custom-call(s32[2]{0:T(128)} %broadcast_1_place.0.place, bf16[512,512]{1,0:T(8,128)(2,1)} %get-tuple-element.64.queries, bf16[512,512]{1,0:T(8,128)(2,1)} %get-tuple-element.65.keys, bf16[512,512]{1,0:T(8,128)(2,1)} %get-tuple-element.66.values, ...), custom_call_target="tpu_custom_call" | custom-call | flops 1000000 | bytes 1000000 | tf_op jit(solution)/shard_map/cond/branch_0_fun/pallas_call | solution.py:390
  72.0 14.4 %collective-permute-done.near = f32[256,2048]{1,0:T(8,128)} collective-permute-done((f32[256,2048]{1,0:T(8,128)}, f32[256,2048]{1,0:T(8,128)}, u32[]{:S(2)}, u32[]{:S(2)}) %collective-permute-start) | collective-permute-done | bytes 2097184 | tf_op jit(solution)/shard_map/ppermute | solution.py:634
  88.8 10.7 %shard_map.283 = (f32[256,2048]{1,0:T(8,128)}, f32[256,2048]{1,0:T(8,128)}) custom-call(s32[1]{0:T(128)} %bitcast.8.core.half, bf16[512,512]{1,0:T(8,128)(2,1)S(1)} %get-tuple-element.185.mixed.refs_5_, bf16[512,2048]{1,0:T(8,128)(2,1)} %get-tuple-element.186.act, bf16[512,2048]{1,0:T(8,128)(2,1)S(1)} %copy-done.4, bf16[2048,2048]{1,0:T(8,128)(2,1)} %weight.6), custom_call_target="tpu_custom_call" | custom-call | flops 1000000 | bytes 1000000 | tf_op jit(solution)/shard_map/pallas_call | solution.py:438
  100.1 7.4 %shard_map.284 = (bf16[512,2048]{1,0:T(8,128)(2,1)}, bf16[512,2048]{1,0:T(8,128)(2,1)}, bf16[16,2,64,1024]{3,2,1,0:T(8,128)(2,1)}, bf16[16,2,64,1024]{3,2,1,0:T(8,128)(2,1)}) custom-call(f32[1,264,2048]{2,1,0:T(8,128)} %copy-done.8, f32[1,264,2048]{2,1,0:T(8,128)} %collective-permute-done.1.other, ...), custom_call_target="tpu_custom_call", output_to_operand_aliasing={{2}: (6, {}), {3}: (7, {})} | custom-call | flops 1000000 | bytes 1000000 | tf_op jit(solution)/shard_map/pallas_call | solution.py:129
  111.3 5.9 %shard_map.287 = (bf16[512,256]{1,0:T(8,128)(2,1)}, bf16[512,256]{1,0:T(8,128)(2,1)}, bf16[512,256]{1,0:T(8,128)(2,1)}, f32[512,128]{1,0:T(8,128)}, f32[512,128]{1,0:T(8,128)}, /*index=5*/f32[512,128]{1,0:T(8,128)}) custom-call(s32[2]{0:T(128)} %pad_add_fusion.place, bf16[512,2048]{1,0:T(8,128)(2,1)} %get-tuple-element.200.first, bf16[2048,1536]{1,0:T(8,128)(2,1)} %qkv.1, ...), custom_call_target="tpu_custom_call" | custom-call | flops 1000000 | bytes 1000000 | tf_op jit(solution)/shard_map/pallas_call | solution.py:336
  117.2 7.1 %shard_map.285.slope = f32[512,1024]{1,0:T(8,128)} custom-call(s32[1]{0:T(128)} %bitcast.9.side, bf16[512,2048]{1,0:T(8,128)(2,1)} %get-tuple-element.195.second, bf16[2048,2048]{1,0:T(8,128)(2,1)} %up.1, f32[4,4,128]{2,1,0:T(4,128)} %bitcast.70), custom_call_target="tpu_custom_call" | custom-call | flops 1000000 | bytes 1000000 | tf_op jit(solution)/shard_map/pallas_call | solution.py:266
  124.3 9.1 %shard_map.286 = (bf16[512,1024]{1,0:T(8,128)(2,1)}, bf16[512,256]{1,0:T(8,128)(2,1)}, bf16[16,2,64,1024]{3,2,1,0:T(8,128)(2,1)}) custom-call(s32[1]{0:T(128)} %bitcast.9.side, f32[256,2048]{1,0:T(8,128)} %collective-permute-done.near, f32[256,2048]{1,0:T(8,128)} %collective-permute-done.2.other, ...), custom_call_target="tpu_custom_call", output_to_operand_aliasing={{2}: (6, {})} | custom-call | flops 1000000 | bytes 1000000 | tf_op jit(solution)/shard_map/pallas_call | solution.py:227
  133.4 4.9 %shard_map.288 = (bf16[512,256]{1,0:T(8,128)(2,1)}, bf16[512,768]{1,0:T(8,128)(2,1)}) custom-call(s32[2]{0:T(128)} %pad_add_fusion.place, bf16[512,256]{1,0:T(8,128)(2,1)} %get-tuple-element.201.queries, bf16[512,256]{1,0:T(8,128)(2,1)} %get-tuple-element.202.keys, bf16[512,256]{1,0:T(8,128)(2,1)} %get-tuple-element.203.values, ...), custom_call_target="tpu_custom_call" | custom-call | flops 1000000 | bytes 1000000 | tf_op jit(solution)/shard_map/pallas_call | solution.py:390
  138.3 16.7 %shard_map.289 = f32[16,128,2048]{2,1,0:T(8,128)} custom-call(s32[1]{0:T(128)} %bitcast.9.side, bf16[16,2,64,1024]{3,2,1,0:T(8,128)(2,1)} %get-tuple-element.191.refs_0_, bf16[16,2,64,1024]{3,2,1,0:T(8,128)(2,1)} %get-tuple-element.196.refs_1_, bf16[16,2,64,1024]{3,2,1,0:T(8,128)(2,1)} %get-tuple-element.197.refs_2_, ...), custom_call_target="tpu_custom_call" | custom-call | flops 1000000 | bytes 1000000 | tf_op jit(solution)/shard_map/pallas_call | solution.py:541
  155.1 15.8 %shard_map.290 = (f32[256,2048]{1,0:T(8,128)}, f32[256,2048]{1,0:T(8,128)}, f32[8,2048]{1,0:T(8,128)}) custom-call(s32[1]{0:T(128)} %bitcast.8.core.half, bf16[512,1536]{1,0:T(8,128)(2,1)} %get-tuple-element.213.refs_7_.packed, bf16[512,2048]{1,0:T(8,128)(2,1)} %get-tuple-element.214.refs_3_.up_grad, bf16[2048,1536]{1,0:T(8,128)(2,1)} %qkv.1, ...), custom_call_target="tpu_custom_call" | custom-call | flops 1000000 | bytes 1000000 | tf_op jit(solution)/shard_map/pallas_call | solution.py:438
  171.1 4.1 %collective-permute-done.12 = f32[256,2048]{1,0:T(8,128)S(1)} collective-permute-done((f32[256,2048]{1,0:T(8,128)}, f32[256,2048]{1,0:T(8,128)S(1)}, u32[]{:S(2)}, u32[]{:S(2)}) %collective-permute-start.12) | collective-permute-done | bytes 2097184 | tf_op jit(solution)/shard_map/ppermute | solution.py:27
  175.2 3.3 %add.87 = f32[256,2048]{1,0:T(8,128)} add(f32[256,2048]{1,0:T(8,128)} %get-tuple-element.224, f32[256,2048]{1,0:T(8,128)S(1)} %collective-permute-done.12) | non-fusion elementwise | flops 524288 | bytes 6291456 | tf_op jit(solution)/shard_map/add | solution.py:690
  180.0 3.2 %collective-permute-start.6 = (f32[64,2048]{1,0:T(8,128)}, f32[64,2048]{1,0:T(8,128)}, u32[]{:S(2)}, u32[]{:S(2)}) collective-permute-start(f32[64,2048]{1,0:T(8,128)} %dynamic-slice_bitcast_fusion.1), channel_id=1, source_target_pairs={{0,64},{64,0},{1,65},{65,1},{2,66},{66,2},{3,67},{67,3},{4,68},{68... | collective-permute-start | bytes 1572872 | tf_op jit(solution)/shard_map/ppermute | solution.py:27
  189.9 4.8 %collective-permute-done.4 = f32[32,512]{1,0:T(8,128)S(1)} collective-permute-done((f32[32,512]{1,0:T(8,128)S(1)}, f32[32,512]{1,0:T(8,128)S(1)}, u32[]{:S(2)}, u32[]{:S(2)}) %collective-permute-start.4) | collective-permute-done | bytes 65568 | tf_op jit(solution)/shard_map/ppermute | solution.py:31
  197.5 4.7 %collective-permute-done.5 = f32[32,512]{1,0:T(8,128)S(1)} collective-permute-done((f32[32,512]{1,0:T(8,128)S(1)}, f32[32,512]{1,0:T(8,128)S(1)}, u32[]{:S(2)}, u32[]{:S(2)}) %collective-permute-start.5) | collective-permute-done | bytes 65568 | tf_op jit(solution)/shard_map/ppermute | solution.py:31
  202.1 37.4 %collective-permute-done.6 = f32[64,2048]{1,0:T(8,128)} collective-permute-done((f32[64,2048]{1,0:T(8,128)}, f32[64,2048]{1,0:T(8,128)}, u32[]{:S(2)}, u32[]{:S(2)}) %collective-permute-start.6) | collective-permute-done | bytes 524320 | tf_op jit(solution)/shard_map/ppermute | solution.py:27
  241.0 2.8 collective-permute-done.7
  243.8 3.3 %collective-permute-start.8 = (f32[32,512]{1,0:T(8,128)S(1)}, f32[32,512]{1,0:T(8,128)S(1)}, u32[]{:S(2)}, u32[]{:S(2)}) collective-permute-start(f32[32,512]{1,0:T(8,128)S(1)} %add.76), channel_id=1, source_target_pairs={{0,8},{4,12},{8,0},{12,4},{1,9},{5,13},{9,1},{13,5},{2,10},{6,14},... | collective-permute-start | bytes 196616 | tf_op jit(solution)/shard_map/ppermute | solution.py:31
  247.1 2.9 collective-permute-done.8
  250.2 3.6 %collective-permute-done.9 = f32[1,512]{1,0:T(1,128)S(1)} collective-permute-done((f32[1,512]{1,0:T(1,128)S(1)}, f32[1,512]{1,0:T(1,128)S(1)}, u32[]{:S(2)}, u32[]{:S(2)}) %collective-permute-start.9) | collective-permute-done | bytes 2080 | tf_op jit(solution)/shard_map/ppermute | solution.py:27
  255.5 4.6 %collective-permute-done.11 = f32[256]{0:T(256)S(1)} collective-permute-done((f32[256]{0:T(256)S(1)}, f32[256]{0:T(256)S(1)}, u32[]{:S(2)}, u32[]{:S(2)}) %collective-permute-start.11) | collective-permute-done | bytes 1056 | tf_op jit(solution)/shard_map/ppermute | solution.py:27
  260.1 4.0 %add.88.combined = f32[256,2048]{1,0:T(8,128)} add(f32[256,2048]{1,0:T(8,128)} %add.87, f32[256,2048]{1,0:T(8,128)} %collective-permute-done.13) | non-fusion elementwise | flops 524288 | bytes 6291456 | tf_op jit(solution)/shard_map/add | solution.py:725
  264.6 4.8 %shard_map.291 = (f32[512,2048]{1,0:T(8,128)}, f32[512,2048]{1,0:T(8,128)}) custom-call(s32[1]{0:T(128)} %bitcast.8.core.half, f32[256,2048]{1,0:T(8,128)} %all-reduce.5.cloned.1.call-done.branch, f32[256,2048]{1,0:T(8,128)} %add.88.combined, bf16[512,2048]{1,0:T(8,128)(2,1)} %hidden.4, bf16[512,2048]{1,0:T(8,128)(2,1)S(1)} %copy-done, ...), custom_call_target="tpu_custom_call" | custom-call | flops 1000000 | bytes 1000000 | tf_op jit(solution)/shard_map/pallas_call | solution.py:488
  271.6 4.1 %shard_map.292 = (f32[512,2048]{1,0:T(8,128)}, f32[512,2048]{1,0:T(8,128)}) custom-call(s32[1]{0:T(128)S(6)} %sub.4.half, f32[256,2048]{1,0:T(8,128)} %collective-permute-done.14.branch, f32[256,2048]{1,0:T(8,128)} %collective-permute-done.15.combined, bf16[512,2048]{1,0:T(8,128)(2,1)S(1)} %copy-done.1, ...), custom_call_target="tpu_custom_call", output_to_operand_aliasing={{0}: (8, {}), {1}: (9, {})} | custom-call | flops 1000000 | bytes 1000000 | tf_op jit(solution)/shard_map/pallas_call | solution.py:488
  280.9 9.9 %collective-permute-done.16.far = f32[64,2048]{1,0:T(8,128)S(1)} collective-permute-done((f32[64,2048]{1,0:T(8,128)S(1)}, f32[64,2048]{1,0:T(8,128)S(1)}, u32[]{:S(2)}, u32[]{:S(2)}) %collective-permute-start.16) | collective-permute-done | bytes 524320 | tf_op jit(solution)/shard_map/ppermute | solution.py:27
  (123 shorter events, 40.3 us)
Async XLA Ops:
  8.0 78.4 %all-gather.3.cloned.1.call-start = ((), (), s32[]{:S(2)}) async-start(), calls=%async_computation.3 | async-start | bytes 6488064 | tf_op jit(solution)/shard_map/all_gather | solution.py:625
  11.9 143.2 %reduce-scatter.7.cloned.1.call-start = ((), (), s32[]{:S(2)}) async-start(), calls=%async_computation.4 | async-start | bytes 17825792
  34.6 5.9 %copy-start.19 = (s32[512]{0:T(512)S(1)}, s32[512]{0:T(512)}, u32[]{:S(2)}) copy-start(s32[512]{0:T(512)} %param.22) | copy-start | bytes 6148
  34.6 5.9 %copy-start.13 = (f32[32,1]{1,0:T(8,128)S(1)}, f32[32,1]{1,0:T(8,128)}, u32[]{:S(2)}) copy-start(f32[32,1]{1,0:T(8,128)} %constant.53.clone.inverse) | copy-start | bytes 388
  34.6 5.9 %copy-start.14 = (f32[2048]{0:T(1024)S(1)}, f32[2048]{0:T(1024)}, u32[]{:S(2)}) copy-start(f32[2048]{0:T(1024)} %param.23) | copy-start | bytes 24580
  34.6 5.9 %copy-start.16 = (f32[2048]{0:T(1024)S(1)}, f32[2048]{0:T(1024)}, u32[]{:S(2)}) copy-start(f32[2048]{0:T(1024)} %param.24) | copy-start | bytes 24580
  34.6 225.4 %all-reduce.5.cloned.1.call-start = ((), (), s32[]{:S(2)}) async-start(), calls=%async_computation.2 | async-start | bytes 4194304 | tf_op jit(solution)/shard_map/psum | solution.py:665
  36.3 50.0 %collective-permute-start = (f32[256,2048]{1,0:T(8,128)}, f32[256,2048]{1,0:T(8,128)}, u32[]{:S(2)}, u32[]{:S(2)}) collective-permute-start(f32[256,2048]{1,0:T(8,128)} %dynamic-slice_convert_fusion), channel_id=1, source_target_pairs={{0,66},{2,64},{64,2},{66,0},{1,67},{3,65},{65,3},{67,1},{4,70},{6,... | collective-permute-start | bytes 6291464 | tf_op jit(solution)/shard_map/ppermute | solution.py:634
  40.5 9.7 %copy-start.2 = (bf16[512,2048]{1,0:T(8,128)(2,1)S(1)}, bf16[512,2048]{1,0:T(8,128)(2,1)}, u32[]{:S(2)}) copy-start(bf16[512,2048]{1,0:T(8,128)(2,1)} %get-tuple-element.52.hidden) | copy-start | bytes 6291460 | tf_op jit(solution)/shard_map/cond
  54.8 8.5 %copy-start.6 = (bf16[512,2048]{1,0:T(8,128)(2,1)S(1)}, bf16[512,2048]{1,0:T(8,128)(2,1)}, u32[]{:S(2)}) copy-start(bf16[512,2048]{1,0:T(8,128)(2,1)} %get-tuple-element.71.refs_1_) | copy-start | bytes 6291460 | tf_op jit(solution)/shard_map/cond
  88.5 11.0 %copy-start.8 = (f32[1,264,2048]{2,1,0:T(8,128)}, f32[1,264,2048]{2,1,0:T(8,128)S(1)}, u32[]{:S(2)}) copy-start(f32[1,264,2048]{2,1,0:T(8,128)S(1)} %constant_dynamic-slice_fusion.2.near) | copy-start | bytes 6488068
  88.5 11.0 %collective-permute-start.1 = (f32[1,264,2048]{2,1,0:T(8,128)S(1)}, f32[1,264,2048]{2,1,0:T(8,128)}, u32[]{:S(2)}, u32[]{:S(2)}) collective-permute-start(f32[1,264,2048]{2,1,0:T(8,128)S(1)} %constant_dynamic-slice_fusion.2.near), channel_id=1, source_target_pairs={{0,1},{1,0},{2,3},{3,2},{4,5},{5,4},{6,7},{7,6},{8,9},{9,8},{10,11... | collective-permute-start | bytes 6488072 | tf_op jit(solution)/shard_map/ppermute | solution.py:27
  99.5 8.0 %collective-permute-start.3 = (f32[256,2048]{1,0:T(8,128)}, f32[256,2048]{1,0:T(8,128)S(1)}, u32[]{:S(2)}, u32[]{:S(2)}) collective-permute-start(f32[256,2048]{1,0:T(8,128)} %get-tuple-element.194), channel_id=1, source_target_pairs={{0,1},{1,0},{2,3},{3,2},{4,5},{5,4},{6,7},{7,6},{8,9},{9,8},{10,11... | collective-permute-start | bytes 6291464 | tf_op jit(solution)/shard_map/ppermute | solution.py:27
  99.6 24.7 %collective-permute-start.2 = (f32[256,2048]{1,0:T(8,128)}, f32[256,2048]{1,0:T(8,128)}, u32[]{:S(2)}, u32[]{:S(2)}) collective-permute-start(f32[256,2048]{1,0:T(8,128)} %collective-permute-done.near), channel_id=1, source_target_pairs={{0,1},{1,0},{2,3},{3,2},{4,5},{5,4},{6,7},{7,6},{8,9},{9,8},{10,11... | collective-permute-start | bytes 6291464 | tf_op jit(solution)/shard_map/ppermute | solution.py:27
  100.1 7.4 %copy-start.9 = (f32[256,2048]{1,0:T(8,128)S(1)}, f32[256,2048]{1,0:T(8,128)}, u32[]{:S(2)}) copy-start(f32[256,2048]{1,0:T(8,128)} %get-tuple-element.222) | copy-start | bytes 6291460
  109.1 166.6 %reduce-scatter.9.cloned.1.call-start = ((), (), s32[]{:S(2)}) async-start(), calls=%async_computation.5 | async-start | bytes 17825792
  117.2 7.1 %copy-start.5 = (bf16[512,2048]{1,0:T(8,128)(2,1)S(1)}, bf16[512,2048]{1,0:T(8,128)(2,1)}, u32[]{:S(2)}) copy-start(bf16[512,2048]{1,0:T(8,128)(2,1)} %dense.3) | copy-start | bytes 6291460
  170.8 4.4 %collective-permute-start.12 = (f32[256,2048]{1,0:T(8,128)}, f32[256,2048]{1,0:T(8,128)S(1)}, u32[]{:S(2)}, u32[]{:S(2)}) collective-permute-start(f32[256,2048]{1,0:T(8,128)} %get-tuple-element.225), channel_id=1, source_target_pairs={{0,1},{1,0},{2,3},{3,2},{4,5},{5,4},{6,7},{7,6},{8,9},{9,8},{10,11... | collective-permute-start | bytes 6291464 | tf_op jit(solution)/shard_map/ppermute | solution.py:27
  178.6 81.5 %collective-permute-start.13 = (f32[256,2048]{1,0:T(8,128)}, f32[256,2048]{1,0:T(8,128)}, u32[]{:S(2)}, u32[]{:S(2)}) collective-permute-start(f32[256,2048]{1,0:T(8,128)} %add.87), channel_id=1, source_target_pairs={{0,2},{2,0},{1,3},{3,1},{4,6},{6,4},{5,7},{7,5},{8,10},{10,8},{9,1... | collective-permute-start | bytes 6291464 | tf_op jit(solution)/shard_map/ppermute | solution.py:27
  180.0 59.6 %collective-permute-start.6 = (f32[64,2048]{1,0:T(8,128)}, f32[64,2048]{1,0:T(8,128)}, u32[]{:S(2)}, u32[]{:S(2)}) collective-permute-start(f32[64,2048]{1,0:T(8,128)} %dynamic-slice_bitcast_fusion.1), channel_id=1, source_target_pairs={{0,64},{64,0},{1,65},{65,1},{2,66},{66,2},{3,67},{67,3},{4,68},{68... | collective-permute-start | bytes 1572872 | tf_op jit(solution)/shard_map/ppermute | solution.py:27
  188.7 6.0 %collective-permute-start.4 = (f32[32,512]{1,0:T(8,128)S(1)}, f32[32,512]{1,0:T(8,128)S(1)}, u32[]{:S(2)}, u32[]{:S(2)}) collective-permute-start(f32[32,512]{1,0:T(8,128)S(1)} %concatenate.27), channel_id=1, source_target_pairs={{0,16},{16,0},{32,48},{48,32},{1,17},{17,1},{33,49},{49,33},{2,18}... | collective-permute-start | bytes 196616 | tf_op jit(solution)/shard_map/ppermute | solution.py:31
  194.7 7.4 %collective-permute-start.5 = (f32[32,512]{1,0:T(8,128)S(1)}, f32[32,512]{1,0:T(8,128)S(1)}, u32[]{:S(2)}, u32[]{:S(2)}) collective-permute-start(f32[32,512]{1,0:T(8,128)S(1)} %add.73), channel_id=1, source_target_pairs={{0,32},{16,48},{32,0},{48,16},{1,33},{17,49},{33,1},{49,17},{2,34}... | collective-permute-start | bytes 196616 | tf_op jit(solution)/shard_map/ppermute | solution.py:31
  239.5 4.3 %collective-permute-start.7 = (f32[32,512]{1,0:T(8,128)S(1)}, f32[32,512]{1,0:T(8,128)S(1)}, u32[]{:S(2)}, u32[]{:S(2)}) collective-permute-start(f32[32,512]{1,0:T(8,128)S(1)} %add.74), channel_id=1, source_target_pairs={{0,4},{4,0},{8,12},{12,8},{1,5},{5,1},{9,13},{13,9},{2,6},{6,2},{1... | collective-permute-start | bytes 196616 | tf_op jit(solution)/shard_map/ppermute | solution.py:31
  243.8 6.3 %collective-permute-start.8 = (f32[32,512]{1,0:T(8,128)S(1)}, f32[32,512]{1,0:T(8,128)S(1)}, u32[]{:S(2)}, u32[]{:S(2)}) collective-permute-start(f32[32,512]{1,0:T(8,128)S(1)} %add.76), channel_id=1, source_target_pairs={{0,8},{4,12},{8,0},{12,4},{1,9},{5,13},{9,1},{13,5},{2,10},{6,14},... | collective-permute-start | bytes 196616 | tf_op jit(solution)/shard_map/ppermute | solution.py:31
  250.1 3.7 %collective-permute-start.9 = (f32[1,512]{1,0:T(1,128)S(1)}, f32[1,512]{1,0:T(1,128)S(1)}, u32[]{:S(2)}, u32[]{:S(2)}) collective-permute-start(f32[1,512]{1,0:T(1,128)S(1)} %constant_dynamic-slice_fusion), channel_id=1, source_target_pairs={{0,64},{64,0},{1,65},{65,1},{2,66},{66,2},{3,67},{67,3},{4,68},{68... | collective-permute-start | bytes 6152 | tf_op jit(solution)/shard_map/ppermute | solution.py:27
  253.8 1.2 collective-permute-start.10
  255.0 5.1 %collective-permute-start.11 = (f32[256]{0:T(256)S(1)}, f32[256]{0:T(256)S(1)}, u32[]{:S(2)}, u32[]{:S(2)}) collective-permute-start(f32[256]{0:T(256)S(1)} %add.84), channel_id=1, source_target_pairs={{0,2},{2,0},{1,3},{3,1},{4,6},{6,4},{5,7},{7,5},{8,10},{10,8},{9,1... | collective-permute-start | bytes 3080 | tf_op jit(solution)/shard_map/ppermute | solution.py:27
  264.1 5.3 %collective-permute-start.15 = (f32[256,2048]{1,0:T(8,128)}, f32[256,2048]{1,0:T(8,128)}, u32[]{:S(2)}, u32[]{:S(2)}) collective-permute-start(f32[256,2048]{1,0:T(8,128)} %add.88.combined), channel_id=1, source_target_pairs={{0,1},{1,0},{2,3},{3,2},{4,5},{5,4},{6,7},{7,6},{8,9},{9,8},{10,11... | collective-permute-start | bytes 6291464 | tf_op jit(solution)/shard_map/ppermute | solution.py:27
  264.1 7.5 %collective-permute-start.14 = (f32[256,2048]{1,0:T(8,128)}, f32[256,2048]{1,0:T(8,128)}, u32[]{:S(2)}, u32[]{:S(2)}) collective-permute-start(f32[256,2048]{1,0:T(8,128)} %all-reduce.5.cloned.1.call-done.branch), channel_id=1, source_target_pairs={{0,1},{1,0},{2,3},{3,2},{4,5},{5,4},{6,7},{7,6},{8,9},{9,8},{10,11... | collective-permute-start | bytes 6291464 | tf_op jit(solution)/shard_map/ppermute | solution.py:27
  264.6 7.0 %copy-start.1 = (bf16[512,2048]{1,0:T(8,128)(2,1)S(1)}, bf16[512,2048]{1,0:T(8,128)(2,1)}, u32[]{:S(2)}) copy-start(bf16[512,2048]{1,0:T(8,128)(2,1)} %hidden.4) | copy-start | bytes 6291460
  276.8 14.0 %collective-permute-start.16 = (f32[64,2048]{1,0:T(8,128)S(1)}, f32[64,2048]{1,0:T(8,128)S(1)}, u32[]{:S(2)}, u32[]{:S(2)}) collective-permute-start(f32[64,2048]{1,0:T(8,128)S(1)} %dynamic-slice_bitcast_fusion), channel_id=1, source_target_pairs={{0,64},{64,0},{1,65},{65,1},{2,66},{66,2},{3,67},{67,3},{4,68},{68... | collective-permute-start | bytes 1572872 | tf_op jit(solution)/shard_map/ppermute | solution.py:27
  279.6 14.8 %copy-start.21 = (f32[64]{0:T(128)}, f32[64]{0:T(128)S(1)}, u32[]{:S(2)}) copy-start(f32[64]{0:T(128)S(1)} %get-tuple-element.327) | copy-start | bytes 772
  (9 other events, 26.2 us)
Sparse Core Ops, SparseCore 0:
  12.0 63.2 all-gather.2
  109.2 72.3 all-reduce.4
Sparse Core Ops, SparseCore 1:
  34.6 112.8 reduce-scatter.6
  155.2 114.5 reduce-scatter.8

commit v3 on v2

--- a/solution.py
+++ b/solution.py
@@ -63,8 +63,13 @@
     return centred * inv_std, inv_std
 
 
-def second_kernel(hidden, cot, gain, shift, second_out, cot_turned, stats):
+def second_kernel(core, hidden, cot, gain, shift, second_out, cot_turned, stats, sent):
     rows = hidden[...].astype(F32)
+
+    @pl.when(pl.program_id(0) == core[0])
+    def _():
+        sent[...] = rows
+
     average = jnp.mean(rows, axis=-1, keepdims=True)
     centred = rows - average
     inv_std = lax.rsqrt(jnp.mean(centred * centred, axis=-1, keepdims=True) + EPSILON)
@@ -72,6 +77,33 @@
     put_turned(cot_turned, cot[...].astype(F32))
     lane = lax.broadcasted_iota(jnp.int32, (rows.shape[0], 128), 1)
     stats[...] = jnp.where(lane < 64, average, inv_std)
+
+
+def second(core, hidden, cot, gain, shift):
+    rows = TOK // 2
+    plain = pl.BlockSpec((rows, D), lambda i, s: (i, 0))
+    return pl.pallas_call(
+        second_kernel,
+        grid_spec=pltpu.PrefetchScalarGridSpec(
+            num_scalar_prefetch=1,
+            grid=(2,),
+            in_specs=[plain] * 2 + [whole((1, D))] * 2,
+            out_specs=[
+                plain,
+                pl.BlockSpec((16, 2, 64, rows), lambda i, s: (0, 0, 0, i)),
+                pl.BlockSpec((rows, 128), lambda i, s: (i, 0)),
+                pl.BlockSpec((rows, D), lambda i, s: (0, 0)),
+            ],
+        ),
+        out_shape=[
+            jax.ShapeDtypeStruct((TOK, D), BF16),
+            jax.ShapeDtypeStruct(TURNED, BF16),
+            jax.ShapeDtypeStruct((TOK, 128), F32),
+            jax.ShapeDtypeStruct((rows, D), F32),
+        ],
+        compiler_params=pltpu.CompilerParams(vmem_limit_bytes=VMEM),
+        cost_estimate=COST,
+    )(core, hidden, cot, gain.reshape(1, D), shift.reshape(1, D))
 
 
 def first_kernel(hidden, gain, shift, gain_two, shift_two, first_out, first_turned, second_turned):
@@ -106,18 +138,16 @@
 TURNED = (16, 2, 64, 2 * TOK)
 
 
-def norm_call(kernel, rows, n_rows, n_plain, n_turned, params, stats=False):
+def norm_call(kernel, rows, n_rows, n_plain, n_turned, params):
     plain = pl.BlockSpec((rows, D), lambda i: (i, 0))
     return pl.pallas_call(
         kernel,
         grid=(TOK // rows,),
         in_specs=[plain] * len(n_rows) + [whole((1, D))] * len(params),
         out_specs=[plain] * n_plain
-        + [pl.BlockSpec((16, 2, 64, rows), lambda i: (0, 0, 0, i))] * n_turned
-        + [pl.BlockSpec((rows, 128), lambda i: (i, 0))] * stats,
+        + [pl.BlockSpec((16, 2, 64, rows), lambda i: (0, 0, 0, i))] * n_turned,
         out_shape=[jax.ShapeDtypeStruct((TOK, D), BF16)] * n_plain
-        + [jax.ShapeDtypeStruct(TURNED, BF16)] * n_turned
-        + [jax.ShapeDtypeStruct((TOK, 128), F32)] * stats,
+        + [jax.ShapeDtypeStruct(TURNED, BF16)] * n_turned,
         compiler_params=pltpu.CompilerParams(vmem_limit_bytes=VMEM),
         cost_estimate=COST,
     )(*n_rows, *(p.reshape(1, D) for p in params))
@@ -618,26 +648,23 @@
     def of_core(values, which):
         return lax.dynamic_slice_in_dim(values, which * half_rows, half_rows, 0)
 
-    marks = jnp.concatenate([segment_ids, positions]).astype(F32).reshape(1, 2 * TOK)
-    hidden_sent = jnp.concatenate(
-        [of_core(hidden_in, core).astype(F32), jnp.pad(marks, ((0, 7), (0, D - 2 * TOK)))], axis=0
+    second_in, cot_turned, stats, hidden_sent = second(
+        at_core, hidden_in, cotangent, ln2_gain, ln2_bias
     )
     hidden_pair = lax.all_gather(hidden_sent, "zl")
-
-    second_in, cot_turned, stats = norm_call(
-        second_kernel, 256, (hidden_in, cotangent), 1, 1, (ln2_gain, ln2_bias), stats=True
-    )
     act_low, slope, down_grad = feed(second_in, cot_turned, fc1_weight, fc1_bias)
     down_sum = after(lax.psum_scatter(down_grad, ("x", "y"), scatter_dimension=0, tiled=True))
     _, cotangent, hidden_in = after((down_grad, cotangent, hidden_in))
 
-    cot_got = lax.ppermute(
-        of_core(cotangent, core).astype(F32), ("zl", "zh"), [(i, 3 - i) for i in range(4)]
-    )
+    marks = jnp.concatenate([segment_ids, positions]).astype(F32).reshape(1, 2 * TOK)
+    cot_sent = jnp.concatenate(
+        [of_core(cotangent, core).astype(F32), jnp.pad(marks, ((0, 7), (0, D - 2 * TOK)))], axis=0
+    )
+    cot_got = lax.ppermute(cot_sent, ("zl", "zh"), [(i, 3 - i) for i in range(4)])
 
     own_marks = marks.reshape(2, TOK)
 
-    def own_step(hidden_in, cotangent, slope):
+    def own_step(hidden_in, cotangent, act_low, slope):
         first_in, first_turned, second_turned = norm_call(
             first_kernel, 256, (hidden_in,), 1, 2, params
         )
@@ -646,17 +673,23 @@
             own_place, 2, projected, (cotangent, dense_weight), own_marks
         )
         grad_up = feed_back(cotangent, fc2_weight, slope)
-        return first_turned, second_turned, mixed_low, grad_packed, grad_up
-
-    first_turned, second_turned, mixed_low, grad_packed, grad_up = lax.cond(
-        core > 1, own_step, own_step, hidden_in, cotangent, slope
-    )
-    hidden_pair, cot_got, mixed_low = after((hidden_pair, cot_got, mixed_low))
+        branches = branch_halves(at_core, mixed_low, act_low, dense_weight, fc2_weight)
+        return first_turned, second_turned, mixed_low, grad_packed, grad_up, *branches
+
+    (
+        first_turned,
+        second_turned,
+        mixed_low,
+        grad_packed,
+        grad_up,
+        branch,
+        branch_other,
+    ) = lax.cond(core > 1, own_step, own_step, hidden_in, cotangent, act_low, slope)
+    hidden_pair, mixed_low = after((hidden_pair, mixed_low))
     hidden_got = lax.dynamic_slice_in_dim(hidden_pair, 1 - side, 1, 0)
-    hidden_too, cot_too = send(hidden_got, "c"), send(cot_got, "c")
-    branch, branch_other = branch_halves(at_core, mixed_low, act_low, dense_weight, fc2_weight)
-    hidden_too, branch_other = after((hidden_too, branch_other))
-    branch_too = send(branch_other, "c")
+    hidden_too, branch_too = send(hidden_got, "c"), send(branch_other, "c")
+    hidden_too, cot_got = after((hidden_too, cot_got))
+    cot_too = send(cot_got, "c")
 
     first_far_in, second_far_in, first_turned, second_turned = first_far(
         hidden_got, hidden_too, params, (first_turned, second_turned)
@@ -664,7 +697,7 @@
     second_far_in, branch_too = after((second_far_in, branch_too))
     branch = lax.psum(branch + branch_too, "zh")
     slope_side = slope_far(at_side, second_far_in, fc1_weight, fc1_bias)
-    marks_got = hidden_got[0, half_rows, : 2 * TOK].reshape(2, 2, half_rows)
+    marks_got = cot_got[half_rows, : 2 * TOK].reshape(2, 2, half_rows)
     marks_far = jnp.where(core == 0, marks_got, marks_got[:, ::-1]).reshape(2, TOK)
     projected_far = project(far_place, 1, first_far_in, qkv_weight, qkv_bias, marks_far)
     grad_up_far, grad_mixed_far, cot_turned = cot_far(
@@ -712,7 +745,6 @@
     for axis in ("x", "y"):
         small = small + swap(small, axis, 1)
         small = small + swap(small, axis, 2)
-        small, down_far = after((small, down_far))
     block = lax.axis_index("x") * 4 + lax.axis_index("y")
     own_small = lax.dynamic_slice_in_dim(small, side * 16 + block, 1, 0)
     far_small = lax.dynamic_slice_in_dim(small, (1 - side) * 16 + block, 1, 0)
@@ -721,7 +753,7 @@
     norms = small[:256]
     norms = norms + send(norms, "c")
     norms = norms + send(norms, "zh")
-    norms, branch, combined_too = after((norms, branch, combined_too))
+    norms, branch, combined_too, down_far = after((norms, branch, combined_too, down_far))
     combined = combined + combined_too
     norms = norms.reshape(4, 64)
     bias_total = small[256:320]

time: 303 us -> 286 us (0.944)
  waiting for transfers between devices: 92.5 us -> 77.5 us
    ppermute x12, waiting for transfers between devices: 62.8 us -> 45.8 us  [send(): return lax.ppermute(value, axis, [(i, (i + step) % n) for i in range(n)])]
    optimization_barrier x1, waiting for transfers between devices: 0.01 us -> 11.6 us  [body(): output, input_grad, joint_sum = after((*finals, joint_sum))]
    ppermute x1, waiting for transfers between devices: 14.4 us -> 3.41 us  [body(): lax.ppermute(cot_sent, ('zl', 'zh'), [(i, 3 - i) for i in range(4)])]
    pallas_call x0 -> x1, Pallas kernels: none -> 5.21 us  [second(): pl.pallas_call(second_kernel, grid_spec=pltpu.PrefetchScalarGridSpec(num_...]
    pallas_call x2 -> x1, Pallas kernels: 8.46 us -> 4.01 us  [norm_call(): pl.pallas_call(kernel, grid=(TOK // rows,), in_specs=[plain] * len(n_rows...]
  transfers between devices with their start and end apart: 21 -> 21, of which waited for: 12 -> 13; matrix products, arithmetic and copies ran while one was open for 9% -> 10% of each run, Pallas kernels for 46% -> 46%
where the time goes in v3:
time: 286 us
  Pallas kernels  138 us (48%)
  waiting for transfers between devices  77.5 us (27%)
  starting transfers between devices  21.4 us (7%)
  other arithmetic  19.1 us (7%)
  between operations  15.8 us (6%)
  local copies, waits for them, and re-layouts  13.7 us (5%)
    ppermute x12, waiting for transfers between devices, send(): return lax.ppermute(value, axis, [(i, (i + step) % n) for i in range(n)])  45.8 us
    pallas_call x2, Pallas kernels, halves_call(): pl.pallas_call(kernel, grid_spec=pltpu.PrefetchScalarGridSpec(num_scalar_...  24.6 us
    pallas_call x1, Pallas kernels, joint(): pl.pallas_call(joint_kernel, grid_spec=pltpu.PrefetchScalarGridSpec(num_s...  16.7 us
    ppermute x4, waiting for transfers between devices, swap(): return lax.ppermute(value, axis, [(i, i ^ bit) for i in range(SIZES[axis])])  16.5 us
    pallas_call x1, Pallas kernels, feed(): pl.pallas_call(feed_kernel, grid=(units // width,), in_specs=[whole((TOK,...  16.4 us
    pallas_call x2, Pallas kernels, project(): pl.pallas_call(project_kernel, grid_spec=pltpu.PrefetchScalarGridSpec(num...  14.6 us
    pallas_call x2, Pallas kernels, attend(): pl.pallas_call(attend_kernel, grid_spec=pltpu.PrefetchScalarGridSpec(num_...  13.8 us
    optimization_barrier x1, waiting for transfers between devices, body(): output, input_grad, joint_sum = after((*finals, joint_sum))  11.6 us
  transfers between devices with their start and end apart: 21, of which 13 were waited for; matrix products, arithmetic and copies ran while one was open for 10% of the time, Pallas kernels for 46%

profile of v3, /device:TPU:0, one launch (start us, length us, event | category | flops | bytes accessed | tf_op | source)
XLA Modules:
  0.0 285.5 jit_solution(2868247570852731416)
XLA Ops:
  8.1 5.2 %shard_map.281 = (bf16[512,2048]{1,0:T(8,128)(2,1)}, bf16[16,2,64,1024]{3,2,1,0:T(8,128)(2,1)}, f32[512,128]{1,0:T(8,128)}, f32[256,2048]{1,0:T(8,128)}) custom-call(s32[1]{0:T(128)} %bitcast.8.core.half, bf16[512,2048]{1,0:T(8,128)(2,1)} %hidden.4, bf16[512,2048]{1,0:T(8,128)(2,1)} %cot.3, f32[1,2048]{1,0:T(1,128)} %bitcast.47, f32[1,2048]{1,0:T(1,128)} %bitcast.56), custom_call_target="tpu_custom_call" | custom-call | flops 1000000 | bytes 1000000 | tf_op jit(solution)/shard_map/pallas_call | solution.py:85
  13.4 16.4 %shard_map.282 = (bf16[512,2048]{1,0:T(8,128)(2,1)}, f32[512,2048]{1,0:T(8,128)}, f32[16,128,2048]{2,1,0:T(8,128)}) custom-call(bf16[512,2048]{1,0:T(8,128)(2,1)} %get-tuple-element.191.second, bf16[16,2,64,1024]{3,2,1,0:T(8,128)(2,1)} %get-tuple-element.192.cot_turned.held, bf16[2048,2048]{1,0:T(8,128)(2,1)} %up.1, f32[4,4,128]{2,1,0:T(4,128)} %bitcast.68), custom_call_target="tpu_custom_call" | custom-call | flops 1000000 | bytes 1000000 | tf_op jit(solution)/shard_map/pallas_call | solution.py:202
  33.5 4.1 %collective-permute-start.1 = (f32[264,2048]{1,0:T(8,128)}, f32[264,2048]{1,0:T(8,128)}, u32[]{:S(2)}, u32[]{:S(2)}) collective-permute-start(f32[264,2048]{1,0:T(8,128)} %select_maximum_fusion), channel_id=1, source_target_pairs={{0,66},{2,64},{64,2},{66,0},{1,67},{3,65},{65,3},{67,1},{4,70},{6,... | collective-permute-start | bytes 6488072 | tf_op jit(solution)/shard_map/ppermute | solution.py:663
  37.6 41.1 %conditional.1 = (bf16[16,2,64,1024]{3,2,1,0:T(8,128)(2,1)}, bf16[16,2,64,1024]{3,2,1,0:T(8,128)(2,1)}, bf16[512,512]{1,0:T(8,128)(2,1)}, bf16[512,1536]{1,0:T(8...) conditional(s32[]{:T(128)} %convert_element_type.33, (f32[2048]{0:T(1024)S(1)}, ...), branch_computations={%region_0.0_spmd, %region_1.2_spmd} | conditional | flops 5000000 | bytes 30165976 | solution.py:687
  37.6 9.5 %branch_0_fun.8 = bf16[512,2048]{1,0:T(8,128)(2,1)} custom-call(bf16[512,2048]{1,0:T(8,128)(2,1)S(1)} %get-tuple-element.78.refs_0_.cot, bf16[2048,2048]{1,0:T(8,128)(2,1)} %get-tuple-element.82.weight.down, f32[512,2048]{1,0:T(8,128)} %get-tuple-element.83.slope), custom_call_target="tpu_custom_call" | custom-call | flops 1000000 | bytes 1000000 | tf_op jit(solution)/shard_map/cond/branch_0_fun/pallas_call | solution.py:229
  47.2 4.0 %branch_0_fun.5 = (bf16[512,2048]{1,0:T(8,128)(2,1)}, bf16[16,2,64,1024]{3,2,1,0:T(8,128)(2,1)}, bf16[16,2,64,1024]{3,2,1,0:T(8,128)(2,1)}) custom-call(bf16[512,2048]{1,0:T(8,128)(2,1)S(1)} %copy-done.2, f32[1,2048]{1,0:T(1,128)S(1)} %bitcast.54, f32[1,2048]{1,0:T(1,128)S(1)} %bitcast.64, f32[1,2048]{1,0:T(1,128)S(1)} %bitcast.50, f32[1,2048]{1,0:T(1,128)S(1)} %bitcast.58), custom_call_target="tpu_custom_call" | custom-call | flops 1000000 | bytes 1000000 | tf_op jit(solution)/shard_map/cond/branch_0_fun/pallas_call | solution.py:143
  51.7 8.5 %branch_0_fun.6 = (bf16[512,512]{1,0:T(8,128)(2,1)}, bf16[512,512]{1,0:T(8,128)(2,1)}, bf16[512,512]{1,0:T(8,128)(2,1)}, f32[512,128]{1,0:T(8,128)}, f32[512,128]{1,0:T(8,128)}, /*index=5*/f32[512,128]{1,0:T(8,128)}) custom-call(s32[2]{0:T(128)} %broadcast_1_place.0.place, bf16[512,2048]{1,0:T(8,128)(2,1)} %get-tuple-element.67.first, ...), custom_call_target="tpu_custom_call" | custom-call | flops 1000000 | bytes 1000000 | tf_op jit(solution)/shard_map/cond/branch_0_fun/pallas_call | solution.py:366
  60.2 8.9 %branch_0_fun.7 = (bf16[512,512]{1,0:T(8,128)(2,1)}, bf16[512,1536]{1,0:T(8,128)(2,1)}) custom-call(s32[2]{0:T(128)} %broadcast_1_place.0.place, bf16[512,512]{1,0:T(8,128)(2,1)} %get-tuple-element.72.queries, bf16[512,512]{1,0:T(8,128)(2,1)} %get-tuple-element.73.keys, bf16[512,512]{1,0:T(8,128)(2,1)} %get-tuple-element.74.values, ...), custom_call_target="tpu_custom_call" | custom-call | flops 1000000 | bytes 1000000 | tf_op jit(solution)/shard_map/cond/branch_0_fun/pallas_call | solution.py:420
  69.1 9.6 %branch_0_fun.9 = (f32[256,2048]{1,0:T(8,128)}, f32[256,2048]{1,0:T(8,128)}) custom-call(s32[1]{0:T(128)} %get-tuple-element.84.core, bf16[512,512]{1,0:T(8,128)(2,1)} %get-tuple-element.302.mixed, bf16[512,2048]{1,0:T(8,128)(2,1)S(1)} %copy-done.7, bf16[512,2048]{1,0:T(8,128)(2,1)S(1)} %copy-done.5, bf16[2048,2048]{1,0:T(8,128)(2,1)} %get-tuple-element.82.weight.down), custom_call_target="tpu_custom_call" | custom-call | flops 1000000 | bytes 1000000 | tf_op jit(solution)/shard_map/cond/branch_0_fun/pallas_call | solution.py:468
  81.4 3.4 %collective-permute-done.1.near = f32[264,2048]{1,0:T(8,128)} collective-permute-done((f32[264,2048]{1,0:T(8,128)}, f32[264,2048]{1,0:T(8,128)}, u32[]{:S(2)}, u32[]{:S(2)}) %collective-permute-start.1) | collective-permute-done | bytes 2162720 | tf_op jit(solution)/shard_map/ppermute | solution.py:663
  88.6 7.1 %shard_map.283 = (bf16[512,2048]{1,0:T(8,128)(2,1)}, bf16[512,2048]{1,0:T(8,128)(2,1)}, bf16[16,2,64,1024]{3,2,1,0:T(8,128)(2,1)}, bf16[16,2,64,1024]{3,2,1,0:T(8,128)(2,1)}) custom-call(f32[1,256,2048]{2,1,0:T(8,128)} %copy-done.9, f32[1,256,2048]{2,1,0:T(8,128)} %copy-done.10, ...), custom_call_target="tpu_custom_call", output_to_operand_aliasing={{2}: (6, {}), {3}: (7, {})} | custom-call | flops 1000000 | bytes 1000000 | tf_op jit(solution)/shard_map/pallas_call | solution.py:159
  95.7 3.5 %add.84 = f32[256,2048]{1,0:T(8,128)} add(f32[256,2048]{1,0:T(8,128)} %get-tuple-element.231, f32[256,2048]{1,0:T(8,128)S(1)} %collective-permute-done.3) | non-fusion elementwise | flops 524288 | bytes 6291456 | tf_op jit(solution)/shard_map/add | solution.py:698
  101.5 6.5 %shard_map.284.slope = f32[512,1024]{1,0:T(8,128)} custom-call(s32[1]{0:T(128)} %bitcast.9.side, bf16[512,2048]{1,0:T(8,128)(2,1)} %get-tuple-element.207.second, bf16[2048,2048]{1,0:T(8,128)(2,1)} %up.1, f32[4,4,128]{2,1,0:T(4,128)} %bitcast.69), custom_call_target="tpu_custom_call" | custom-call | flops 1000000 | bytes 1000000 | tf_op jit(solution)/shard_map/pallas_call | solution.py:296
  108.0 6.1 %shard_map.286 = (bf16[512,256]{1,0:T(8,128)(2,1)}, bf16[512,256]{1,0:T(8,128)(2,1)}, bf16[512,256]{1,0:T(8,128)(2,1)}, f32[512,128]{1,0:T(8,128)}, f32[512,128]{1,0:T(8,128)}, /*index=5*/f32[512,128]{1,0:T(8,128)}) custom-call(s32[2]{0:T(128)} %pad_add_fusion.place, bf16[512,2048]{1,0:T(8,128)(2,1)} %get-tuple-element.213.first, bf16[2048,1536]{1,0:T(8,128)(2,1)} %qkv.1, ...), custom_call_target="tpu_custom_call" | custom-call | flops 1000000 | bytes 1000000 | tf_op jit(solution)/shard_map/pallas_call | solution.py:366
  114.1 8.3 %shard_map.285 = (bf16[512,1024]{1,0:T(8,128)(2,1)}, bf16[512,256]{1,0:T(8,128)(2,1)}, bf16[16,2,64,1024]{3,2,1,0:T(8,128)(2,1)}) custom-call(s32[1]{0:T(128)} %bitcast.9.side, f32[264,2048]{1,0:T(8,128)} %collective-permute-done.1.near, f32[264,2048]{1,0:T(8,128)} %collective-permute-done.2.other, ...), custom_call_target="tpu_custom_call", output_to_operand_aliasing={{2}: (6, {})} | custom-call | flops 1000000 | bytes 1000000 | tf_op jit(solution)/shard_map/pallas_call | solution.py:257
  122.4 4.9 %shard_map.287 = (bf16[512,256]{1,0:T(8,128)(2,1)}, bf16[512,768]{1,0:T(8,128)(2,1)}) custom-call(s32[2]{0:T(128)} %pad_add_fusion.place, bf16[512,256]{1,0:T(8,128)(2,1)} %get-tuple-element.214.queries, bf16[512,256]{1,0:T(8,128)(2,1)} %get-tuple-element.215.keys, bf16[512,256]{1,0:T(8,128)(2,1)} %get-tuple-element.216.values, ...), custom_call_target="tpu_custom_call" | custom-call | flops 1000000 | bytes 1000000 | tf_op jit(solution)/shard_map/pallas_call | solution.py:420
  127.3 16.7 %shard_map.288 = f32[16,128,2048]{2,1,0:T(8,128)} custom-call(s32[1]{0:T(128)} %bitcast.9.side, bf16[16,2,64,1024]{3,2,1,0:T(8,128)(2,1)} %get-tuple-element.203.refs_0_, bf16[16,2,64,1024]{3,2,1,0:T(8,128)(2,1)} %get-tuple-element.208.refs_1_, bf16[16,2,64,1024]{3,2,1,0:T(8,128)(2,1)} %get-tuple-element.209.refs_2_, ...), custom_call_target="tpu_custom_call" | custom-call | flops 1000000 | bytes 1000000 | tf_op jit(solution)/shard_map/pallas_call | solution.py:571
  144.1 15.0 %shard_map.289 = (f32[256,2048]{1,0:T(8,128)}, f32[256,2048]{1,0:T(8,128)}, f32[8,2048]{1,0:T(8,128)}) custom-call(s32[1]{0:T(128)} %bitcast.8.core.half, bf16[512,1536]{1,0:T(8,128)(2,1)} %get-tuple-element.226.refs_7_.packed, bf16[512,2048]{1,0:T(8,128)(2,1)} %get-tuple-element.227.refs_3_.up_grad, bf16[2048,1536]{1,0:T(8,128)(2,1)} %qkv.1, ...), custom_call_target="tpu_custom_call" | custom-call | flops 1000000 | bytes 1000000 | tf_op jit(solution)/shard_map/pallas_call | solution.py:468
  160.2 4.0 %collective-permute-done.11 = f32[256,2048]{1,0:T(8,128)S(1)} collective-permute-done((f32[256,2048]{1,0:T(8,128)}, f32[256,2048]{1,0:T(8,128)S(1)}, u32[]{:S(2)}, u32[]{:S(2)}) %collective-permute-start.11) | collective-permute-done | bytes 2097184 | tf_op jit(solution)/shard_map/ppermute | solution.py:27
  164.2 3.2 %add.85 = f32[256,2048]{1,0:T(8,128)} add(f32[256,2048]{1,0:T(8,128)} %get-tuple-element.233, f32[256,2048]{1,0:T(8,128)S(1)} %collective-permute-done.11) | non-fusion elementwise | flops 524288 | bytes 6291456 | tf_op jit(solution)/shard_map/add | solution.py:723
  175.4 4.6 %collective-permute-done.4 = f32[32,512]{1,0:T(8,128)S(1)} collective-permute-done((f32[32,512]{1,0:T(8,128)S(1)}, f32[32,512]{1,0:T(8,128)S(1)}, u32[]{:S(2)}, u32[]{:S(2)}) %collective-permute-start.4) | collective-permute-done | bytes 65568 | tf_op jit(solution)/shard_map/ppermute | solution.py:31
  180.0 2.7 collective-permute-start.5
  184.4 3.0 %collective-permute-done.5 = f32[32,512]{1,0:T(8,128)S(1)} collective-permute-done((f32[32,512]{1,0:T(8,128)S(1)}, f32[32,512]{1,0:T(8,128)S(1)}, u32[]{:S(2)}, u32[]{:S(2)}) %collective-permute-start.5) | collective-permute-done | bytes 65568 | tf_op jit(solution)/shard_map/ppermute | solution.py:31
  188.9 4.2 %collective-permute-done.6 = f32[32,512]{1,0:T(8,128)S(1)} collective-permute-done((f32[32,512]{1,0:T(8,128)S(1)}, f32[32,512]{1,0:T(8,128)S(1)}, u32[]{:S(2)}, u32[]{:S(2)}) %collective-permute-start.6) | collective-permute-done | bytes 65568 | tf_op jit(solution)/shard_map/ppermute | solution.py:31
  195.6 4.7 %collective-permute-done.7 = f32[32,512]{1,0:T(8,128)S(1)} collective-permute-done((f32[32,512]{1,0:T(8,128)S(1)}, f32[32,512]{1,0:T(8,128)S(1)}, u32[]{:S(2)}, u32[]{:S(2)}) %collective-permute-start.7) | collective-permute-done | bytes 65568 | tf_op jit(solution)/shard_map/ppermute | solution.py:31
  200.8 25.7 %collective-permute-done.8 = f32[1,512]{1,0:T(1,128)S(1)} collective-permute-done((f32[1,512]{1,0:T(1,128)S(1)}, f32[1,512]{1,0:T(1,128)S(1)}, u32[]{:S(2)}, u32[]{:S(2)}) %collective-permute-start.8) | collective-permute-done | bytes 2080 | tf_op jit(solution)/shard_map/ppermute | solution.py:27
  230.0 2.8 collective-permute-done.10
  232.8 3.9 %add.87.combined = f32[256,2048]{1,0:T(8,128)} add(f32[256,2048]{1,0:T(8,128)} %add.85, f32[256,2048]{1,0:T(8,128)} %collective-permute-done.12) | non-fusion elementwise | flops 524288 | bytes 6291456 | tf_op jit(solution)/shard_map/add | solution.py:757
  238.8 4.8 %shard_map.290 = (f32[512,2048]{1,0:T(8,128)}, f32[512,2048]{1,0:T(8,128)}) custom-call(s32[1]{0:T(128)} %bitcast.8.core.half, f32[256,2048]{1,0:T(8,128)} %all-reduce.5.cloned.1.call-done.branch, f32[256,2048]{1,0:T(8,128)} %add.87.combined, bf16[512,2048]{1,0:T(8,128)(2,1)} %hidden.4, bf16[512,2048]{1,0:T(8,128)(2,1)S(1)} %copy-done, ...), custom_call_target="tpu_custom_call" | custom-call | flops 1000000 | bytes 1000000 | tf_op jit(solution)/shard_map/pallas_call | solution.py:518
  244.3 4.2 %shard_map.291 = (f32[512,2048]{1,0:T(8,128)}, f32[512,2048]{1,0:T(8,128)}) custom-call(s32[1]{0:T(128)S(6)} %sub.4.half, f32[256,2048]{1,0:T(8,128)} %collective-permute-done.14.branch, f32[256,2048]{1,0:T(8,128)} %collective-permute-done.15.combined, bf16[512,2048]{1,0:T(8,128)(2,1)S(1)} %copy-done.1, ...), custom_call_target="tpu_custom_call", output_to_operand_aliasing={{0}: (8, {}), {1}: (9, {})} | custom-call | flops 1000000 | bytes 1000000 | tf_op jit(solution)/shard_map/pallas_call | solution.py:518
  248.5 11.6 %reduce-scatter.9.cloned.1.call-done.near = f32[1,128,2048]{2,1,0:T(8,128)} async-done(((f32[16,128,2048]{2,1,0:T(8,128)}), f32[1,128,2048]{2,1,0:T(8,128)}) %reduce-scatter.9.cloned.1.call-update) | async-done | bytes 1048592 | tf_op jit(solution)/shard_map/optimization_barrier | solution.py:765
  265.3 9.3 %collective-permute-done.16.far = f32[64,2048]{1,0:T(8,128)S(1)} collective-permute-done((f32[64,2048]{1,0:T(8,128)S(1)}, f32[64,2048]{1,0:T(8,128)S(1)}, u32[]{:S(2)}, u32[]{:S(2)}) %collective-permute-start.16) | collective-permute-done | bytes 524320 | tf_op jit(solution)/shard_map/ppermute | solution.py:27
  (122 shorter events, 43.1 us)
Async XLA Ops:
  8.0 70.7 %all-gather.3.cloned.1.call-start = ((), (), s32[]{:S(2)}) async-start(), calls=%async_computation.3 | async-start | bytes 6291456 | tf_op jit(solution)/shard_map/all_gather | solution.py:654
  13.3 130.8 %reduce-scatter.7.cloned.1.call-start = ((), (), s32[]{:S(2)}) async-start(), calls=%async_computation.4 | async-start | bytes 17825792
  29.8 203.0 %all-reduce.5.cloned.1.call-start = ((), (), s32[]{:S(2)}) async-start(), calls=%async_computation.2 | async-start | bytes 4194304 | tf_op jit(solution)/shard_map/psum | solution.py:698
  31.8 5.7 %copy-start.13 = (f32[2048]{0:T(1024)S(1)}, f32[2048]{0:T(1024)}, u32[]{:S(2)}) copy-start(f32[2048]{0:T(1024)} %param.29) | copy-start | bytes 24580
  31.8 5.7 %copy-start.14 = (f32[32,1]{1,0:T(8,128)S(1)}, f32[32,1]{1,0:T(8,128)}, u32[]{:S(2)}) copy-start(f32[32,1]{1,0:T(8,128)} %constant.53.clone.inverse) | copy-start | bytes 388
  31.9 5.7 %copy-start.15 = (f32[2048]{0:T(1024)S(1)}, f32[2048]{0:T(1024)}, u32[]{:S(2)}) copy-start(f32[2048]{0:T(1024)} %param.23) | copy-start | bytes 24580
  31.9 5.7 %copy-start.16 = (f32[2048]{0:T(1024)S(1)}, f32[2048]{0:T(1024)}, u32[]{:S(2)}) copy-start(f32[2048]{0:T(1024)} %param.30) | copy-start | bytes 24580
  33.5 51.3 %collective-permute-start.1 = (f32[264,2048]{1,0:T(8,128)}, f32[264,2048]{1,0:T(8,128)}, u32[]{:S(2)}, u32[]{:S(2)}) collective-permute-start(f32[264,2048]{1,0:T(8,128)} %select_maximum_fusion), channel_id=1, source_target_pairs={{0,66},{2,64},{64,2},{66,0},{1,67},{3,65},{65,3},{67,1},{4,70},{6,... | collective-permute-start | bytes 6488072 | tf_op jit(solution)/shard_map/ppermute | solution.py:663
  37.6 9.6 %copy-start.2 = (bf16[512,2048]{1,0:T(8,128)(2,1)S(1)}, bf16[512,2048]{1,0:T(8,128)(2,1)}, u32[]{:S(2)}) copy-start(bf16[512,2048]{1,0:T(8,128)(2,1)} %get-tuple-element.60.hidden) | copy-start | bytes 6291460 | tf_op jit(solution)/shard_map/cond
  51.7 8.5 %copy-start.5 = (bf16[512,2048]{1,0:T(8,128)(2,1)S(1)}, bf16[512,2048]{1,0:T(8,128)(2,1)}, u32[]{:S(2)}) copy-start(bf16[512,2048]{1,0:T(8,128)(2,1)} %get-tuple-element.79.refs_1_.dense) | copy-start | bytes 6291460 | tf_op jit(solution)/shard_map/cond
  60.2 8.9 %copy-start.7 = (bf16[512,2048]{1,0:T(8,128)(2,1)S(1)}, bf16[512,2048]{1,0:T(8,128)(2,1)}, u32[]{:S(2)}) copy-start(bf16[512,2048]{1,0:T(8,128)(2,1)} %get-tuple-element.85.act) | copy-start | bytes 6291460 | tf_op jit(solution)/shard_map/cond
  80.8 7.8 %copy-start.9 = (f32[1,256,2048]{2,1,0:T(8,128)}, f32[1,256,2048]{2,1,0:T(8,128)S(1)}, u32[]{:S(2)}) copy-start(f32[1,256,2048]{2,1,0:T(8,128)S(1)} %constant_dynamic-slice_fusion.1.near) | copy-start | bytes 6291460
  80.8 6.3 %collective-permute-start = (f32[1,256,2048]{2,1,0:T(8,128)S(1)}, f32[1,256,2048]{2,1,0:T(8,128)S(1)}, u32[]{:S(2)}, u32[]{:S(2)}) collective-permute-start(f32[1,256,2048]{2,1,0:T(8,128)S(1)} %constant_dynamic-slice_fusion.1.near), channel_id=1, source_target_pairs={{0,1},{1,0},{2,3},{3,2},{4,5},{5,4},{6,7},{7,6},{8,9},{9,8},{10,11... | collective-permute-start | bytes 6291464 | tf_op jit(solution)/shard_map/ppermute | solution.py:27
  80.9 14.8 %collective-permute-start.3 = (f32[256,2048]{1,0:T(8,128)}, f32[256,2048]{1,0:T(8,128)S(1)}, u32[]{:S(2)}, u32[]{:S(2)}) collective-permute-start(f32[256,2048]{1,0:T(8,128)} %get-tuple-element.206), channel_id=1, source_target_pairs={{0,1},{1,0},{2,3},{3,2},{4,5},{5,4},{6,7},{7,6},{8,9},{9,8},{10,11... | collective-permute-start | bytes 6291464 | tf_op jit(solution)/shard_map/ppermute | solution.py:27
  88.4 25.7 %collective-permute-start.2 = (f32[264,2048]{1,0:T(8,128)}, f32[264,2048]{1,0:T(8,128)}, u32[]{:S(2)}, u32[]{:S(2)}) collective-permute-start(f32[264,2048]{1,0:T(8,128)} %collective-permute-done.1.near), channel_id=1, source_target_pairs={{0,1},{1,0},{2,3},{3,2},{4,5},{5,4},{6,7},{7,6},{8,9},{9,8},{10,11... | collective-permute-start | bytes 6488072 | tf_op jit(solution)/shard_map/ppermute | solution.py:27
  99.2 160.9 %reduce-scatter.9.cloned.1.call-start = ((), (), s32[]{:S(2)}) async-start(), calls=%async_computation.5 | async-start | bytes 17825792
  108.0 6.1 %copy-start.4 = (bf16[512,2048]{1,0:T(8,128)(2,1)S(1)}, bf16[512,2048]{1,0:T(8,128)(2,1)}, u32[]{:S(2)}) copy-start(bf16[512,2048]{1,0:T(8,128)(2,1)} %dense.1) | copy-start | bytes 6291460
  159.1 5.1 %collective-permute-start.11 = (f32[256,2048]{1,0:T(8,128)}, f32[256,2048]{1,0:T(8,128)S(1)}, u32[]{:S(2)}, u32[]{:S(2)}) collective-permute-start(f32[256,2048]{1,0:T(8,128)} %get-tuple-element.234), channel_id=1, source_target_pairs={{0,1},{1,0},{2,3},{3,2},{4,5},{5,4},{6,7},{7,6},{8,9},{9,8},{10,11... | collective-permute-start | bytes 6291464 | tf_op jit(solution)/shard_map/ppermute | solution.py:27
  167.5 65.4 %collective-permute-start.12 = (f32[256,2048]{1,0:T(8,128)}, f32[256,2048]{1,0:T(8,128)}, u32[]{:S(2)}, u32[]{:S(2)}) collective-permute-start(f32[256,2048]{1,0:T(8,128)} %add.85), channel_id=1, source_target_pairs={{0,2},{2,0},{1,3},{3,1},{4,6},{6,4},{5,7},{7,5},{8,10},{10,8},{9,1... | collective-permute-start | bytes 6291464 | tf_op jit(solution)/shard_map/ppermute | solution.py:27
  171.2 11.6 %copy-start.11 = (f32[1,128,2048]{2,1,0:T(8,128)S(1)}, f32[1,128,2048]{2,1,0:T(8,128)}, u32[]{:S(2)}) copy-start(f32[1,128,2048]{2,1,0:T(8,128)} %reduce-scatter.7.cloned.1.call-done) | copy-start | bytes 3145732
  174.1 5.8 %collective-permute-start.4 = (f32[32,512]{1,0:T(8,128)S(1)}, f32[32,512]{1,0:T(8,128)S(1)}, u32[]{:S(2)}, u32[]{:S(2)}) collective-permute-start(f32[32,512]{1,0:T(8,128)S(1)} %concatenate.27), channel_id=1, source_target_pairs={{0,16},{16,0},{32,48},{48,32},{1,17},{17,1},{33,49},{49,33},{2,18}... | collective-permute-start | bytes 196616 | tf_op jit(solution)/shard_map/ppermute | solution.py:31
  180.0 7.5 %collective-permute-start.5 = (f32[32,512]{1,0:T(8,128)S(1)}, f32[32,512]{1,0:T(8,128)S(1)}, u32[]{:S(2)}, u32[]{:S(2)}) collective-permute-start(f32[32,512]{1,0:T(8,128)S(1)} %add.72), channel_id=1, source_target_pairs={{0,32},{16,48},{32,0},{48,16},{1,33},{17,49},{33,1},{49,17},{2,34}... | collective-permute-start | bytes 196616 | tf_op jit(solution)/shard_map/ppermute | solution.py:31
  183.6 49.3 %collective-permute-start.13 = (f32[64,2048]{1,0:T(8,128)}, f32[64,2048]{1,0:T(8,128)}, u32[]{:S(2)}, u32[]{:S(2)}) collective-permute-start(f32[64,2048]{1,0:T(8,128)} %dynamic-slice_bitcast_fusion.1), channel_id=1, source_target_pairs={{0,64},{64,0},{1,65},{65,1},{2,66},{66,2},{3,67},{67,3},{4,68},{68... | collective-permute-start | bytes 1572872 | tf_op jit(solution)/shard_map/ppermute | solution.py:27
  187.5 5.6 %collective-permute-start.6 = (f32[32,512]{1,0:T(8,128)S(1)}, f32[32,512]{1,0:T(8,128)S(1)}, u32[]{:S(2)}, u32[]{:S(2)}) collective-permute-start(f32[32,512]{1,0:T(8,128)S(1)} %add.73), channel_id=1, source_target_pairs={{0,4},{4,0},{8,12},{12,8},{1,5},{5,1},{9,13},{13,9},{2,6},{6,2},{1... | collective-permute-start | bytes 196616 | tf_op jit(solution)/shard_map/ppermute | solution.py:31
  193.1 7.2 %collective-permute-start.7 = (f32[32,512]{1,0:T(8,128)S(1)}, f32[32,512]{1,0:T(8,128)S(1)}, u32[]{:S(2)}, u32[]{:S(2)}) collective-permute-start(f32[32,512]{1,0:T(8,128)S(1)} %add.74), channel_id=1, source_target_pairs={{0,8},{4,12},{8,0},{12,4},{1,9},{5,13},{9,1},{13,5},{2,10},{6,14},... | collective-permute-start | bytes 196616 | tf_op jit(solution)/shard_map/ppermute | solution.py:31
  200.4 26.1 %collective-permute-start.8 = (f32[1,512]{1,0:T(1,128)S(1)}, f32[1,512]{1,0:T(1,128)S(1)}, u32[]{:S(2)}, u32[]{:S(2)}) collective-permute-start(f32[1,512]{1,0:T(1,128)S(1)} %constant_dynamic-slice_fusion), channel_id=1, source_target_pairs={{0,64},{64,0},{1,65},{65,1},{2,66},{66,2},{3,67},{67,3},{4,68},{68... | collective-permute-start | bytes 6152 | tf_op jit(solution)/shard_map/ppermute | solution.py:27
  226.5 1.2 collective-permute-start.9
  227.7 5.1 %collective-permute-start.10 = (f32[256]{0:T(256)S(1)}, f32[256]{0:T(256)S(1)}, u32[]{:S(2)}, u32[]{:S(2)}) collective-permute-start(f32[256]{0:T(256)S(1)} %add.82), channel_id=1, source_target_pairs={{0,2},{2,0},{1,3},{3,1},{4,6},{6,4},{5,7},{7,5},{8,10},{10,8},{9,1... | collective-permute-start | bytes 3080 | tf_op jit(solution)/shard_map/ppermute | solution.py:27
  236.8 6.9 %collective-permute-start.15 = (f32[256,2048]{1,0:T(8,128)}, f32[256,2048]{1,0:T(8,128)}, u32[]{:S(2)}, u32[]{:S(2)}) collective-permute-start(f32[256,2048]{1,0:T(8,128)} %add.87.combined), channel_id=1, source_target_pairs={{0,1},{1,0},{2,3},{3,2},{4,5},{5,4},{6,7},{7,6},{8,9},{9,8},{10,11... | collective-permute-start | bytes 6291464 | tf_op jit(solution)/shard_map/ppermute | solution.py:27
  236.8 7.5 %collective-permute-start.14 = (f32[256,2048]{1,0:T(8,128)}, f32[256,2048]{1,0:T(8,128)}, u32[]{:S(2)}, u32[]{:S(2)}) collective-permute-start(f32[256,2048]{1,0:T(8,128)} %all-reduce.5.cloned.1.call-done.branch), channel_id=1, source_target_pairs={{0,1},{1,0},{2,3},{3,2},{4,5},{5,4},{6,7},{7,6},{8,9},{9,8},{10,11... | collective-permute-start | bytes 6291464 | tf_op jit(solution)/shard_map/ppermute | solution.py:27
  238.1 39.5 %copy-start.22 = (f32[64]{0:T(128)}, f32[64]{0:T(128)S(1)}, u32[]{:S(2)}) copy-start(f32[64]{0:T(128)S(1)} %get-tuple-element.341) | copy-start | bytes 772
  261.1 13.4 %collective-permute-start.16 = (f32[64,2048]{1,0:T(8,128)S(1)}, f32[64,2048]{1,0:T(8,128)S(1)}, u32[]{:S(2)}, u32[]{:S(2)}) collective-permute-start(f32[64,2048]{1,0:T(8,128)S(1)} %dynamic-slice_bitcast_fusion), channel_id=1, source_target_pairs={{0,64},{64,0},{1,65},{65,1},{2,66},{66,2},{3,67},{67,3},{4,68},{68... | collective-permute-start | bytes 1572872 | tf_op jit(solution)/shard_map/ppermute | solution.py:27
  (9 other events, 24.8 us)
Sparse Core Ops, SparseCore 0:
  13.4 61.7 all-gather.2
  99.3 70.4 all-reduce.4
Sparse Core Ops, SparseCore 1:
  29.9 112.8 reduce-scatter.6
  146.5 113.5 reduce-scatter.8

commit v4 on v3

--- a/solution.py
+++ b/solution.py
@@ -40,6 +40,7 @@
 
 
 VMEM = 56 * 1024 * 1024
+VMEM_LESS = 24 * 1024 * 1024
 COST = pl.CostEstimate(flops=1000000, bytes_accessed=1000000, transcendentals=0)
 
 
@@ -63,7 +64,7 @@
     return centred * inv_std, inv_std
 
 
-def second_kernel(core, hidden, cot, gain, shift, second_out, cot_turned, stats, sent):
+def second_kernel(core, hidden, gain, shift, second_out, stats, sent):
     rows = hidden[...].astype(F32)
 
     @pl.when(pl.program_id(0) == core[0])
@@ -74,12 +75,11 @@
     centred = rows - average
     inv_std = lax.rsqrt(jnp.mean(centred * centred, axis=-1, keepdims=True) + EPSILON)
     second_out[...] = (centred * inv_std * gain[...] + shift[...]).astype(BF16)
-    put_turned(cot_turned, cot[...].astype(F32))
     lane = lax.broadcasted_iota(jnp.int32, (rows.shape[0], 128), 1)
     stats[...] = jnp.where(lane < 64, average, inv_std)
 
 
-def second(core, hidden, cot, gain, shift):
+def second(core, hidden, gain, shift):
     rows = TOK // 2
     plain = pl.BlockSpec((rows, D), lambda i, s: (i, 0))
     return pl.pallas_call(
@@ -87,31 +87,32 @@
         grid_spec=pltpu.PrefetchScalarGridSpec(
             num_scalar_prefetch=1,
             grid=(2,),
-            in_specs=[plain] * 2 + [whole((1, D))] * 2,
+            in_specs=[plain] + [whole((1, D))] * 2,
             out_specs=[
                 plain,
-                pl.BlockSpec((16, 2, 64, rows), lambda i, s: (0, 0, 0, i)),
                 pl.BlockSpec((rows, 128), lambda i, s: (i, 0)),
                 pl.BlockSpec((rows, D), lambda i, s: (0, 0)),
             ],
         ),
         out_shape=[
             jax.ShapeDtypeStruct((TOK, D), BF16),
-            jax.ShapeDtypeStruct(TURNED, BF16),
             jax.ShapeDtypeStruct((TOK, 128), F32),
             jax.ShapeDtypeStruct((rows, D), F32),
         ],
         compiler_params=pltpu.CompilerParams(vmem_limit_bytes=VMEM),
         cost_estimate=COST,
-    )(core, hidden, cot, gain.reshape(1, D), shift.reshape(1, D))
-
-
-def first_kernel(hidden, gain, shift, gain_two, shift_two, first_out, first_turned, second_turned):
+    )(core, hidden, gain.reshape(1, D), shift.reshape(1, D))
+
+
+def first_kernel(
+    hidden, cot, gain, shift, gain_two, shift_two, first_out, first_turned, second_turned, cot_turned
+):
     normed, _ = normalise(hidden[...].astype(F32))
     first = normed * gain[...] + shift[...]
     first_out[...] = first.astype(BF16)
     put_turned(first_turned, first)
     put_turned(second_turned, normed * gain_two[...] + shift_two[...])
+    put_turned(cot_turned, cot[...].astype(F32))
 
 
 def first_far_kernel(near, other, gain, shift, gain_two, shift_two, *refs):
@@ -187,16 +188,19 @@
     return jnp.concatenate([block[i : i + 1, :] for i in range(block.shape[0])], axis=1)
 
 
-def feed_kernel(second, cot_turned, weight, bias, act_out, slope_out, down_grad):
+def feed_kernel(second, cot, weight, bias, act_out, slope_out, down_grad):
     upward = plain_dot(second[...], weight[...]) + as_row(bias[0])
     below = phi(upward)
     act = (upward * below).astype(BF16)
     act_out[...] = act
     slope_out[...] = gelu_slope(upward, below)
-    down_grad[...] = plain_dot(cot_turned[...].reshape(D, TOK), act).reshape(16, 128, -1)
-
-
-def feed(second, cot_turned, weight, bias):
+    total = lax.dot_general(cot[...], act, (((0,), (0,)), ((), ())), preferred_element_type=F32)
+    for z in range(2):
+        rows = total[z * 1024 : z * 1024 + 1024]
+        down_grad[:, z * 64 : z * 64 + 64] = rows.reshape(16, 64, -1)
+
+
+def feed(second, cot, weight, bias):
     units, width = weight.shape[1], 512
     column = pl.BlockSpec((TOK, width), lambda j: (0, j))
     return pl.pallas_call(
@@ -204,7 +208,7 @@
         grid=(units // width,),
         in_specs=[
             whole((TOK, D)),
-            whole((16, 2, 64, TOK)),
+            whole((TOK, D)),
             pl.BlockSpec((D, width), lambda j: (0, j)),
             pl.BlockSpec((1, width // 128, 128), lambda j: (j, 0, 0)),
         ],
@@ -216,7 +220,7 @@
         ],
         compiler_params=pltpu.CompilerParams(vmem_limit_bytes=VMEM),
         cost_estimate=COST,
-    )(second, cot_turned, weight, bias.reshape(-1, width // 128, 128))
+    )(second, cot, weight, bias.reshape(-1, width // 128, 128))
 
 
 def feed_back_kernel(cot, weight, slope, up_grad):
@@ -285,14 +289,16 @@
     )(side, near, other, weight, slope, dense, held)
 
 
-def slope_far_kernel(side, second, weight, bias, slope):
+def slope_far_kernel(side, second, weight, bias, sums, sums_too, slope, total):
     upward = plain_dot(second[...], weight[...]) + as_row(bias[0])
     slope[...] = gelu_slope(upward, phi(upward))
-
-
-def slope_far(side, second, weight, bias):
+    total[...] = sums[...] + sums_too[...]
+
+
+def slope_far(side, second, weight, bias, sums, sums_too):
     units, width = weight.shape[1] // 2, 512
     steps = units // width
+    piece = pl.BlockSpec((TOK // 2 // steps, D), lambda j, s: (j, 0))
     return pl.pallas_call(
         slope_far_kernel,
         grid_spec=pltpu.PrefetchScalarGridSpec(
@@ -302,13 +308,18 @@
                 whole((TOK, D)),
                 pl.BlockSpec((D, width), lambda j, s: (0, s[0] * steps + j)),
                 pl.BlockSpec((1, width // 128, 128), lambda j, s: (s[0] * steps + j, 0, 0)),
+                piece,
+                piece,
             ],
-            out_specs=pl.BlockSpec((TOK, width), lambda j, s: (0, j)),
-        ),
-        out_shape=jax.ShapeDtypeStruct((TOK, units), F32),
-        compiler_params=pltpu.CompilerParams(vmem_limit_bytes=VMEM),
-        cost_estimate=COST,
-    )(side, second, weight, bias.reshape(-1, width // 128, 128))
+            out_specs=[pl.BlockSpec((TOK, width), lambda j, s: (0, j)), piece],
+        ),
+        out_shape=[
+            jax.ShapeDtypeStruct((TOK, units), F32),
+            jax.ShapeDtypeStruct((TOK // 2, D), F32),
+        ],
+        compiler_params=pltpu.CompilerParams(vmem_limit_bytes=VMEM),
+        cost_estimate=COST,
+    )(side, second, weight, bias.reshape(-1, width // 128, 128), sums, sums_too)
 
 
 def turn(values, tables, sign):
@@ -528,7 +539,7 @@
         ),
         out_shape=[jax.ShapeDtypeStruct((TOK, D), F32)] * 2,
         input_output_aliases={8: 0, 9: 1} if held else {},
-        compiler_params=pltpu.CompilerParams(vmem_limit_bytes=VMEM),
+        compiler_params=pltpu.CompilerParams(vmem_limit_bytes=VMEM_LESS),
         cost_estimate=COST,
     )(half, branch, combined, hidden, cot, stats, *(b.reshape(1, D) for b in biases), *held)
 
@@ -612,7 +623,7 @@
             out_specs=[pl.BlockSpec(shape, lambda i, s: (0, 0)) for shape in shapes],
         ),
         out_shape=[jax.ShapeDtypeStruct(shape, F32) for shape in shapes],
-        compiler_params=pltpu.CompilerParams(vmem_limit_bytes=VMEM),
+        compiler_params=pltpu.CompilerParams(vmem_limit_bytes=VMEM_LESS),
         cost_estimate=COST,
     )(side, near, far)
 
@@ -648,11 +659,9 @@
     def of_core(values, which):
         return lax.dynamic_slice_in_dim(values, which * half_rows, half_rows, 0)
 
-    second_in, cot_turned, stats, hidden_sent = second(
-        at_core, hidden_in, cotangent, ln2_gain, ln2_bias
-    )
+    second_in, stats, hidden_sent = second(at_core, hidden_in, ln2_gain, ln2_bias)
     hidden_pair = lax.all_gather(hidden_sent, "zl")
-    act_low, slope, down_grad = feed(second_in, cot_turned, fc1_weight, fc1_bias)
+    act_low, slope, down_grad = feed(second_in, cotangent, fc1_weight, fc1_bias)
     down_sum = after(lax.psum_scatter(down_grad, ("x", "y"), scatter_dimension=0, tiled=True))
     _, cotangent, hidden_in = after((down_grad, cotangent, hidden_in))
 
@@ -665,8 +674,8 @@
     own_marks = marks.reshape(2, TOK)
 
     def own_step(hidden_in, cotangent, act_low, slope):
-        first_in, first_turned, second_turned = norm_call(
-            first_kernel, 256, (hidden_in,), 1, 2, params
+        first_in, first_turned, second_turned, cot_turned = norm_call(
+            first_kernel, 256, (hidden_in, cotangent), 1, 3, params
         )
         projected = project(own_place, 2, first_in, qkv_weight, qkv_bias, own_marks)
         mixed_low, grad_packed = attend(
@@ -674,11 +683,12 @@
         )
         grad_up = feed_back(cotangent, fc2_weight, slope)
         branches = branch_halves(at_core, mixed_low, act_low, dense_weight, fc2_weight)
-        return first_turned, second_turned, mixed_low, grad_packed, grad_up, *branches
+        return first_turned, second_turned, cot_turned, mixed_low, grad_packed, grad_up, *branches
 
     (
         first_turned,
         second_turned,
+        cot_turned,
         mixed_low,
         grad_packed,
         grad_up,
@@ -694,9 +704,10 @@
     first_far_in, second_far_in, first_turned, second_turned = first_far(
         hidden_got, hidden_too, params, (first_turned, second_turned)
     )
-    second_far_in, branch_too = after((second_far_in, branch_too))
-    branch = lax.psum(branch + branch_too, "zh")
-    slope_side = slope_far(at_side, second_far_in, fc1_weight, fc1_bias)
+    slope_side, branch = slope_far(
+        at_side, second_far_in, fc1_weight, fc1_bias, branch, branch_too
+    )
+    branch = lax.psum(branch, "zh")
     marks_got = cot_got[half_rows, : 2 * TOK].reshape(2, 2, half_rows)
     marks_far = jnp.where(core == 0, marks_got, marks_got[:, ::-1]).reshape(2, TOK)
     projected_far = project(far_place, 1, first_far_in, qkv_weight, qkv_bias, marks_far)

time: 286 us -> 283 us (0.990)
  other arithmetic: 19.1 us -> 13.3 us
    ppermute x12, waiting for transfers between devices: 45.8 us -> 50.6 us  [send(): return lax.ppermute(value, axis, [(i, (i + step) % n) for i in range(n)])]
    pallas_call x1, Pallas kernels: 6.48 us -> 10.1 us  [slope_far(): pl.pallas_call(slope_far_kernel, grid_spec=pltpu.PrefetchScalarGridSpec(n...]
    add x1 -> x0, other arithmetic: 3.5 us -> none  [body(): branch = lax.psum(branch + branch_too, 'zh')]
  transfers between devices with their start and end apart: 21 -> 21, of which waited for: 13 -> 13; matrix products, arithmetic and copies ran while one was open for 10% -> 7% of each run, Pallas kernels for 46% -> 47%
where the time goes in v4:
time: 283 us; the launch traced here: 282 us
  Pallas kernels  139 us (49%)
  waiting for transfers between devices  80.2 us (28%)
  starting transfers between devices  22.6 us (8%)
  between operations  15.9 us (6%)
  other arithmetic  13.3 us (5%)
  local copies, waits for them, and re-layouts  11.8 us (4%)
    ppermute x12, waiting for transfers between devices, send(): return lax.ppermute(value, axis, [(i, (i + step) % n) for i in range(n)])  50.6 us
    pallas_call x2, Pallas kernels, halves_call(): pl.pallas_call(kernel, grid_spec=pltpu.PrefetchScalarGridSpec(num_scalar_...  24.2 us
    ppermute x4, waiting for transfers between devices, swap(): return lax.ppermute(value, axis, [(i, i ^ bit) for i in range(SIZES[axis])])  17.2 us
    pallas_call x1, Pallas kernels, joint(): pl.pallas_call(joint_kernel, grid_spec=pltpu.PrefetchScalarGridSpec(num_s...  16.7 us
    pallas_call x1, Pallas kernels, feed(): pl.pallas_call(feed_kernel, grid=(units // width,), in_specs=[whole((TOK,...  16 us
    pallas_call x2, Pallas kernels, project(): pl.pallas_call(project_kernel, grid_spec=pltpu.PrefetchScalarGridSpec(num...  14.5 us
    pallas_call x2, Pallas kernels, attend(): pl.pallas_call(attend_kernel, grid_spec=pltpu.PrefetchScalarGridSpec(num_...  14 us
    pallas_call x1, Pallas kernels, slope_far(): pl.pallas_call(slope_far_kernel, grid_spec=pltpu.PrefetchScalarGridSpec(n...  10.1 us
  transfers between devices with their start and end apart: 21, of which 13 were waited for; matrix products, arithmetic and copies ran while one was open for 7% of the time, Pallas kernels for 47%

profile of v4, /device:TPU:0, one launch (start us, length us, event | category | flops | bytes accessed | tf_op | source)
XLA Modules:
  0.0 282.3 jit_solution(5547726252974489015)
XLA Ops:
  8.1 4.4 %shard_map.281 = (bf16[512,2048]{1,0:T(8,128)(2,1)}, f32[512,128]{1,0:T(8,128)}, f32[256,2048]{1,0:T(8,128)}) custom-call(s32[1]{0:T(128)} %bitcast.8.core.half, bf16[512,2048]{1,0:T(8,128)(2,1)} %hidden.4, f32[1,2048]{1,0:T(1,128)} %bitcast.51, f32[1,2048]{1,0:T(1,128)} %bitcast.60), custom_call_target="tpu_custom_call" | custom-call | flops 1000000 | bytes 1000000 | tf_op jit(solution)/shard_map/pallas_call | solution.py:85
  12.5 16.0 %shard_map.282 = (bf16[512,2048]{1,0:T(8,128)(2,1)}, f32[512,2048]{1,0:T(8,128)}, f32[16,128,2048]{2,1,0:T(8,128)}) custom-call(bf16[512,2048]{1,0:T(8,128)(2,1)} %get-tuple-element.193.second, bf16[512,2048]{1,0:T(8,128)(2,1)S(1)} %copy-done.4, bf16[2048,2048]{1,0:T(8,128)(2,1)} %up.1, f32[4,4,128]{2,1,0:T(4,128)} %bitcast.72), custom_call_target="tpu_custom_call" | custom-call | flops 1000000 | bytes 1000000 | tf_op jit(solution)/shard_map/pallas_call | solution.py:206
  31.2 4.2 %collective-permute-start.1 = (f32[264,2048]{1,0:T(8,128)}, f32[264,2048]{1,0:T(8,128)}, u32[]{:S(2)}, u32[]{:S(2)}) collective-permute-start(f32[264,2048]{1,0:T(8,128)} %select_maximum_fusion), channel_id=1, source_target_pairs={{0,66},{2,64},{64,2},{66,0},{1,67},{3,65},{65,3},{67,1},{4,70},{6,... | collective-permute-start | bytes 6488072 | tf_op jit(solution)/shard_map/ppermute | solution.py:672
  35.4 41.7 %conditional.1 = (bf16[16,2,64,1024]{3,2,1,0:T(8,128)(2,1)}, bf16[16,2,64,1024]{3,2,1,0:T(8,128)(2,1)}, bf16[16,2,64,1024]{3,2,1,0:T(8,128)(2,1)}, bf16[512,512]...) conditional(s32[]{:T(128)} %convert_element_type.33, ...), branch_computations={%region_0.0_spmd, %region_1.2_spmd} | conditional | flops 5000000 | bytes 30165984 | solution.py:697
  35.4 9.4 %branch_0_fun.8 = bf16[512,2048]{1,0:T(8,128)(2,1)} custom-call(bf16[512,2048]{1,0:T(8,128)(2,1)S(1)} %get-tuple-element.61.cot.refs_0_, bf16[2048,2048]{1,0:T(8,128)(2,1)} %get-tuple-element.83.weight.down, f32[512,2048]{1,0:T(8,128)} %get-tuple-element.84.slope), custom_call_target="tpu_custom_call" | custom-call | flops 1000000 | bytes 1000000 | tf_op jit(solution)/shard_map/cond/branch_0_fun/pallas_call | solution.py:233
  44.9 4.6 %branch_0_fun.5 = (bf16[512,2048]{1,0:T(8,128)(2,1)}, bf16[16,2,64,1024]{3,2,1,0:T(8,128)(2,1)}, bf16[16,2,64,1024]{3,2,1,0:T(8,128)(2,1)}, bf16[16,2,64,1024]{3,2,1,0:T(8,128)(2,1)}) custom-call(bf16[512,2048]{1,0:T(8,128)(2,1)S(1)} %copy-done.7, bf16[512,2048]{1,0:T(8,128)(2,1)S(1)} %get-tuple-element.61.cot.refs_0_, f32[1,2048]{1,0:T(1,128)S(1)} %bitcast.58, ...), custom_call_target="tpu_custom_call" | custom-call | flops 1000000 | bytes 1000000 | tf_op jit(solution)/shard_map/cond/branch_0_fun/pallas_call | solution.py:144
  50.0 8.5 %branch_0_fun.6 = (bf16[512,512]{1,0:T(8,128)(2,1)}, bf16[512,512]{1,0:T(8,128)(2,1)}, bf16[512,512]{1,0:T(8,128)(2,1)}, f32[512,128]{1,0:T(8,128)}, f32[512,128]{1,0:T(8,128)}, /*index=5*/f32[512,128]{1,0:T(8,128)}) custom-call(s32[2]{0:T(128)} %broadcast_1_place.0.place, bf16[512,2048]{1,0:T(8,128)(2,1)} %get-tuple-element.69.first, ...), custom_call_target="tpu_custom_call" | custom-call | flops 1000000 | bytes 1000000 | tf_op jit(solution)/shard_map/cond/branch_0_fun/pallas_call | solution.py:377
  58.4 9.0 %branch_0_fun.7 = (bf16[512,512]{1,0:T(8,128)(2,1)}, bf16[512,1536]{1,0:T(8,128)(2,1)}) custom-call(s32[2]{0:T(128)} %broadcast_1_place.0.place, bf16[512,512]{1,0:T(8,128)(2,1)} %get-tuple-element.74.queries, bf16[512,512]{1,0:T(8,128)(2,1)} %get-tuple-element.75.keys, bf16[512,512]{1,0:T(8,128)(2,1)} %get-tuple-element.76.values, ...), custom_call_target="tpu_custom_call" | custom-call | flops 1000000 | bytes 1000000 | tf_op jit(solution)/shard_map/cond/branch_0_fun/pallas_call | solution.py:431
  67.4 9.6 %branch_0_fun.9 = (f32[256,2048]{1,0:T(8,128)}, f32[256,2048]{1,0:T(8,128)}) custom-call(s32[1]{0:T(128)} %get-tuple-element.85.core, bf16[512,512]{1,0:T(8,128)(2,1)} %get-tuple-element.305.mixed, bf16[512,2048]{1,0:T(8,128)(2,1)S(1)} %copy-done.14, bf16[512,2048]{1,0:T(8,128)(2,1)S(1)} %copy-done.10, bf16[2048,2048]{1,0:T(8,128)(2,1)} %get-tuple-element.83.weight.down), custom_call_target="tpu_custom_call" | custom-call | flops 1000000 | bytes 1000000 | tf_op jit(solution)/shard_map/cond/branch_0_fun/pallas_call | solution.py:479
  79.6 2.9 %collective-permute-done.1.near = f32[264,2048]{1,0:T(8,128)} collective-permute-done((f32[264,2048]{1,0:T(8,128)}, f32[264,2048]{1,0:T(8,128)}, u32[]{:S(2)}, u32[]{:S(2)}) %collective-permute-start.1) | collective-permute-done | bytes 2162720 | tf_op jit(solution)/shard_map/ppermute | solution.py:672
  82.5 2.8 collective-permute-done.other
  86.7 6.7 %shard_map.283 = (bf16[512,2048]{1,0:T(8,128)(2,1)}, bf16[512,2048]{1,0:T(8,128)(2,1)}, bf16[16,2,64,1024]{3,2,1,0:T(8,128)(2,1)S(1)}, bf16[16,2,64,1024]{3,2,1,0:T(8,128)(2,1)}) custom-call(f32[1,256,2048]{2,1,0:T(8,128)} %copy-done.16, f32[1,256,2048]{2,1,0:T(8,128)} %copy-done.17, ...), custom_call_target="tpu_custom_call", output_to_operand_aliasing={{2}: (6, {}), {3}: (7, {})} | custom-call | flops 1000000 | bytes 1000000 | tf_op jit(solution)/shard_map/pallas_call | solution.py:160
  93.4 10.1 %shard_map.284 = (f32[512,1024]{1,0:T(8,128)}, f32[256,2048]{1,0:T(8,128)}) custom-call(s32[1]{0:T(128)} %bitcast.9.side, bf16[512,2048]{1,0:T(8,128)(2,1)} %get-tuple-element.206.second, bf16[2048,2048]{1,0:T(8,128)(2,1)} %up.1, f32[4,4,128]{2,1,0:T(4,128)} %bitcast.73, f32[256,2048]{1,0:T(8,128)} %get-tuple-element.207.sums, ...), custom_call_target="tpu_custom_call" | custom-call | flops 1000000 | bytes 1000000 | tf_op jit(solution)/shard_map/pallas_call | solution.py:302
  106.0 6.0 %shard_map.286 = (bf16[512,256]{1,0:T(8,128)(2,1)}, bf16[512,256]{1,0:T(8,128)(2,1)}, bf16[512,256]{1,0:T(8,128)(2,1)}, f32[512,128]{1,0:T(8,128)}, f32[512,128]{1,0:T(8,128)}, /*index=5*/f32[512,128]{1,0:T(8,128)}) custom-call(s32[2]{0:T(128)} %pad_add_fusion.place, bf16[512,2048]{1,0:T(8,128)(2,1)} %get-tuple-element.216.first, bf16[2048,1536]{1,0:T(8,128)(2,1)} %qkv.1, ...), custom_call_target="tpu_custom_call" | custom-call | flops 1000000 | bytes 1000000 | tf_op jit(solution)/shard_map/pallas_call | solution.py:377
  112.0 8.4 %shard_map.285 = (bf16[512,1024]{1,0:T(8,128)(2,1)}, bf16[512,256]{1,0:T(8,128)(2,1)}, bf16[16,2,64,1024]{3,2,1,0:T(8,128)(2,1)}) custom-call(s32[1]{0:T(128)} %bitcast.9.side, f32[264,2048]{1,0:T(8,128)} %collective-permute-done.1.near, f32[264,2048]{1,0:T(8,128)} %collective-permute-done.2.other, ...), custom_call_target="tpu_custom_call", output_to_operand_aliasing={{2}: (6, {})} | custom-call | flops 1000000 | bytes 1000000 | tf_op jit(solution)/shard_map/pallas_call | solution.py:261
  120.4 5.0 %shard_map.287 = (bf16[512,256]{1,0:T(8,128)(2,1)}, bf16[512,768]{1,0:T(8,128)(2,1)}) custom-call(s32[2]{0:T(128)} %pad_add_fusion.place, bf16[512,256]{1,0:T(8,128)(2,1)} %get-tuple-element.217.queries, bf16[512,256]{1,0:T(8,128)(2,1)} %get-tuple-element.218.keys, bf16[512,256]{1,0:T(8,128)(2,1)} %get-tuple-element.219.values, ...), custom_call_target="tpu_custom_call" | custom-call | flops 1000000 | bytes 1000000 | tf_op jit(solution)/shard_map/pallas_call | solution.py:431
  125.3 16.7 %shard_map.288 = f32[16,128,2048]{2,1,0:T(8,128)} custom-call(s32[1]{0:T(128)} %bitcast.9.side, bf16[16,2,64,1024]{3,2,1,0:T(8,128)(2,1)} %get-tuple-element.204.refs_0_, bf16[16,2,64,1024]{3,2,1,0:T(8,128)(2,1)} %get-tuple-element.211.refs_1_, bf16[16,2,64,1024]{3,2,1,0:T(8,128)(2,1)} %copy-done.13, bf16[512,2048]{1,0:T(8,128)(2,1)} %get-tuple-element.230.refs_3_.up_grad, ...), custom_call_target="tpu_custom_call" | custom-call | flops 1000000 | bytes 1000000 | tf_op jit(solution)/shard_map/pallas_call | solution.py:582
  142.1 14.6 %shard_map.289 = (f32[256,2048]{1,0:T(8,128)}, f32[256,2048]{1,0:T(8,128)}, f32[8,2048]{1,0:T(8,128)}) custom-call(s32[1]{0:T(128)} %bitcast.8.core.half, bf16[512,1536]{1,0:T(8,128)(2,1)} %get-tuple-element.229.refs_7_.packed, bf16[512,2048]{1,0:T(8,128)(2,1)} %get-tuple-element.230.refs_3_.up_grad, bf16[2048,1536]{1,0:T(8,128)(2,1)} %qkv.1, ...), custom_call_target="tpu_custom_call" | custom-call | flops 1000000 | bytes 1000000 | tf_op jit(solution)/shard_map/pallas_call | solution.py:479
  156.8 4.3 %collective-permute-done.11 = f32[256,2048]{1,0:T(8,128)S(1)} collective-permute-done((f32[256,2048]{1,0:T(8,128)}, f32[256,2048]{1,0:T(8,128)S(1)}, u32[]{:S(2)}, u32[]{:S(2)}) %collective-permute-start.11) | collective-permute-done | bytes 2097184 | tf_op jit(solution)/shard_map/ppermute | solution.py:27
  161.1 3.3 %add.81 = f32[256,2048]{1,0:T(8,128)} add(f32[256,2048]{1,0:T(8,128)} %get-tuple-element.235, f32[256,2048]{1,0:T(8,128)S(1)} %collective-permute-done.11) | non-fusion elementwise | flops 524288 | bytes 6291456 | tf_op jit(solution)/shard_map/add | solution.py:734
  173.7 4.6 %collective-permute-done.4 = f32[32,512]{1,0:T(8,128)S(1)} collective-permute-done((f32[32,512]{1,0:T(8,128)S(1)}, f32[32,512]{1,0:T(8,128)S(1)}, u32[]{:S(2)}, u32[]{:S(2)}) %collective-permute-start.4) | collective-permute-done | bytes 65568 | tf_op jit(solution)/shard_map/ppermute | solution.py:31
  178.4 2.8 %collective-permute-start.5 = (f32[32,512]{1,0:T(8,128)S(1)}, f32[32,512]{1,0:T(8,128)S(1)}, u32[]{:S(2)}, u32[]{:S(2)}) collective-permute-start(f32[32,512]{1,0:T(8,128)S(1)} %add.69), channel_id=1, source_target_pairs={{0,32},{16,48},{32,0},{48,16},{1,33},{17,49},{33,1},{49,17},{2,34}... | collective-permute-start | bytes 196616 | tf_op jit(solution)/shard_map/ppermute | solution.py:31
  181.8 3.9 %collective-permute-done.5 = f32[32,512]{1,0:T(8,128)S(1)} collective-permute-done((f32[32,512]{1,0:T(8,128)S(1)}, f32[32,512]{1,0:T(8,128)S(1)}, u32[]{:S(2)}, u32[]{:S(2)}) %collective-permute-start.5) | collective-permute-done | bytes 65568 | tf_op jit(solution)/shard_map/ppermute | solution.py:31
  187.2 4.2 %collective-permute-done.6 = f32[32,512]{1,0:T(8,128)S(1)} collective-permute-done((f32[32,512]{1,0:T(8,128)S(1)}, f32[32,512]{1,0:T(8,128)S(1)}, u32[]{:S(2)}, u32[]{:S(2)}) %collective-permute-start.6) | collective-permute-done | bytes 65568 | tf_op jit(solution)/shard_map/ppermute | solution.py:31
  191.4 2.8 %collective-permute-start.7 = (f32[32,512]{1,0:T(8,128)S(1)}, f32[32,512]{1,0:T(8,128)S(1)}, u32[]{:S(2)}, u32[]{:S(2)}) collective-permute-start(f32[32,512]{1,0:T(8,128)S(1)} %add.71), channel_id=1, source_target_pairs={{0,8},{4,12},{8,0},{12,4},{1,9},{5,13},{9,1},{13,5},{2,10},{6,14},... | collective-permute-start | bytes 196616 | tf_op jit(solution)/shard_map/ppermute | solution.py:31
  194.3 4.4 %collective-permute-done.7 = f32[32,512]{1,0:T(8,128)S(1)} collective-permute-done((f32[32,512]{1,0:T(8,128)S(1)}, f32[32,512]{1,0:T(8,128)S(1)}, u32[]{:S(2)}, u32[]{:S(2)}) %collective-permute-start.7) | collective-permute-done | bytes 65568 | tf_op jit(solution)/shard_map/ppermute | solution.py:31
  199.1 28.8 %collective-permute-done.8 = f32[1,512]{1,0:T(1,128)S(1)} collective-permute-done((f32[1,512]{1,0:T(1,128)S(1)}, f32[1,512]{1,0:T(1,128)S(1)}, u32[]{:S(2)}, u32[]{:S(2)}) %collective-permute-start.8) | collective-permute-done | bytes 2080 | tf_op jit(solution)/shard_map/ppermute | solution.py:27
  229.2 2.9 %collective-permute-start.10 = (f32[256]{0:T(256)S(1)}, f32[256]{0:T(256)S(1)}, u32[]{:S(2)}, u32[]{:S(2)}) collective-permute-start(f32[256]{0:T(256)S(1)} %add.79), channel_id=1, source_target_pairs={{0,2},{2,0},{1,3},{3,1},{4,6},{6,4},{5,7},{7,5},{8,10},{10,8},{9,1... | collective-permute-start | bytes 3080 | tf_op jit(solution)/shard_map/ppermute | solution.py:27
  239.9 4.4 %shard_map.290 = (f32[512,2048]{1,0:T(8,128)}, f32[512,2048]{1,0:T(8,128)}) custom-call(s32[1]{0:T(128)} %bitcast.8.core.half, f32[256,2048]{1,0:T(8,128)} %all-reduce.5.cloned.1.call-done.branch, f32[256,2048]{1,0:T(8,128)S(1)} %add.83.combined, bf16[512,2048]{1,0:T(8,128)(2,1)} %hidden.4, bf16[512,2048]{1,0:T(8,128)(2,1)} %cot.3, f32[512,128]{1,0:T(8,128)S(1)} %copy-done, ...), custom_call_target="tpu_custom_call" | custom-call | flops 1000000 | bytes 1000000 | tf_op jit(solution)/shard_map/pallas_call | solution.py:529
  245.3 4.1 %shard_map.291 = (f32[512,2048]{1,0:T(8,128)}, f32[512,2048]{1,0:T(8,128)}) custom-call(s32[1]{0:T(128)S(6)} %sub.4.half, f32[256,2048]{1,0:T(8,128)} %collective-permute-done.14.branch, f32[256,2048]{1,0:T(8,128)} %collective-permute-done.15.combined, bf16[512,2048]{1,0:T(8,128)(2,1)S(1)} %copy-done.6, ...), custom_call_target="tpu_custom_call", output_to_operand_aliasing={{0}: (8, {}), {1}: (9, {})} | custom-call | flops 1000000 | bytes 1000000 | tf_op jit(solution)/shard_map/pallas_call | solution.py:529
  249.4 9.4 %reduce-scatter.9.cloned.1.call-done.near = f32[1,128,2048]{2,1,0:T(8,128)} async-done(((f32[16,128,2048]{2,1,0:T(8,128)}), f32[1,128,2048]{2,1,0:T(8,128)}) %reduce-scatter.9.cloned.1.call-update) | async-done | bytes 1048592 | tf_op jit(solution)/shard_map/optimization_barrier | solution.py:776
  263.0 10.3 %collective-permute-done.16.far = f32[64,2048]{1,0:T(8,128)S(1)} collective-permute-done((f32[64,2048]{1,0:T(8,128)S(1)}, f32[64,2048]{1,0:T(8,128)S(1)}, u32[]{:S(2)}, u32[]{:S(2)}) %collective-permute-start.16) | collective-permute-done | bytes 524320 | tf_op jit(solution)/shard_map/ppermute | solution.py:27
  (137 shorter events, 37.2 us)
Async XLA Ops:
  8.0 69.1 %all-gather.3.cloned.1.call-start = ((), (), s32[]{:S(2)}) async-start(), calls=%async_computation.3 | async-start | bytes 6291456 | tf_op jit(solution)/shard_map/all_gather | solution.py:663
  12.5 129.6 %reduce-scatter.7.cloned.1.call-start = ((), (), s32[]{:S(2)}) async-start(), calls=%async_computation.4 | async-start | bytes 17825792
  28.6 205.7 %all-reduce.5.cloned.1.call-start = ((), (), s32[]{:S(2)}) async-start(), calls=%async_computation.2 | async-start | bytes 4194304 | tf_op jit(solution)/shard_map/psum | solution.py:710
  31.2 51.4 %collective-permute-start.1 = (f32[264,2048]{1,0:T(8,128)}, f32[264,2048]{1,0:T(8,128)}, u32[]{:S(2)}, u32[]{:S(2)}) collective-permute-start(f32[264,2048]{1,0:T(8,128)} %select_maximum_fusion), channel_id=1, source_target_pairs={{0,66},{2,64},{64,2},{66,0},{1,67},{3,65},{65,3},{67,1},{4,70},{6,... | collective-permute-start | bytes 6488072 | tf_op jit(solution)/shard_map/ppermute | solution.py:672
  35.4 9.4 %copy-start.7 = (bf16[512,2048]{1,0:T(8,128)(2,1)S(1)}, bf16[512,2048]{1,0:T(8,128)(2,1)}, u32[]{:S(2)}) copy-start(bf16[512,2048]{1,0:T(8,128)(2,1)} %get-tuple-element.60.hidden) | copy-start | bytes 6291460 | tf_op jit(solution)/shard_map/cond
  50.0 8.5 %copy-start.10 = (bf16[512,2048]{1,0:T(8,128)(2,1)S(1)}, bf16[512,2048]{1,0:T(8,128)(2,1)}, u32[]{:S(2)}) copy-start(bf16[512,2048]{1,0:T(8,128)(2,1)} %get-tuple-element.80.refs_1_.dense) | copy-start | bytes 6291460 | tf_op jit(solution)/shard_map/cond
  58.4 9.0 %copy-start.14 = (bf16[512,2048]{1,0:T(8,128)(2,1)S(1)}, bf16[512,2048]{1,0:T(8,128)(2,1)}, u32[]{:S(2)}) copy-start(bf16[512,2048]{1,0:T(8,128)(2,1)} %get-tuple-element.86.act) | copy-start | bytes 6291460 | tf_op jit(solution)/shard_map/cond
  77.1 9.7 %copy-start.12 = (bf16[16,2,64,1024]{3,2,1,0:T(8,128)(2,1)S(1)}, bf16[16,2,64,1024]{3,2,1,0:T(8,128)(2,1)}, u32[]{:S(2)}) copy-start(bf16[16,2,64,1024]{3,2,1,0:T(8,128)(2,1)} %get-tuple-element.202.refs_0_) | copy-start | bytes 12582916
  79.0 6.5 %copy-start.16 = (f32[1,256,2048]{2,1,0:T(8,128)}, f32[1,256,2048]{2,1,0:T(8,128)S(1)}, u32[]{:S(2)}) copy-start(f32[1,256,2048]{2,1,0:T(8,128)S(1)} %constant_dynamic-slice_fusion.1.near) | copy-start | bytes 6291460
  79.0 6.3 %collective-permute-start = (f32[1,256,2048]{2,1,0:T(8,128)S(1)}, f32[1,256,2048]{2,1,0:T(8,128)S(1)}, u32[]{:S(2)}, u32[]{:S(2)}) collective-permute-start(f32[1,256,2048]{2,1,0:T(8,128)S(1)} %constant_dynamic-slice_fusion.1.near), channel_id=1, source_target_pairs={{0,1},{1,0},{2,3},{3,2},{4,5},{5,4},{6,7},{7,6},{8,9},{9,8},{10,11... | collective-permute-start | bytes 6291464 | tf_op jit(solution)/shard_map/ppermute | solution.py:27
  79.1 14.3 %collective-permute-start.3 = (f32[256,2048]{1,0:T(8,128)}, f32[256,2048]{1,0:T(8,128)}, u32[]{:S(2)}, u32[]{:S(2)}) collective-permute-start(f32[256,2048]{1,0:T(8,128)} %get-tuple-element.208), channel_id=1, source_target_pairs={{0,1},{1,0},{2,3},{3,2},{4,5},{5,4},{6,7},{7,6},{8,9},{9,8},{10,11... | collective-permute-start | bytes 6291464 | tf_op jit(solution)/shard_map/ppermute | solution.py:27
  85.3 26.6 %collective-permute-start.2 = (f32[264,2048]{1,0:T(8,128)}, f32[264,2048]{1,0:T(8,128)}, u32[]{:S(2)}, u32[]{:S(2)}) collective-permute-start(f32[264,2048]{1,0:T(8,128)} %collective-permute-done.1.near), channel_id=1, source_target_pairs={{0,1},{1,0},{2,3},{3,2},{4,5},{5,4},{6,7},{7,6},{8,9},{9,8},{10,11... | collective-permute-start | bytes 6488072 | tf_op jit(solution)/shard_map/ppermute | solution.py:27
  93.4 10.1 %copy-start.13 = (bf16[16,2,64,1024]{3,2,1,0:T(8,128)(2,1)}, bf16[16,2,64,1024]{3,2,1,0:T(8,128)(2,1)S(1)}, u32[]{:S(2)}) copy-start(bf16[16,2,64,1024]{3,2,1,0:T(8,128)(2,1)S(1)} %get-tuple-element.212.refs_2_) | copy-start | bytes 12582916
  103.6 155.2 %reduce-scatter.9.cloned.1.call-start = ((), (), s32[]{:S(2)}) async-start(), calls=%async_computation.5 | async-start | bytes 17825792
  106.0 6.0 %copy-start.9 = (bf16[512,2048]{1,0:T(8,128)(2,1)S(1)}, bf16[512,2048]{1,0:T(8,128)(2,1)}, u32[]{:S(2)}) copy-start(bf16[512,2048]{1,0:T(8,128)(2,1)} %dense.1) | copy-start | bytes 6291460
  156.7 4.4 %collective-permute-start.11 = (f32[256,2048]{1,0:T(8,128)}, f32[256,2048]{1,0:T(8,128)S(1)}, u32[]{:S(2)}, u32[]{:S(2)}) collective-permute-start(f32[256,2048]{1,0:T(8,128)} %get-tuple-element.236), channel_id=1, source_target_pairs={{0,1},{1,0},{2,3},{3,2},{4,5},{5,4},{6,7},{7,6},{8,9},{9,8},{10,11... | collective-permute-start | bytes 6291464 | tf_op jit(solution)/shard_map/ppermute | solution.py:27
  164.3 70.8 %collective-permute-start.12 = (f32[256,2048]{1,0:T(8,128)}, f32[256,2048]{1,0:T(8,128)}, u32[]{:S(2)}, u32[]{:S(2)}) collective-permute-start(f32[256,2048]{1,0:T(8,128)} %add.81), channel_id=1, source_target_pairs={{0,2},{2,0},{1,3},{3,1},{4,6},{6,4},{5,7},{7,5},{8,10},{10,8},{9,1... | collective-permute-start | bytes 6291464 | tf_op jit(solution)/shard_map/ppermute | solution.py:27
  169.5 11.7 %copy-start.18 = (f32[1,128,2048]{2,1,0:T(8,128)S(1)}, f32[1,128,2048]{2,1,0:T(8,128)}, u32[]{:S(2)}) copy-start(f32[1,128,2048]{2,1,0:T(8,128)} %reduce-scatter.7.cloned.1.call-done) | copy-start | bytes 3145732
  172.4 5.9 %collective-permute-start.4 = (f32[32,512]{1,0:T(8,128)S(1)}, f32[32,512]{1,0:T(8,128)S(1)}, u32[]{:S(2)}, u32[]{:S(2)}) collective-permute-start(f32[32,512]{1,0:T(8,128)S(1)} %concatenate.27), channel_id=1, source_target_pairs={{0,16},{16,0},{32,48},{48,32},{1,17},{17,1},{33,49},{49,33},{2,18}... | collective-permute-start | bytes 196616 | tf_op jit(solution)/shard_map/ppermute | solution.py:31
  178.4 7.4 %collective-permute-start.5 = (f32[32,512]{1,0:T(8,128)S(1)}, f32[32,512]{1,0:T(8,128)S(1)}, u32[]{:S(2)}, u32[]{:S(2)}) collective-permute-start(f32[32,512]{1,0:T(8,128)S(1)} %add.69), channel_id=1, source_target_pairs={{0,32},{16,48},{32,0},{48,16},{1,33},{17,49},{33,1},{49,17},{2,34}... | collective-permute-start | bytes 196616 | tf_op jit(solution)/shard_map/ppermute | solution.py:31
  181.2 53.1 %collective-permute-start.13 = (f32[64,2048]{1,0:T(8,128)S(1)}, f32[64,2048]{1,0:T(8,128)S(1)}, u32[]{:S(2)}, u32[]{:S(2)}) collective-permute-start(f32[64,2048]{1,0:T(8,128)S(1)} %dynamic-slice_bitcast_fusion.1), channel_id=1, source_target_pairs={{0,64},{64,0},{1,65},{65,1},{2,66},{66,2},{3,67},{67,3},{4,68},{68... | collective-permute-start | bytes 1572872 | tf_op jit(solution)/shard_map/ppermute | solution.py:27
  185.8 5.6 %collective-permute-start.6 = (f32[32,512]{1,0:T(8,128)S(1)}, f32[32,512]{1,0:T(8,128)S(1)}, u32[]{:S(2)}, u32[]{:S(2)}) collective-permute-start(f32[32,512]{1,0:T(8,128)S(1)} %add.70), channel_id=1, source_target_pairs={{0,4},{4,0},{8,12},{12,8},{1,5},{5,1},{9,13},{13,9},{2,6},{6,2},{1... | collective-permute-start | bytes 196616 | tf_op jit(solution)/shard_map/ppermute | solution.py:31
  191.4 7.2 %collective-permute-start.7 = (f32[32,512]{1,0:T(8,128)S(1)}, f32[32,512]{1,0:T(8,128)S(1)}, u32[]{:S(2)}, u32[]{:S(2)}) collective-permute-start(f32[32,512]{1,0:T(8,128)S(1)} %add.71), channel_id=1, source_target_pairs={{0,8},{4,12},{8,0},{12,4},{1,9},{5,13},{9,1},{13,5},{2,10},{6,14},... | collective-permute-start | bytes 196616 | tf_op jit(solution)/shard_map/ppermute | solution.py:31
  198.7 29.3 %collective-permute-start.8 = (f32[1,512]{1,0:T(1,128)S(1)}, f32[1,512]{1,0:T(1,128)S(1)}, u32[]{:S(2)}, u32[]{:S(2)}) collective-permute-start(f32[1,512]{1,0:T(1,128)S(1)} %constant_dynamic-slice_fusion), channel_id=1, source_target_pairs={{0,64},{64,0},{1,65},{65,1},{2,66},{66,2},{3,67},{67,3},{4,68},{68... | collective-permute-start | bytes 6152 | tf_op jit(solution)/shard_map/ppermute | solution.py:27
  228.0 1.2 collective-permute-start.9
  229.2 5.1 %collective-permute-start.10 = (f32[256]{0:T(256)S(1)}, f32[256]{0:T(256)S(1)}, u32[]{:S(2)}, u32[]{:S(2)}) collective-permute-start(f32[256]{0:T(256)S(1)} %add.79), channel_id=1, source_target_pairs={{0,2},{2,0},{1,3},{3,1},{4,6},{6,4},{5,7},{7,5},{8,10},{10,8},{9,1... | collective-permute-start | bytes 3080 | tf_op jit(solution)/shard_map/ppermute | solution.py:27
  237.7 6.6 %collective-permute-start.15 = (f32[256,2048]{1,0:T(8,128)S(1)}, f32[256,2048]{1,0:T(8,128)}, u32[]{:S(2)}, u32[]{:S(2)}) collective-permute-start(f32[256,2048]{1,0:T(8,128)S(1)} %add.83.combined), channel_id=1, source_target_pairs={{0,1},{1,0},{2,3},{3,2},{4,5},{5,4},{6,7},{7,6},{8,9},{9,8},{10,11... | collective-permute-start | bytes 6291464 | tf_op jit(solution)/shard_map/ppermute | solution.py:27
  237.8 7.5 %collective-permute-start.14 = (f32[256,2048]{1,0:T(8,128)}, f32[256,2048]{1,0:T(8,128)}, u32[]{:S(2)}, u32[]{:S(2)}) collective-permute-start(f32[256,2048]{1,0:T(8,128)} %all-reduce.5.cloned.1.call-done.branch), channel_id=1, source_target_pairs={{0,1},{1,0},{2,3},{3,2},{4,5},{5,4},{6,7},{7,6},{8,9},{9,8},{10,11... | collective-permute-start | bytes 6291464 | tf_op jit(solution)/shard_map/ppermute | solution.py:27
  239.1 35.3 %copy-start.30 = (f32[64]{0:T(128)}, f32[64]{0:T(128)S(1)}, u32[]{:S(2)}) copy-start(f32[64]{0:T(128)S(1)} %get-tuple-element.345) | copy-start | bytes 772
  245.3 16.9 %copy-start.20 = (f32[64,2048]{1,0:T(8,128)S(1)}, f32[64,2048]{1,0:T(8,128)}, u32[]{:S(2)}) copy-start(f32[64,2048]{1,0:T(8,128)} %copy-done.19) | copy-start | bytes 1572868
  258.8 14.6 %copy-start.1 = (f32[1,128,2048]{2,1,0:T(8,128)S(1)}, f32[1,128,2048]{2,1,0:T(8,128)}, u32[]{:S(2)}) copy-start(f32[1,128,2048]{2,1,0:T(8,128)} %reduce-scatter.9.cloned.1.call-done.near) | copy-start | bytes 3145732
  260.0 13.4 %collective-permute-start.16 = (f32[64,2048]{1,0:T(8,128)S(1)}, f32[64,2048]{1,0:T(8,128)S(1)}, u32[]{:S(2)}, u32[]{:S(2)}) collective-permute-start(f32[64,2048]{1,0:T(8,128)S(1)} %dynamic-slice_bitcast_fusion), channel_id=1, source_target_pairs={{0,64},{64,0},{1,65},{65,1},{2,66},{66,2},{3,67},{67,3},{4,68},{68... | collective-permute-start | bytes 1572872 | tf_op jit(solution)/shard_map/ppermute | solution.py:27
  (17 other events, 73.3 us)
Sparse Core Ops, SparseCore 0:
  12.6 61.7 all-gather.2
  103.7 74.3 all-reduce.4
Sparse Core Ops, SparseCore 1:
  28.7 112.9 reduce-scatter.6
  145.3 113.4 reduce-scatter.8

commit v5 on v3

--- a/solution.py
+++ b/solution.py
@@ -40,6 +40,7 @@
 
 
 VMEM = 56 * 1024 * 1024
+VMEM_LESS = 24 * 1024 * 1024
 COST = pl.CostEstimate(flops=1000000, bytes_accessed=1000000, transcendentals=0)
 
 
@@ -60,65 +61,37 @@
     average = jnp.mean(hidden, axis=-1, keepdims=True)
     centred = hidden - average
     inv_std = lax.rsqrt(jnp.mean(centred * centred, axis=-1, keepdims=True) + EPSILON)
-    return centred * inv_std, inv_std
-
-
-def second_kernel(core, hidden, cot, gain, shift, second_out, cot_turned, stats, sent):
-    rows = hidden[...].astype(F32)
-
-    @pl.when(pl.program_id(0) == core[0])
-    def _():
-        sent[...] = rows
-
-    average = jnp.mean(rows, axis=-1, keepdims=True)
-    centred = rows - average
-    inv_std = lax.rsqrt(jnp.mean(centred * centred, axis=-1, keepdims=True) + EPSILON)
-    second_out[...] = (centred * inv_std * gain[...] + shift[...]).astype(BF16)
-    put_turned(cot_turned, cot[...].astype(F32))
-    lane = lax.broadcasted_iota(jnp.int32, (rows.shape[0], 128), 1)
-    stats[...] = jnp.where(lane < 64, average, inv_std)
-
-
-def second(core, hidden, cot, gain, shift):
-    rows = TOK // 2
-    plain = pl.BlockSpec((rows, D), lambda i, s: (i, 0))
-    return pl.pallas_call(
-        second_kernel,
-        grid_spec=pltpu.PrefetchScalarGridSpec(
-            num_scalar_prefetch=1,
-            grid=(2,),
-            in_specs=[plain] * 2 + [whole((1, D))] * 2,
-            out_specs=[
-                plain,
-                pl.BlockSpec((16, 2, 64, rows), lambda i, s: (0, 0, 0, i)),
-                pl.BlockSpec((rows, 128), lambda i, s: (i, 0)),
-                pl.BlockSpec((rows, D), lambda i, s: (0, 0)),
-            ],
-        ),
-        out_shape=[
-            jax.ShapeDtypeStruct((TOK, D), BF16),
-            jax.ShapeDtypeStruct(TURNED, BF16),
-            jax.ShapeDtypeStruct((TOK, 128), F32),
-            jax.ShapeDtypeStruct((rows, D), F32),
-        ],
-        compiler_params=pltpu.CompilerParams(vmem_limit_bytes=VMEM),
-        cost_estimate=COST,
-    )(core, hidden, cot, gain.reshape(1, D), shift.reshape(1, D))
-
-
-def first_kernel(hidden, gain, shift, gain_two, shift_two, first_out, first_turned, second_turned):
-    normed, _ = normalise(hidden[...].astype(F32))
+    return centred * inv_std, average, inv_std
+
+
+def first_kernel(
+    hidden,
+    cot,
+    gain,
+    shift,
+    gain_two,
+    shift_two,
+    first_out,
+    first_turned,
+    second_turned,
+    cot_turned,
+    stats,
+):
+    normed, average, inv_std = normalise(hidden[...].astype(F32))
     first = normed * gain[...] + shift[...]
     first_out[...] = first.astype(BF16)
     put_turned(first_turned, first)
     put_turned(second_turned, normed * gain_two[...] + shift_two[...])
+    put_turned(cot_turned, cot[...].astype(F32))
+    lane = lax.broadcasted_iota(jnp.int32, (normed.shape[0], 128), 1)
+    stats[...] = jnp.where(lane < 64, average, inv_std)
 
 
 def first_far_kernel(near, other, gain, shift, gain_two, shift_two, *refs):
     first_out, second_out, first_turned, second_turned = refs[2:]
 
     def step(rows):
-        normed, _ = normalise(rows)
+        normed, _, _ = normalise(rows)
         first = normed * gain[...] + shift[...]
         second = normed * gain_two[...] + shift_two[...]
         first_out[...] = first.astype(BF16)
@@ -128,29 +101,32 @@
 
     @pl.when(pl.program_id(0) < 2)
     def _():
-        step(near[0])
+        step(near[...])
 
     @pl.when(pl.program_id(0) >= 2)
     def _():
-        step(other[0])
+        step(other[...])
 
 
 TURNED = (16, 2, 64, 2 * TOK)
 
 
-def norm_call(kernel, rows, n_rows, n_plain, n_turned, params):
+def first(hidden, cot, params):
+    rows = TOK // 2
     plain = pl.BlockSpec((rows, D), lambda i: (i, 0))
     return pl.pallas_call(
-        kernel,
-        grid=(TOK // rows,),
-        in_specs=[plain] * len(n_rows) + [whole((1, D))] * len(params),
-        out_specs=[plain] * n_plain
-        + [pl.BlockSpec((16, 2, 64, rows), lambda i: (0, 0, 0, i))] * n_turned,
-        out_shape=[jax.ShapeDtypeStruct((TOK, D), BF16)] * n_plain
-        + [jax.ShapeDtypeStruct(TURNED, BF16)] * n_turned,
-        compiler_params=pltpu.CompilerParams(vmem_limit_bytes=VMEM),
-        cost_estimate=COST,
-    )(*n_rows, *(p.reshape(1, D) for p in params))
+        first_kernel,
+        grid=(2,),
+        in_specs=[plain] * 2 + [whole((1, D))] * 4,
+        out_specs=[plain]
+        + [pl.BlockSpec((16, 2, 64, rows), lambda i: (0, 0, 0, i))] * 3
+        + [pl.BlockSpec((rows, 128), lambda i: (i, 0))],
+        out_shape=[jax.ShapeDtypeStruct((TOK, D), BF16)]
+        + [jax.ShapeDtypeStruct(TURNED, BF16)] * 3
+        + [jax.ShapeDtypeStruct((TOK, 128), F32)],
+        compiler_params=pltpu.CompilerParams(vmem_limit_bytes=VMEM),
+        cost_estimate=COST,
+    )(hidden, cot, *(p.reshape(1, D) for p in params))
 
 
 def first_far(near, other, params, held):
@@ -160,8 +136,8 @@
         first_far_kernel,
         grid=(TOK // rows,),
         in_specs=[
-            pl.BlockSpec((1, rows, D), lambda i: (0, lax.min(i, 1), 0)),
-            pl.BlockSpec((1, rows, D), lambda i: (0, lax.max(i - 2, 0), 0)),
+            pl.BlockSpec((rows, D), lambda i: (lax.min(i, 1), 0)),
+            pl.BlockSpec((rows, D), lambda i: (lax.max(i - 2, 0), 0)),
         ]
         + [whole((1, D))] * 4
         + [pl.BlockSpec(memory_space=pl.ANY)] * 2,
@@ -187,16 +163,26 @@
     return jnp.concatenate([block[i : i + 1, :] for i in range(block.shape[0])], axis=1)
 
 
-def feed_kernel(second, cot_turned, weight, bias, act_out, slope_out, down_grad):
+def feed_kernel(hidden, gain, shift, cot, weight, bias, act_out, slope_out, down_grad, second):
+    @pl.when(pl.program_id(0) == 0)
+    def _():
+        for start in (0, TOK // 2):
+            rows = slice(start, start + TOK // 2)
+            normed, _, _ = normalise(hidden[rows].astype(F32))
+            second[rows] = (normed * gain[...] + shift[...]).astype(BF16)
+
     upward = plain_dot(second[...], weight[...]) + as_row(bias[0])
     below = phi(upward)
     act = (upward * below).astype(BF16)
     act_out[...] = act
     slope_out[...] = gelu_slope(upward, below)
-    down_grad[...] = plain_dot(cot_turned[...].reshape(D, TOK), act).reshape(16, 128, -1)
-
-
-def feed(second, cot_turned, weight, bias):
+    total = lax.dot_general(cot[...], act, (((0,), (0,)), ((), ())), preferred_element_type=F32)
+    for z in range(2):
+        rows = total[z * 1024 : z * 1024 + 1024]
+        down_grad[:, z * 64 : z * 64 + 64] = rows.reshape(16, 64, -1)
+
+
+def feed(hidden, gain, shift, cot, weight, bias):
     units, width = weight.shape[1], 512
     column = pl.BlockSpec((TOK, width), lambda j: (0, j))
     return pl.pallas_call(
@@ -204,7 +190,9 @@
         grid=(units // width,),
         in_specs=[
             whole((TOK, D)),
-            whole((16, 2, 64, TOK)),
+            whole((1, D)),
+            whole((1, D)),
+            whole((TOK, D)),
             pl.BlockSpec((D, width), lambda j: (0, j)),
             pl.BlockSpec((1, width // 128, 128), lambda j: (j, 0, 0)),
         ],
@@ -214,9 +202,17 @@
             jax.ShapeDtypeStruct((TOK, units), F32),
             jax.ShapeDtypeStruct((16, 128, units), F32),
         ],
-        compiler_params=pltpu.CompilerParams(vmem_limit_bytes=VMEM),
-        cost_estimate=COST,
-    )(second, cot_turned, weight, bias.reshape(-1, width // 128, 128))
+        scratch_shapes=[pltpu.VMEM((TOK, D), BF16)],
+        compiler_params=pltpu.CompilerParams(vmem_limit_bytes=VMEM),
+        cost_estimate=COST,
+    )(
+        hidden,
+        gain.reshape(1, D),
+        shift.reshape(1, D),
+        cot,
+        weight,
+        bias.reshape(-1, width // 128, 128),
+    )
 
 
 def feed_back_kernel(cot, weight, slope, up_grad):
@@ -528,7 +524,7 @@
         ),
         out_shape=[jax.ShapeDtypeStruct((TOK, D), F32)] * 2,
         input_output_aliases={8: 0, 9: 1} if held else {},
-        compiler_params=pltpu.CompilerParams(vmem_limit_bytes=VMEM),
+        compiler_params=pltpu.CompilerParams(vmem_limit_bytes=VMEM_LESS),
         cost_estimate=COST,
     )(half, branch, combined, hidden, cot, stats, *(b.reshape(1, D) for b in biases), *held)
 
@@ -538,46 +534,54 @@
     step = pl.program_id(0)
     copies = [pltpu.make_async_copy(lefts[k], held[k], arrived.at[k]) for k in range(3)]
 
+    def put(columns, k, given):
+        right = jnp.concatenate([rights[2 * k][:, given], rights[2 * k + 1][:, given]], axis=0)
+        total = plain_dot(held[k][...].reshape(D, 2 * TOK), right)
+        target[:, :, columns] = total.reshape(16, 128, -1)
+
     @pl.when(step == 0)
     def _():
         for copy in copies:
             copy.start()
-
-    for k, (start, stop) in enumerate(((0, 4), (4, 5), (5, 8))):
-
-        @pl.when(step == start)
-        def _(k=k):
-            copies[k].wait()
-
-        @pl.when((step >= start) & (step < stop))
-        def _(k=k):
-            right = jnp.concatenate([rights[2 * k][...], rights[2 * k + 1][...]], axis=0)
-            total = plain_dot(held[k][...].reshape(D, 2 * TOK), right)
-            target[...] = total.reshape(16, 128, -1)
+        copies[0].wait()
+
+    @pl.when(step < 2)
+    def _():
+        put(slice(0, 512), 0, slice(0, 512))
+
+    @pl.when(step == 2)
+    def _():
+        copies[1].wait()
+        copies[2].wait()
+        put(slice(0, HD), 1, slice(0, HD))
+        put(slice(HD, 512), 2, slice(0, 512 - HD))
+
+    @pl.when(step == 3)
+    def _():
+        put(slice(0, 512), 2, slice(512 - HD, 3 * HD))
 
 
 def joint(side, lefts, rights):
-    width = 256
     specs = [pl.BlockSpec(memory_space=pl.ANY)] * 3
-    for start, n in ((0, 4), (4, 1), (5, 3)):
-
-        def near(j, s, start=start, n=n):
-            return (0, s[0] * n + jnp.clip(j - start, 0, n - 1))
-
-        def far(j, s, start=start, n=n):
-            return (0, jnp.clip(j - start, 0, n - 1))
+    for width, n in ((512, 2), (HD, 1), (3 * HD, 1)):
+
+        def near(j, s, n=n):
+            return (0, s[0] * n + jnp.clip(j, 0, n - 1))
+
+        def far(j, s, n=n):
+            return (0, jnp.clip(j, 0, n - 1))
 
         specs += [pl.BlockSpec((TOK, width), near), pl.BlockSpec((TOK, width), far)]
     return pl.pallas_call(
         joint_kernel,
         grid_spec=pltpu.PrefetchScalarGridSpec(
             num_scalar_prefetch=1,
-            grid=(8,),
+            grid=(4,),
             in_specs=specs,
-            out_specs=pl.BlockSpec((16, 128, width), lambda j, s: (0, 0, j)),
+            out_specs=pl.BlockSpec((16, 128, 512), lambda j, s: (0, 0, j)),
             scratch_shapes=[pltpu.VMEM(TURNED, BF16)] * 3 + [pltpu.SemaphoreType.DMA((3,))],
         ),
-        out_shape=jax.ShapeDtypeStruct((16, 128, 8 * width), F32),
+        out_shape=jax.ShapeDtypeStruct((16, 128, 2048), F32),
         compiler_params=pltpu.CompilerParams(vmem_limit_bytes=VMEM),
         cost_estimate=COST,
     )(side, *lefts, *rights)
@@ -612,7 +616,7 @@
             out_specs=[pl.BlockSpec(shape, lambda i, s: (0, 0)) for shape in shapes],
         ),
         out_shape=[jax.ShapeDtypeStruct(shape, F32) for shape in shapes],
-        compiler_params=pltpu.CompilerParams(vmem_limit_bytes=VMEM),
+        compiler_params=pltpu.CompilerParams(vmem_limit_bytes=VMEM_LESS),
         cost_estimate=COST,
     )(side, near, far)
 
@@ -648,14 +652,13 @@
     def of_core(values, which):
         return lax.dynamic_slice_in_dim(values, which * half_rows, half_rows, 0)
 
-    second_in, cot_turned, stats, hidden_sent = second(
-        at_core, hidden_in, cotangent, ln2_gain, ln2_bias
-    )
-    hidden_pair = lax.all_gather(hidden_sent, "zl")
-    act_low, slope, down_grad = feed(second_in, cot_turned, fc1_weight, fc1_bias)
+    act_low, slope, down_grad = feed(
+        hidden_in, ln2_gain, ln2_bias, cotangent, fc1_weight, fc1_bias
+    )
     down_sum = after(lax.psum_scatter(down_grad, ("x", "y"), scatter_dimension=0, tiled=True))
     _, cotangent, hidden_in = after((down_grad, cotangent, hidden_in))
 
+    hidden_got = send(of_core(hidden_in, core).astype(F32), "zl")
     marks = jnp.concatenate([segment_ids, positions]).astype(F32).reshape(1, 2 * TOK)
     cot_sent = jnp.concatenate(
         [of_core(cotangent, core).astype(F32), jnp.pad(marks, ((0, 7), (0, D - 2 * TOK)))], axis=0
@@ -665,37 +668,36 @@
     own_marks = marks.reshape(2, TOK)
 
     def own_step(hidden_in, cotangent, act_low, slope):
-        first_in, first_turned, second_turned = norm_call(
-            first_kernel, 256, (hidden_in,), 1, 2, params
-        )
+        first_in, *turned, stats = first(hidden_in, cotangent, params)
         projected = project(own_place, 2, first_in, qkv_weight, qkv_bias, own_marks)
         mixed_low, grad_packed = attend(
             own_place, 2, projected, (cotangent, dense_weight), own_marks
         )
         grad_up = feed_back(cotangent, fc2_weight, slope)
         branches = branch_halves(at_core, mixed_low, act_low, dense_weight, fc2_weight)
-        return first_turned, second_turned, mixed_low, grad_packed, grad_up, *branches
+        return *turned, stats, mixed_low, grad_packed, grad_up, *branches
 
     (
         first_turned,
         second_turned,
+        cot_turned,
+        stats,
         mixed_low,
         grad_packed,
         grad_up,
         branch,
         branch_other,
     ) = lax.cond(core > 1, own_step, own_step, hidden_in, cotangent, act_low, slope)
-    hidden_pair, mixed_low = after((hidden_pair, mixed_low))
-    hidden_got = lax.dynamic_slice_in_dim(hidden_pair, 1 - side, 1, 0)
-    hidden_too, branch_too = send(hidden_got, "c"), send(branch_other, "c")
+    branch_too = send(branch_other, "c")
+    hidden_got, cot_got, branch_too = after((hidden_got, cot_got, branch_too))
+    hidden_too = send(hidden_got, "c")
+    branch = lax.psum(branch + branch_too, "zh")
     hidden_too, cot_got = after((hidden_too, cot_got))
     cot_too = send(cot_got, "c")
 
     first_far_in, second_far_in, first_turned, second_turned = first_far(
         hidden_got, hidden_too, params, (first_turned, second_turned)
     )
-    second_far_in, branch_too = after((second_far_in, branch_too))
-    branch = lax.psum(branch + branch_too, "zh")
     slope_side = slope_far(at_side, second_far_in, fc1_weight, fc1_bias)
     marks_got = cot_got[half_rows, : 2 * TOK].reshape(2, 2, half_rows)
     marks_far = jnp.where(core == 0, marks_got, marks_got[:, ::-1]).reshape(2, TOK)

time: 286 us -> 288 us (level); the launches traced: 286 us -> 283 us
  local copies, waits for them, and re-layouts: 13.7 us -> 7.92 us
  Pallas kernels: 138 us -> 135 us
  waiting for transfers between devices: 77.5 us -> 80.5 us
    ppermute x12 -> x13, waiting for transfers between devices: 45.8 us -> 54.7 us  [send(): return lax.ppermute(value, axis, [(i, (i + step) % n) for i in range(n)])]
    pallas_call x2 -> x1, Pallas kernels: 9.22 us -> 5.02 us  [first(): pl.pallas_call(first_kernel, grid=(2,), in_specs=[plain] * 2 + [whole((1,...]
    unnamed x37 -> x43, local copies, waits for them, and re-layouts: 5.71 us -> 2.66 us
    convert_element_type x0 -> x1, other arithmetic: none -> 2.99 us  [body(): hidden_got = send(of_core(hidden_in, core).astype(F32), 'zl')]
    ppermute x12 -> x13, starting transfers between devices: 8.96 us -> 11.2 us  [send(): return lax.ppermute(value, axis, [(i, (i + step) % n) for i in range(n)])]
  transfers between devices with their start and end apart: 21 -> 21, of which waited for: 13 -> 14; matrix products, arithmetic and copies ran while one was open for 10% -> 9% of each run, Pallas kernels for 46% -> 41%
where the time goes in v5:
time: 288 us; the launch traced here: 283 us
  Pallas kernels  135 us (47%)
  waiting for transfers between devices  80.5 us (28%)
  starting transfers between devices  23.4 us (8%)
  other arithmetic  19.9 us (7%)
  between operations  16.1 us (6%)
  local copies, waits for them, and re-layouts  7.92 us (3%)
    ppermute x13, waiting for transfers between devices, send(): return lax.ppermute(value, axis, [(i, (i + step) % n) for i in range(n)])  54.7 us
    pallas_call x2, Pallas kernels, halves_call(): pl.pallas_call(kernel, grid_spec=pltpu.PrefetchScalarGridSpec(num_scalar_...  25.4 us
    pallas_call x1, Pallas kernels, feed(): pl.pallas_call(feed_kernel, grid=(units // width,), in_specs=[whole((TOK,...  18.2 us
    pallas_call x1, Pallas kernels, joint(): pl.pallas_call(joint_kernel, grid_spec=pltpu.PrefetchScalarGridSpec(num_s...  16.3 us
    ppermute x4, waiting for transfers between devices, swap(): return lax.ppermute(value, axis, [(i, i ^ bit) for i in range(SIZES[axis])])  15.9 us
    pallas_call x2, Pallas kernels, project(): pl.pallas_call(project_kernel, grid_spec=pltpu.PrefetchScalarGridSpec(num...  14.6 us
    pallas_call x2, Pallas kernels, attend(): pl.pallas_call(attend_kernel, grid_spec=pltpu.PrefetchScalarGridSpec(num_...  13.7 us
    ppermute x13, starting transfers between devices, send(): return lax.ppermute(value, axis, [(i, (i + step) % n) for i in range(n)])  11.2 us
  transfers between devices with their start and end apart: 21, of which 14 were waited for; matrix products, arithmetic and copies ran while one was open for 9% of the time, Pallas kernels for 41%

profile of v5, /device:TPU:0, one launch (start us, length us, event | category | flops | bytes accessed | tf_op | source)
XLA Modules:
  0.0 282.7 jit_solution(10048700364486777958)
XLA Ops:
  8.1 18.2 %shard_map.281 = (bf16[512,2048]{1,0:T(8,128)(2,1)}, f32[512,2048]{1,0:T(8,128)}, f32[16,128,2048]{2,1,0:T(8,128)}) custom-call(bf16[512,2048]{1,0:T(8,128)(2,1)} %hidden.4, f32[1,2048]{1,0:T(1,128)} %bitcast.49, f32[1,2048]{1,0:T(1,128)} %bitcast.60, bf16[512,2048]{1,0:T(8,128)(2,1)} %cot.3, bf16[2048,2048]{1,0:T(8,128)(2,1)} %up.1, f32[4,4,128]{2,1,0:T(4,128)} %bitcast.70), custom_call_target="tpu_custom_call" | custom-call | flops 1000000 | bytes 1000000 | tf_op jit(solution)/shard_map/pallas_call | solution.py:188
  33.2 3.0 %collective-permute-start.1 = (f32[264,2048]{1,0:T(8,128)}, f32[264,2048]{1,0:T(8,128)}, u32[]{:S(2)}, u32[]{:S(2)}) collective-permute-start(f32[264,2048]{1,0:T(8,128)} %select_maximum_fusion), channel_id=1, source_target_pairs={{0,66},{2,64},{64,2},{66,0},{1,67},{3,65},{65,3},{67,1},{4,70},{6,... | collective-permute-start | bytes 6488072 | tf_op jit(solution)/shard_map/ppermute | solution.py:666
  36.3 42.0 %conditional.1 = (bf16[16,2,64,1024]{3,2,1,0:T(8,128)(2,1)}, bf16[16,2,64,1024]{3,2,1,0:T(8,128)(2,1)}, bf16[16,2,64,1024]{3,2,1,0:T(8,128)(2,1)}, f32[512,128]{...) conditional(s32[]{:T(128)} %convert_element_type.39, ...), branch_computations={%region_0.0_spmd, %region_1.2_spmd} | conditional | flops 5000000 | bytes 30165992 | solution.py:690
  36.4 9.4 %branch_0_fun.8 = bf16[512,2048]{1,0:T(8,128)(2,1)} custom-call(bf16[512,2048]{1,0:T(8,128)(2,1)S(1)} %get-tuple-element.61.cot.refs_0_, bf16[2048,2048]{1,0:T(8,128)(2,1)} %get-tuple-element.84.weight.down, f32[512,2048]{1,0:T(8,128)} %get-tuple-element.85.slope), custom_call_target="tpu_custom_call" | custom-call | flops 1000000 | bytes 1000000 | tf_op jit(solution)/shard_map/cond/branch_0_fun/pallas_call | solution.py:225
  45.7 5.0 %branch_0_fun.5 = (bf16[512,2048]{1,0:T(8,128)(2,1)}, bf16[16,2,64,1024]{3,2,1,0:T(8,128)(2,1)}, bf16[16,2,64,1024]{3,2,1,0:T(8,128)(2,1)}, bf16[16,2,64,1024]{3,2,1,0:T(8,128)(2,1)}, f32[512,128]{1,0:T(8,128)S(1)}) custom-call(bf16[512,2048]{1,0:T(8,128)(2,1)S(1)} %copy-done.6, bf16[512,2048]{1,0:T(8,128)(2,1)S(1)} %get-tuple-element.61.cot.refs_0_, ...), custom_call_target="tpu_custom_call" | custom-call | flops 1000000 | bytes 1000000 | tf_op jit(solution)/shard_map/cond/branch_0_fun/pallas_call | solution.py:117
  51.2 8.5 %branch_0_fun.6 = (bf16[512,512]{1,0:T(8,128)(2,1)}, bf16[512,512]{1,0:T(8,128)(2,1)}, bf16[512,512]{1,0:T(8,128)(2,1)}, f32[512,128]{1,0:T(8,128)}, f32[512,128]{1,0:T(8,128)}, /*index=5*/f32[512,128]{1,0:T(8,128)}) custom-call(s32[2]{0:T(128)} %broadcast_1_place.0.place, bf16[512,2048]{1,0:T(8,128)(2,1)} %get-tuple-element.70.first, ...), custom_call_target="tpu_custom_call" | custom-call | flops 1000000 | bytes 1000000 | tf_op jit(solution)/shard_map/cond/branch_0_fun/pallas_call | solution.py:362
  59.7 8.8 %branch_0_fun.7 = (bf16[512,512]{1,0:T(8,128)(2,1)}, bf16[512,1536]{1,0:T(8,128)(2,1)}) custom-call(s32[2]{0:T(128)} %broadcast_1_place.0.place, bf16[512,512]{1,0:T(8,128)(2,1)} %get-tuple-element.75.queries, bf16[512,512]{1,0:T(8,128)(2,1)} %get-tuple-element.76.keys, bf16[512,512]{1,0:T(8,128)(2,1)} %get-tuple-element.77.values, ...), custom_call_target="tpu_custom_call" | custom-call | flops 1000000 | bytes 1000000 | tf_op jit(solution)/shard_map/cond/branch_0_fun/pallas_call | solution.py:416
  68.5 9.8 %branch_0_fun.9 = (f32[256,2048]{1,0:T(8,128)}, f32[256,2048]{1,0:T(8,128)}) custom-call(s32[1]{0:T(128)} %get-tuple-element.86.core, bf16[512,512]{1,0:T(8,128)(2,1)} %get-tuple-element.302.mixed, bf16[512,2048]{1,0:T(8,128)(2,1)S(1)} %copy-done.11, bf16[512,2048]{1,0:T(8,128)(2,1)S(1)} %copy-done.9, bf16[2048,2048]{1,0:T(8,128)(2,1)} %get-tuple-element.84.weight.down), custom_call_target="tpu_custom_call" | custom-call | flops 1000000 | bytes 1000000 | tf_op jit(solution)/shard_map/cond/branch_0_fun/pallas_call | solution.py:464
  78.3 4.4 %collective-permute-done.2 = f32[256,2048]{1,0:T(8,128)S(1)} collective-permute-done((f32[256,2048]{1,0:T(8,128)}, f32[256,2048]{1,0:T(8,128)S(1)}, u32[]{:S(2)}, u32[]{:S(2)}) %collective-permute-start.2) | collective-permute-done | bytes 2097184 | tf_op jit(solution)/shard_map/ppermute | solution.py:27
  83.8 4.5 %collective-permute-done.3.other = f32[256,2048]{1,0:T(8,128)} collective-permute-done((f32[256,2048]{1,0:T(8,128)}, f32[256,2048]{1,0:T(8,128)}, u32[]{:S(2)}, u32[]{:S(2)}) %collective-permute-start.3) | collective-permute-done | bytes 2097184 | tf_op jit(solution)/shard_map/ppermute | solution.py:27
  88.4 3.2 %add.80 = f32[256,2048]{1,0:T(8,128)} add(f32[256,2048]{1,0:T(8,128)} %get-tuple-element.229, f32[256,2048]{1,0:T(8,128)S(1)} %collective-permute-done.2) | non-fusion elementwise | flops 524288 | bytes 6291456 | tf_op jit(solution)/shard_map/add | solution.py:694
  94.0 7.0 %shard_map.282 = (bf16[512,2048]{1,0:T(8,128)(2,1)}, bf16[512,2048]{1,0:T(8,128)(2,1)}, bf16[16,2,64,1024]{3,2,1,0:T(8,128)(2,1)}, bf16[16,2,64,1024]{3,2,1,0:T(8,128)(2,1)}) custom-call(f32[256,2048]{1,0:T(8,128)} %collective-permute-done.near, f32[256,2048]{1,0:T(8,128)} %collective-permute-done.3.other, ...), custom_call_target="tpu_custom_call", output_to_operand_aliasing={{2}: (6, {}), {3}: (7, {})} | custom-call | flops 1000000 | bytes 1000000 | tf_op jit(solution)/shard_map/pallas_call | solution.py:135
  101.0 7.0 %shard_map.283.slope = f32[512,1024]{1,0:T(8,128)} custom-call(s32[1]{0:T(128)} %bitcast.9.side, bf16[512,2048]{1,0:T(8,128)(2,1)} %get-tuple-element.204.second, bf16[2048,2048]{1,0:T(8,128)(2,1)} %up.1, f32[4,4,128]{2,1,0:T(4,128)} %bitcast.71), custom_call_target="tpu_custom_call" | custom-call | flops 1000000 | bytes 1000000 | tf_op jit(solution)/shard_map/pallas_call | solution.py:292
  108.0 6.1 %shard_map.285 = (bf16[512,256]{1,0:T(8,128)(2,1)}, bf16[512,256]{1,0:T(8,128)(2,1)}, bf16[512,256]{1,0:T(8,128)(2,1)}, f32[512,128]{1,0:T(8,128)}, f32[512,128]{1,0:T(8,128)}, /*index=5*/f32[512,128]{1,0:T(8,128)}) custom-call(s32[2]{0:T(128)} %pad_add_fusion.place, bf16[512,2048]{1,0:T(8,128)(2,1)} %get-tuple-element.211.first, bf16[2048,1536]{1,0:T(8,128)(2,1)} %qkv.1, ...), custom_call_target="tpu_custom_call" | custom-call | flops 1000000 | bytes 1000000 | tf_op jit(solution)/shard_map/pallas_call | solution.py:362
  114.2 8.4 %shard_map.284 = (bf16[512,1024]{1,0:T(8,128)(2,1)}, bf16[512,256]{1,0:T(8,128)(2,1)}, bf16[16,2,64,1024]{3,2,1,0:T(8,128)(2,1)}) custom-call(s32[1]{0:T(128)} %bitcast.9.side, f32[264,2048]{1,0:T(8,128)} %collective-permute-done.1.near, f32[264,2048]{1,0:T(8,128)} %collective-permute-done.4.other, ...), custom_call_target="tpu_custom_call", output_to_operand_aliasing={{2}: (6, {})} | custom-call | flops 1000000 | bytes 1000000 | tf_op jit(solution)/shard_map/pallas_call | solution.py:253
  122.5 4.9 %shard_map.286 = (bf16[512,256]{1,0:T(8,128)(2,1)}, bf16[512,768]{1,0:T(8,128)(2,1)}) custom-call(s32[2]{0:T(128)} %pad_add_fusion.place, bf16[512,256]{1,0:T(8,128)(2,1)} %get-tuple-element.212.queries, bf16[512,256]{1,0:T(8,128)(2,1)} %get-tuple-element.213.keys, bf16[512,256]{1,0:T(8,128)(2,1)} %get-tuple-element.214.values, ...), custom_call_target="tpu_custom_call" | custom-call | flops 1000000 | bytes 1000000 | tf_op jit(solution)/shard_map/pallas_call | solution.py:416
  127.5 16.3 %shard_map.287 = f32[16,128,2048]{2,1,0:T(8,128)} custom-call(s32[1]{0:T(128)} %bitcast.9.side, bf16[16,2,64,1024]{3,2,1,0:T(8,128)(2,1)} %get-tuple-element.202.refs_0_, bf16[16,2,64,1024]{3,2,1,0:T(8,128)(2,1)} %get-tuple-element.206.refs_1_, bf16[16,2,64,1024]{3,2,1,0:T(8,128)(2,1)} %get-tuple-element.207.refs_2_, ...), custom_call_target="tpu_custom_call" | custom-call | flops 1000000 | bytes 1000000 | tf_op jit(solution)/shard_map/pallas_call | solution.py:575
  143.8 15.7 %shard_map.288 = (f32[256,2048]{1,0:T(8,128)}, f32[256,2048]{1,0:T(8,128)}, f32[8,2048]{1,0:T(8,128)}) custom-call(s32[1]{0:T(128)} %bitcast.8.core.half, bf16[512,1536]{1,0:T(8,128)(2,1)} %get-tuple-element.224.refs_7_.packed, bf16[512,2048]{1,0:T(8,128)(2,1)} %get-tuple-element.225.refs_3_.up_grad, bf16[2048,1536]{1,0:T(8,128)(2,1)} %qkv.1, ...), custom_call_target="tpu_custom_call" | custom-call | flops 1000000 | bytes 1000000 | tf_op jit(solution)/shard_map/pallas_call | solution.py:464
  159.6 4.3 %collective-permute-done.12 = f32[256,2048]{1,0:T(8,128)S(1)} collective-permute-done((f32[256,2048]{1,0:T(8,128)}, f32[256,2048]{1,0:T(8,128)S(1)}, u32[]{:S(2)}, u32[]{:S(2)}) %collective-permute-start.12) | collective-permute-done | bytes 2097184 | tf_op jit(solution)/shard_map/ppermute | solution.py:27
  163.9 3.3 %add.81 = f32[256,2048]{1,0:T(8,128)} add(f32[256,2048]{1,0:T(8,128)} %get-tuple-element.231, f32[256,2048]{1,0:T(8,128)S(1)} %collective-permute-done.12) | non-fusion elementwise | flops 524288 | bytes 6291456 | tf_op jit(solution)/shard_map/add | solution.py:725
  167.2 3.0 %collective-permute-start.13 = (f32[256,2048]{1,0:T(8,128)}, f32[256,2048]{1,0:T(8,128)}, u32[]{:S(2)}, u32[]{:S(2)}) collective-permute-start(f32[256,2048]{1,0:T(8,128)} %add.81), channel_id=1, source_target_pairs={{0,2},{2,0},{1,3},{3,1},{4,6},{6,4},{5,7},{7,5},{8,10},{10,8},{9,1... | collective-permute-start | bytes 6291464 | tf_op jit(solution)/shard_map/ppermute | solution.py:27
  177.0 4.7 %collective-permute-done.5 = f32[32,512]{1,0:T(8,128)S(1)} collective-permute-done((f32[32,512]{1,0:T(8,128)S(1)}, f32[32,512]{1,0:T(8,128)S(1)}, u32[]{:S(2)}, u32[]{:S(2)}) %collective-permute-start.5) | collective-permute-done | bytes 65568 | tf_op jit(solution)/shard_map/ppermute | solution.py:31
  185.6 3.6 %collective-permute-done.6 = f32[32,512]{1,0:T(8,128)S(1)} collective-permute-done((f32[32,512]{1,0:T(8,128)S(1)}, f32[32,512]{1,0:T(8,128)S(1)}, u32[]{:S(2)}, u32[]{:S(2)}) %collective-permute-start.6) | collective-permute-done | bytes 65568 | tf_op jit(solution)/shard_map/ppermute | solution.py:31
  190.7 3.7 %collective-permute-done.7 = f32[32,512]{1,0:T(8,128)S(1)} collective-permute-done((f32[32,512]{1,0:T(8,128)S(1)}, f32[32,512]{1,0:T(8,128)S(1)}, u32[]{:S(2)}, u32[]{:S(2)}) %collective-permute-start.7) | collective-permute-done | bytes 65568 | tf_op jit(solution)/shard_map/ppermute | solution.py:31
  194.5 3.4 %collective-permute-start.8 = (f32[32,512]{1,0:T(8,128)S(1)}, f32[32,512]{1,0:T(8,128)S(1)}, u32[]{:S(2)}, u32[]{:S(2)}) collective-permute-start(f32[32,512]{1,0:T(8,128)S(1)} %add.70), channel_id=1, source_target_pairs={{0,8},{4,12},{8,0},{12,4},{1,9},{5,13},{9,1},{13,5},{2,10},{6,14},... | collective-permute-start | bytes 196616 | tf_op jit(solution)/shard_map/ppermute | solution.py:31
  197.9 3.8 %collective-permute-done.8 = f32[32,512]{1,0:T(8,128)S(1)} collective-permute-done((f32[32,512]{1,0:T(8,128)S(1)}, f32[32,512]{1,0:T(8,128)S(1)}, u32[]{:S(2)}, u32[]{:S(2)}) %collective-permute-start.8) | collective-permute-done | bytes 65568 | tf_op jit(solution)/shard_map/ppermute | solution.py:31
  202.6 25.6 %collective-permute-done.9 = f32[1,512]{1,0:T(1,128)S(1)} collective-permute-done((f32[1,512]{1,0:T(1,128)S(1)}, f32[1,512]{1,0:T(1,128)S(1)}, u32[]{:S(2)}, u32[]{:S(2)}) %collective-permute-start.9) | collective-permute-done | bytes 2080 | tf_op jit(solution)/shard_map/ppermute | solution.py:27
  231.1 3.7 %collective-permute-done.11 = f32[256]{0:T(256)S(1)} collective-permute-done((f32[256]{0:T(256)S(1)}, f32[256]{0:T(256)S(1)}, u32[]{:S(2)}, u32[]{:S(2)}) %collective-permute-start.11) | collective-permute-done | bytes 1056 | tf_op jit(solution)/shard_map/ppermute | solution.py:27
  240.6 4.5 %shard_map.289 = (f32[512,2048]{1,0:T(8,128)}, f32[512,2048]{1,0:T(8,128)}) custom-call(s32[1]{0:T(128)} %bitcast.8.core.half, f32[256,2048]{1,0:T(8,128)} %all-reduce.5.cloned.1.call-done.branch, f32[256,2048]{1,0:T(8,128)S(1)} %add.83.combined, bf16[512,2048]{1,0:T(8,128)(2,1)} %hidden.4, bf16[512,2048]{1,0:T(8,128)(2,1)} %cot.3, ...), custom_call_target="tpu_custom_call" | custom-call | flops 1000000 | bytes 1000000 | tf_op jit(solution)/shard_map/pallas_call | solution.py:514
  246.1 4.1 %shard_map.290 = (f32[512,2048]{1,0:T(8,128)}, f32[512,2048]{1,0:T(8,128)}) custom-call(s32[1]{0:T(128)S(6)} %sub.8.half, f32[256,2048]{1,0:T(8,128)} %collective-permute-done.15.branch, f32[256,2048]{1,0:T(8,128)} %collective-permute-done.16.combined, bf16[512,2048]{1,0:T(8,128)(2,1)S(1)} %copy-done.5, ...), custom_call_target="tpu_custom_call", output_to_operand_aliasing={{0}: (8, {}), {1}: (9, {})} | custom-call | flops 1000000 | bytes 1000000 | tf_op jit(solution)/shard_map/pallas_call | solution.py:514
  250.2 8.8 %reduce-scatter.9.cloned.1.call-done.near = f32[1,128,2048]{2,1,0:T(8,128)} async-done(((f32[16,128,2048]{2,1,0:T(8,128)}), f32[1,128,2048]{2,1,0:T(8,128)}) %reduce-scatter.9.cloned.1.call-update) | async-done | bytes 1048592 | tf_op jit(solution)/shard_map/optimization_barrier | solution.py:767
  263.3 10.1 %collective-permute-done.17.far = f32[64,2048]{1,0:T(8,128)S(1)} collective-permute-done((f32[64,2048]{1,0:T(8,128)S(1)}, f32[64,2048]{1,0:T(8,128)S(1)}, u32[]{:S(2)}, u32[]{:S(2)}) %collective-permute-start.17) | collective-permute-done | bytes 524320 | tf_op jit(solution)/shard_map/ppermute | solution.py:27
  (126 shorter events, 39.6 us)
Async XLA Ops:
  8.0 135.8 %reduce-scatter.7.cloned.1.call-start = ((), (), s32[]{:S(2)}) async-start(), calls=%async_computation.3 | async-start | bytes 17825792
  26.3 208.5 %all-reduce.5.cloned.1.call-start = ((), (), s32[]{:S(2)}) async-start(), calls=%async_computation.2 | async-start | bytes 4194304 | tf_op jit(solution)/shard_map/psum | solution.py:694
  29.3 49.0 %collective-permute-start = (f32[256,2048]{1,0:T(8,128)}, f32[256,2048]{1,0:T(8,128)}, u32[]{:S(2)}, u32[]{:S(2)}) collective-permute-start(f32[256,2048]{1,0:T(8,128)} %dynamic-slice_convert_fusion.1), channel_id=1, source_target_pairs={{0,64},{64,0},{1,65},{65,1},{2,66},{66,2},{3,67},{67,3},{4,68},{68... | collective-permute-start | bytes 6291464 | tf_op jit(solution)/shard_map/ppermute | solution.py:27
  33.2 50.5 %collective-permute-start.1 = (f32[264,2048]{1,0:T(8,128)}, f32[264,2048]{1,0:T(8,128)}, u32[]{:S(2)}, u32[]{:S(2)}) collective-permute-start(f32[264,2048]{1,0:T(8,128)} %select_maximum_fusion), channel_id=1, source_target_pairs={{0,66},{2,64},{64,2},{66,0},{1,67},{3,65},{65,3},{67,1},{4,70},{6,... | collective-permute-start | bytes 6488072 | tf_op jit(solution)/shard_map/ppermute | solution.py:666
  36.3 9.4 %copy-start.6 = (bf16[512,2048]{1,0:T(8,128)(2,1)S(1)}, bf16[512,2048]{1,0:T(8,128)(2,1)}, u32[]{:S(2)}) copy-start(bf16[512,2048]{1,0:T(8,128)(2,1)} %get-tuple-element.60.hidden) | copy-start | bytes 6291460 | tf_op jit(solution)/shard_map/cond
  51.2 8.5 %copy-start.9 = (bf16[512,2048]{1,0:T(8,128)(2,1)S(1)}, bf16[512,2048]{1,0:T(8,128)(2,1)}, u32[]{:S(2)}) copy-start(bf16[512,2048]{1,0:T(8,128)(2,1)} %get-tuple-element.81.refs_1_.dense) | copy-start | bytes 6291460 | tf_op jit(solution)/shard_map/cond
  59.7 8.8 %copy-start.11 = (bf16[512,2048]{1,0:T(8,128)(2,1)S(1)}, bf16[512,2048]{1,0:T(8,128)(2,1)}, u32[]{:S(2)}) copy-start(bf16[512,2048]{1,0:T(8,128)(2,1)} %get-tuple-element.87.act) | copy-start | bytes 6291460 | tf_op jit(solution)/shard_map/cond
  78.3 4.4 %collective-permute-start.2 = (f32[256,2048]{1,0:T(8,128)}, f32[256,2048]{1,0:T(8,128)S(1)}, u32[]{:S(2)}, u32[]{:S(2)}) collective-permute-start(f32[256,2048]{1,0:T(8,128)} %get-tuple-element.196), channel_id=1, source_target_pairs={{0,1},{1,0},{2,3},{3,2},{4,5},{5,4},{6,7},{7,6},{8,9},{9,8},{10,11... | collective-permute-start | bytes 6291464 | tf_op jit(solution)/shard_map/ppermute | solution.py:27
  83.8 4.5 %collective-permute-start.3 = (f32[256,2048]{1,0:T(8,128)}, f32[256,2048]{1,0:T(8,128)}, u32[]{:S(2)}, u32[]{:S(2)}) collective-permute-start(f32[256,2048]{1,0:T(8,128)} %collective-permute-done.near), channel_id=1, source_target_pairs={{0,1},{1,0},{2,3},{3,2},{4,5},{5,4},{6,7},{7,6},{8,9},{9,8},{10,11... | collective-permute-start | bytes 6291464 | tf_op jit(solution)/shard_map/ppermute | solution.py:27
  88.3 25.9 %collective-permute-start.4 = (f32[264,2048]{1,0:T(8,128)}, f32[264,2048]{1,0:T(8,128)}, u32[]{:S(2)}, u32[]{:S(2)}) collective-permute-start(f32[264,2048]{1,0:T(8,128)} %collective-permute-done.1.near), channel_id=1, source_target_pairs={{0,1},{1,0},{2,3},{3,2},{4,5},{5,4},{6,7},{7,6},{8,9},{9,8},{10,11... | collective-permute-start | bytes 6488072 | tf_op jit(solution)/shard_map/ppermute | solution.py:27
  91.7 167.3 %reduce-scatter.9.cloned.1.call-start = ((), (), s32[]{:S(2)}) async-start(), calls=%async_computation.4 | async-start | bytes 17825792
  108.0 6.1 %copy-start.8 = (bf16[512,2048]{1,0:T(8,128)(2,1)S(1)}, bf16[512,2048]{1,0:T(8,128)(2,1)}, u32[]{:S(2)}) copy-start(bf16[512,2048]{1,0:T(8,128)(2,1)} %dense.1) | copy-start | bytes 6291460
  159.5 4.4 %collective-permute-start.12 = (f32[256,2048]{1,0:T(8,128)}, f32[256,2048]{1,0:T(8,128)S(1)}, u32[]{:S(2)}, u32[]{:S(2)}) collective-permute-start(f32[256,2048]{1,0:T(8,128)} %get-tuple-element.232), channel_id=1, source_target_pairs={{0,1},{1,0},{2,3},{3,2},{4,5},{5,4},{6,7},{7,6},{8,9},{9,8},{10,11... | collective-permute-start | bytes 6291464 | tf_op jit(solution)/shard_map/ppermute | solution.py:27
  167.2 68.5 %collective-permute-start.13 = (f32[256,2048]{1,0:T(8,128)}, f32[256,2048]{1,0:T(8,128)}, u32[]{:S(2)}, u32[]{:S(2)}) collective-permute-start(f32[256,2048]{1,0:T(8,128)} %add.81), channel_id=1, source_target_pairs={{0,2},{2,0},{1,3},{3,1},{4,6},{6,4},{5,7},{7,5},{8,10},{10,8},{9,1... | collective-permute-start | bytes 6291464 | tf_op jit(solution)/shard_map/ppermute | solution.py:27
  172.5 11.9 %copy-start.13 = (f32[1,128,2048]{2,1,0:T(8,128)S(1)}, f32[1,128,2048]{2,1,0:T(8,128)}, u32[]{:S(2)}) copy-start(f32[1,128,2048]{2,1,0:T(8,128)} %reduce-scatter.7.cloned.1.call-done) | copy-start | bytes 3145732
  175.7 6.0 %collective-permute-start.5 = (f32[32,512]{1,0:T(8,128)S(1)}, f32[32,512]{1,0:T(8,128)S(1)}, u32[]{:S(2)}, u32[]{:S(2)}) collective-permute-start(f32[32,512]{1,0:T(8,128)S(1)} %concatenate.27), channel_id=1, source_target_pairs={{0,16},{16,0},{32,48},{48,32},{1,17},{17,1},{33,49},{49,33},{2,18}... | collective-permute-start | bytes 196616 | tf_op jit(solution)/shard_map/ppermute | solution.py:31
  181.6 7.6 %collective-permute-start.6 = (f32[32,512]{1,0:T(8,128)S(1)}, f32[32,512]{1,0:T(8,128)S(1)}, u32[]{:S(2)}, u32[]{:S(2)}) collective-permute-start(f32[32,512]{1,0:T(8,128)S(1)} %add.68), channel_id=1, source_target_pairs={{0,32},{16,48},{32,0},{48,16},{1,33},{17,49},{33,1},{49,17},{2,34}... | collective-permute-start | bytes 196616 | tf_op jit(solution)/shard_map/ppermute | solution.py:31
  184.4 50.4 %collective-permute-start.14 = (f32[64,2048]{1,0:T(8,128)S(1)}, f32[64,2048]{1,0:T(8,128)S(1)}, u32[]{:S(2)}, u32[]{:S(2)}) collective-permute-start(f32[64,2048]{1,0:T(8,128)S(1)} %dynamic-slice_bitcast_fusion.1), channel_id=1, source_target_pairs={{0,64},{64,0},{1,65},{65,1},{2,66},{66,2},{3,67},{67,3},{4,68},{68... | collective-permute-start | bytes 1572872 | tf_op jit(solution)/shard_map/ppermute | solution.py:27
  189.2 5.2 %collective-permute-start.7 = (f32[32,512]{1,0:T(8,128)S(1)}, f32[32,512]{1,0:T(8,128)S(1)}, u32[]{:S(2)}, u32[]{:S(2)}) collective-permute-start(f32[32,512]{1,0:T(8,128)S(1)} %add.69), channel_id=1, source_target_pairs={{0,4},{4,0},{8,12},{12,8},{1,5},{5,1},{9,13},{13,9},{2,6},{6,2},{1... | collective-permute-start | bytes 196616 | tf_op jit(solution)/shard_map/ppermute | solution.py:31
  194.5 7.2 %collective-permute-start.8 = (f32[32,512]{1,0:T(8,128)S(1)}, f32[32,512]{1,0:T(8,128)S(1)}, u32[]{:S(2)}, u32[]{:S(2)}) collective-permute-start(f32[32,512]{1,0:T(8,128)S(1)} %add.70), channel_id=1, source_target_pairs={{0,8},{4,12},{8,0},{12,4},{1,9},{5,13},{9,1},{13,5},{2,10},{6,14},... | collective-permute-start | bytes 196616 | tf_op jit(solution)/shard_map/ppermute | solution.py:31
  201.7 26.5 %collective-permute-start.9 = (f32[1,512]{1,0:T(1,128)S(1)}, f32[1,512]{1,0:T(1,128)S(1)}, u32[]{:S(2)}, u32[]{:S(2)}) collective-permute-start(f32[1,512]{1,0:T(1,128)S(1)} %constant_dynamic-slice_fusion), channel_id=1, source_target_pairs={{0,64},{64,0},{1,65},{65,1},{2,66},{66,2},{3,67},{67,3},{4,68},{68... | collective-permute-start | bytes 6152 | tf_op jit(solution)/shard_map/ppermute | solution.py:27
  228.2 1.5 collective-permute-start.10
  229.7 5.1 %collective-permute-start.11 = (f32[256]{0:T(256)S(1)}, f32[256]{0:T(256)S(1)}, u32[]{:S(2)}, u32[]{:S(2)}) collective-permute-start(f32[256]{0:T(256)S(1)} %add.78), channel_id=1, source_target_pairs={{0,2},{2,0},{1,3},{3,1},{4,6},{6,4},{5,7},{7,5},{8,10},{10,8},{9,1... | collective-permute-start | bytes 3080 | tf_op jit(solution)/shard_map/ppermute | solution.py:27
  234.8 5.8 %copy-start.1 = (f32[2048]{0:T(1024)S(1)}, f32[2048]{0:T(1024)}, u32[]{:S(2)}) copy-start(f32[2048]{0:T(1024)} %param.28) | copy-start | bytes 24580
  234.8 5.8 %copy-start.2 = (f32[2048]{0:T(1024)S(1)}, f32[2048]{0:T(1024)}, u32[]{:S(2)}) copy-start(f32[2048]{0:T(1024)} %param.34) | copy-start | bytes 24580
  238.5 6.6 %collective-permute-start.16 = (f32[256,2048]{1,0:T(8,128)S(1)}, f32[256,2048]{1,0:T(8,128)}, u32[]{:S(2)}, u32[]{:S(2)}) collective-permute-start(f32[256,2048]{1,0:T(8,128)S(1)} %add.83.combined), channel_id=1, source_target_pairs={{0,1},{1,0},{2,3},{3,2},{4,5},{5,4},{6,7},{7,6},{8,9},{9,8},{10,11... | collective-permute-start | bytes 6291464 | tf_op jit(solution)/shard_map/ppermute | solution.py:27
  238.6 7.5 %collective-permute-start.15 = (f32[256,2048]{1,0:T(8,128)}, f32[256,2048]{1,0:T(8,128)}, u32[]{:S(2)}, u32[]{:S(2)}) collective-permute-start(f32[256,2048]{1,0:T(8,128)} %all-reduce.5.cloned.1.call-done.branch), channel_id=1, source_target_pairs={{0,1},{1,0},{2,3},{3,2},{4,5},{5,4},{6,7},{7,6},{8,9},{9,8},{10,11... | collective-permute-start | bytes 6291464 | tf_op jit(solution)/shard_map/ppermute | solution.py:27
  239.9 34.6 %copy-start.25 = (f32[64]{0:T(128)}, f32[64]{0:T(128)S(1)}, u32[]{:S(2)}) copy-start(f32[64]{0:T(128)S(1)} %get-tuple-element.343) | copy-start | bytes 772
  240.6 5.4 %copy-start.5 = (bf16[512,2048]{1,0:T(8,128)(2,1)S(1)}, bf16[512,2048]{1,0:T(8,128)(2,1)}, u32[]{:S(2)}) copy-start(bf16[512,2048]{1,0:T(8,128)(2,1)} %hidden.4) | copy-start | bytes 6291460
  246.1 16.4 %copy-start.15 = (f32[64,2048]{1,0:T(8,128)S(1)}, f32[64,2048]{1,0:T(8,128)}, u32[]{:S(2)}) copy-start(f32[64,2048]{1,0:T(8,128)} %copy-done.14) | copy-start | bytes 1572868
  259.0 14.4 %copy-start = (f32[1,128,2048]{2,1,0:T(8,128)S(1)}, f32[1,128,2048]{2,1,0:T(8,128)}, u32[]{:S(2)}) copy-start(f32[1,128,2048]{2,1,0:T(8,128)} %reduce-scatter.9.cloned.1.call-done.near) | copy-start | bytes 3145732
  260.2 13.2 %collective-permute-start.17 = (f32[64,2048]{1,0:T(8,128)S(1)}, f32[64,2048]{1,0:T(8,128)S(1)}, u32[]{:S(2)}, u32[]{:S(2)}) collective-permute-start(f32[64,2048]{1,0:T(8,128)S(1)} %dynamic-slice_bitcast_fusion), channel_id=1, source_target_pairs={{0,64},{64,0},{1,65},{65,1},{2,66},{66,2},{3,67},{67,3},{4,68},{68... | collective-permute-start | bytes 1572872 | tf_op jit(solution)/shard_map/ppermute | solution.py:27
  (12 other events, 52.1 us)
Sparse Core Ops, SparseCore 0:
  26.4 112.9 reduce-scatter.6
  144.0 114.9 reduce-scatter.8
Sparse Core Ops, SparseCore 1:
  91.8 71.9 all-reduce.4
